TPU v7x, 32 devices: a whole 2x2x4 slice. The times are simulated.
32 devices in a mesh: role: 2 (over core), group: 4 (over z), tp: 4 (over y, x).
Axes of the slice: x: 2, y: 2, z: 4, core: 2. Of those that a mesh axis runs over, the one named last changes fastest.
Arguments:
- kv_pages: bfloat16 [2, 4, 4, 64, 128, 512], P('role', 'group', 'tp'), may hold values from -24 to 24, as said below
- send_list: int32 [4, 12, 3], replicated, may hold values from 0 to 63, as said below
- wanted: int32 [4, 6], replicated, may hold values from 0 to 31, as said below
- lengths: int32 [4, 8], P('group'), may hold values from 1 to 1024, as said below
- tables: int32 [4, 8, 8], P('group'), may hold values from 0 to 69, as said below
- queries: bfloat16 [4, 8, 8192], P('group', None, 'tp'), may hold values from -160 to 160
- new_kv: bfloat16 [4, 8, 2048], P('group', None, 'tp'), may hold values from -24 to 24, as said below
- out_weight: bfloat16 [8192, 8192], P('tp', 'role'), may hold values from -3 to 3
Outputs:
- mixed: bfloat16 [4, 8, 8192], P('group', None, ('role', 'tp'))
Inputs may be any that keep to these rules, and one draw needn't show every extreme that they name: `send_list`: column 0 holds 12 distinct store pages of a prefill group, from 8 on; column 1 the destination decode group; column 2 the destination slot. The pairs (destination group, slot) are distinct over all groups. At most 4 pages go from one prefill group to one decode group, and one decode group receives exactly 4 from every prefill group. `wanted`: row g lists 6 distinct pages; page o * 8 + p is store slot p of prefill group o. Each row names pages of exactly 3 owner groups, 2 of each. `lengths`: in every group some row has exactly 1024 tokens. `tables`: entry j of a row serves its tokens j * 128 to (j + 1) * 128 - 1 below its length. An entry below 64 names a slot of the decode device's cache; an entry s from 64 on names the (s - 64)-th wanted page of the group. The entries a row reads are distinct, no cache slot is read by two rows of a group, and entries past a row's last page are 0. `new_kv`: indices of tp that hold the same key-value head hold equal new keys and values. `kv_pages`: indices of tp that hold the same key-value head hold equal pages.
All inputs are finite; a program needn't handle non-finite values.
Results may differ from a plain program's by a relative error of at most 0.006.
Values may be sent and summed in bfloat16 or wider, within the bound.
No kernel may reach another device: no remote copies, remote signals or barrier semaphores. Data moves between devices by JAX's collectives and lax.ppermute only.
A program may use at most 128 MiB of HBM per device.

v0:
```python
import functools
import math

import jax
import jax.numpy as jnp
from jax import lax
from jax.experimental import pallas as pl
from jax.experimental.pallas import tpu as pltpu
from jax.sharding import PartitionSpec as P

KVH = 8
HD = 128
CAP = 4
CAPP = 2
PRE_DEV = 8
LANES = 128
PAGE = 128
NEG = -1e30
FLOOR = -1e29
SCALE = 1.0 / math.sqrt(HD)
PARTS = CAP + CAPP
CHUNK = 4
STATIC = (4, 5, 6, 7, 8)
STATS = 16
MIB = 2**20


def dot(a, b, ca, cb):
    return lax.dot_general(a, b, (((ca,), (cb,)), ((), ())), preferred_element_type=jnp.float32)


def query_block(qa, held, per_held):
    q = qa[:, : held * per_held * HD].astype(jnp.float32)
    rows = q.shape[0]
    bands = []
    for j in range(held):
        heads = [q[:, (j * per_held + i) * HD : (j * per_held + i + 1) * HD] for i in range(per_held)]
        band = jnp.concatenate(heads, 0)
        blank = jnp.zeros_like(band)
        bands.append(jnp.concatenate([band if i == j else blank for i in range(held)], 1))
    return jnp.concatenate(bands, 0).astype(jnp.bfloat16)


def entry_rows(qa, held, per_held, maxp):
    rows = qa.shape[0]
    wide = held * per_held * HD
    aux = qa[:, wide : wide + LANES].astype(jnp.float32)
    lane = lax.broadcasted_iota(jnp.int32, (rows, LANES), 1) - maxp
    row = lax.broadcasted_iota(jnp.int32, (rows, LANES), 0)
    parts = jnp.where(lane == row, 8.0 * aux[:1], jnp.where(lane == row + rows, aux[:1], 0.0))
    length = jnp.sum(parts, 1, keepdims=True)
    turned = jnp.concatenate([jnp.where(lane == 0, length, aux)] * (held * per_held), 0).T
    first = lax.broadcasted_iota(jnp.int32, (maxp, 1), 0).astype(jnp.float32) * PAGE
    return turned[:maxp], jnp.clip(turned[maxp : maxp + 1] - first, 0.0, PAGE)


def lanes_of(page, first, held):
    return jnp.concatenate([page[:, (2 * j + first) * HD : (2 * j + first + 1) * HD] for j in range(held)], 1)


def pieces(x):
    high = x.astype(jnp.bfloat16).astype(jnp.float32)
    middle = (x - high).astype(jnp.bfloat16).astype(jnp.float32)
    return [high, middle, x - high - middle]


def write_part(out, acc, top, total, held, per_held):
    count = acc.shape[0]
    band = count // held
    out[:count, :] = jnp.concatenate(
        [acc[j * band : (j + 1) * band, j * HD : (j + 1) * HD] for j in range(held)], 0
    ).astype(out.dtype)
    rows = pieces(top) + pieces(total)
    block = jnp.concatenate(rows + [jnp.zeros((STATS - len(rows), count), jnp.float32)], 0)
    if count < LANES:
        block = jnp.concatenate([block, jnp.zeros((STATS, LANES - count), jnp.float32)], 1)
    out[count:, :] = block.astype(out.dtype)


def owner_part(qa, pages, entries, out, held, per_held, maxp):
    q = query_block(qa, held, per_held)
    tab, cnt = entry_rows(qa, held, per_held, maxp)
    count = q.shape[0]
    token = lax.broadcasted_iota(jnp.int32, (PAGE, count), 0).astype(jnp.float32)
    masks = []
    for c in range(PARTS):
        valid = jnp.sum(jnp.where(tab == entries[c : c + 1, :count], cnt, 0.0), 0, keepdims=True)
        masks.append(token < valid)
    mask = jnp.concatenate(masks, 0)
    keys = jnp.concatenate([lanes_of(pages.at[c], 0, held) for c in range(PARTS)], 0)
    values = jnp.concatenate([lanes_of(pages.at[c], 1, held) for c in range(PARTS)], 0)
    s = jnp.where(mask, dot(keys, q, 1, 1) * SCALE, NEG)
    top = jnp.max(s, 0, keepdims=True)
    p = jnp.where(mask, jnp.exp(s - top), 0.0)
    total = jnp.sum(p, 0, keepdims=True)
    acc = dot(p.astype(jnp.bfloat16), values, 0, 0)
    write_part(out, acc, top, total, held, per_held)


def resident_part(qa, lists_ready, send, tables, lengths, maxp, group, kv, pages, flags, listed, sems, out, held, per_held):
    rows = qa.shape[0]
    slots = kv.shape[0]
    q = query_block(qa, held, per_held)
    count = q.shape[0]
    lane_row = lax.rem(lax.broadcasted_iota(jnp.int32, (1, count), 1), rows)
    token = lax.broadcasted_iota(jnp.int32, (PAGE, count), 0)
    for i in range(slots):
        flags[i] = 0

    lists_ready()
    for o in range(send.shape[1]):
        for i in range(send.shape[2]):
            flags[jnp.where(send[1, o, i] == group, send[2, o, i], slots)] = 1

    def page_copy(slot, i):
        return pltpu.make_async_copy(kv.at[slot], pages.at[i], sems.at[i])

    listed_count = jnp.int32(0)
    for r in range(rows):
        length = lengths[0, r]
        for e in range(maxp):
            slot = tables[r, e]
            tokens = jnp.minimum(length - e * PAGE, PAGE)
            here = jnp.logical_and(slot < slots, flags[jnp.minimum(slot, slots - 1)] == 0)
            needed = jnp.logical_and(tokens > 0, here)
            listed[0, listed_count] = r
            listed[1, listed_count] = tokens

            @pl.when(needed)
            def _(slot=slot, at=listed_count):
                page_copy(slot, at).start()

            listed_count = listed_count + needed.astype(jnp.int32)
    chunks = jnp.maximum((listed_count + CHUNK - 1) // CHUNK, STATIC[0])

    def fill(i, _):
        listed[0, i] = 0
        listed[1, i] = 0
        page_copy(0, i).start()
        return 0

    lax.fori_loop(listed_count, chunks * CHUNK, fill, 0)

    def score(c):
        first = c * CHUNK
        masks = []
        for i in range(CHUNK):
            masks.append(token < jnp.where(lane_row == listed[0, first + i], listed[1, first + i], 0))
        for i in range(CHUNK):
            page_copy(0, first + i).wait()
        keys = jnp.concatenate([lanes_of(pages.at[first + i], 0, held) for i in range(CHUNK)], 0)
        return jnp.where(jnp.concatenate(masks, 0), dot(keys, q, 1, 1) * SCALE, NEG)

    def weigh(c, s, top):
        p = jnp.exp(s - top)
        values = jnp.concatenate([lanes_of(pages.at[c * CHUNK + i], 1, held) for i in range(CHUNK)], 0)
        return jnp.sum(p, 0, keepdims=True), dot(p.astype(jnp.bfloat16), values, 0, 0)

    floor = jnp.full((1, count), FLOOR, jnp.float32)

    def straight(number):
        scores = [score(c) for c in range(number)]
        top = functools.reduce(jnp.maximum, [jnp.max(s, 0, keepdims=True) for s in scores], floor)
        terms = [weigh(c, s, top) for c, s in enumerate(scores)]
        total = functools.reduce(jnp.add, [t for t, _ in terms])
        acc = functools.reduce(jnp.add, [a for _, a in terms])
        write_part(out, acc, top, total, held, per_held)

    def step(c, carry):
        top, total, acc = carry
        s = score(c)
        new_top = jnp.maximum(top, jnp.max(s, 0, keepdims=True))
        fade = jnp.exp(top - new_top)
        more, part = weigh(c, s, new_top)
        return new_top, total * fade + more, acc * jnp.broadcast_to(fade, (8, count)).T[:, :1] + part

    for number in STATIC:

        @pl.when(chunks == number)
        def _(number=number):
            straight(number)

    @pl.when(chunks > STATIC[-1])
    def _():
        start = (floor, jnp.zeros((1, count), jnp.float32), jnp.zeros((count, held * HD), jnp.float32))
        top, total, acc = lax.fori_loop(0, chunks, step, start)
        write_part(out, acc, top, total, held, per_held)


def list_pages(send, wanted, owner, target, slots, page_list, slot_list, base):
    for c in range(PARTS):
        page_list[base + c] = 0
        slot_list[base + c] = -1
    at = jnp.int32(base)
    for i in range(send.shape[2]):
        hit = send[1, owner, i] == target
        page_list[at] = send[0, owner, i]
        slot_list[at] = jnp.where(hit, send[2, owner, i], -1)
        at = at + hit.astype(jnp.int32)
    at = jnp.int32(base + CAP)
    page_list[at] = 0
    slot_list[at] = -1
    for i in range(wanted.shape[1]):
        page = wanted[target, i] - owner * PRE_DEV
        hit = jnp.logical_and(page >= 0, page < PRE_DEV)
        page_list[at] = jnp.where(hit, page, 0)
        slot_list[at] = jnp.where(hit, slots + i, -1)
        at = at + hit.astype(jnp.int32)


def copy_lists(pairs, sems):
    copies = [pltpu.make_async_copy(a, b, sems.at[i]) for i, (a, b) in enumerate(pairs)]
    for copy in copies:
        copy.start()

    def ready():
        for copy in copies:
            copy.wait()

    return ready


def first_kernel(held, per_held, groups, maxp, qa, send_hbm, wanted_hbm, tables_hbm, lengths_hbm, kv, *refs):
    out, sent, chosen, entries, pages, send, wanted, tables, lengths = refs[:9]
    flags, listed, page_list, slot_list, list_sems, chosen_sems, sems = refs[9:]
    group = lax.axis_index("group")
    prefill = lax.axis_index("role") == 0
    lists = ((send_hbm, send), (wanted_hbm, wanted), (tables_hbm, tables), (lengths_hbm, lengths))
    lists_ready = copy_lists(lists, list_sems)

    @pl.when(prefill)
    def _():
        lists_ready()
        copies = []
        for k in range(groups):
            target = lax.bitwise_xor(group, k)
            list_pages(send, wanted, group, target, kv.shape[0], page_list, slot_list, k * PARTS)
            for c in range(PARTS):
                at = k * PARTS + c
                copy = pltpu.make_async_copy(kv.at[page_list[at]], chosen.at[at], chosen_sems.at[at])
                copy.start()
                copies.append(copy)
                entry = slot_list[at].astype(jnp.float32)
                entries[at : at + 1, :] = jnp.full((1, LANES), entry, jnp.float32)
        for copy in copies[:PARTS]:
            copy.wait()
        owner_part(qa, chosen.at[pl.ds(0, PARTS)], entries[:PARTS, :], sent, held, per_held, maxp)
        for copy in copies[PARTS:]:
            copy.wait()

    @pl.when(jnp.logical_not(prefill))
    def _():
        resident_part(
            qa, lists_ready, send, tables, lengths, maxp, group, kv, pages, flags, listed, sems, out, held, per_held
        )


def fresh_kernel(held, per_held, qa, new_kv, out):
    rows = qa.shape[0]
    q = query_block(qa, held, per_held)
    count = q.shape[0]
    lane_row = lax.rem(lax.broadcasted_iota(jnp.int32, (1, count), 1), rows)
    fresh = new_kv[...].astype(jnp.float32)
    fresh = jnp.concatenate([fresh, jnp.zeros_like(fresh)], 0).astype(jnp.bfloat16)
    mask = lax.broadcasted_iota(jnp.int32, (2 * rows, count), 0) == lane_row
    s = jnp.where(mask, dot(lanes_of(fresh, 0, held), q, 1, 1) * SCALE, NEG)
    top = jnp.max(s, 0, keepdims=True)
    p = jnp.exp(s - top)
    acc = dot(p.astype(jnp.bfloat16), lanes_of(fresh, 1, held), 0, 0)
    write_part(out, acc, top, jnp.sum(p, 0, keepdims=True), held, per_held)


def second_kernel(held, per_held, maxp, count, chosen, entries, *refs):
    qas, outs = refs[:count][::-1], refs[count:]

    @pl.when(lax.axis_index("role") == 0)
    def _():
        for k in range(count):
            at = (k + 1) * PARTS
            owner_part(
                qas[k], chosen.at[pl.ds(at, PARTS)], entries[at : at + PARTS, :], outs[k], held, per_held, maxp
            )


def merge_kernel(heads, rows, *refs):
    parts, out = refs[:-1], refs[-1]
    count = heads * rows
    pad = -len(parts) % 8
    stats = [part[count:, :].astype(jnp.float32)[:, :count] for part in parts]
    tops = jnp.concatenate([s[0:1] + (s[1:2] + s[2:3]) for s in stats], 0)
    totals = jnp.concatenate([s[3:4] + (s[4:5] + s[5:6]) for s in stats], 0)
    factors = jnp.exp(tops - jnp.max(tops, 0, keepdims=True))
    factors = factors / jnp.sum(factors * totals, 0, keepdims=True)
    factors = jnp.concatenate([factors, jnp.zeros((pad, count), jnp.float32)], 0).T
    terms = [factors[:, i : i + 1] * part[:count, :].astype(jnp.float32) for i, part in enumerate(parts)]
    merged = functools.reduce(jnp.add, terms)
    out[...] = jnp.concatenate([merged[h * rows : (h + 1) * rows] for h in range(heads)], 1).astype(out.dtype)


def project_kernel(steps, attended, partner, weight, *outs):
    tps = lax.axis_size("tp")
    share = outs[0].shape[1]
    here = jnp.where(lax.axis_index("role") == 0, partner[...].astype(jnp.float32), attended[...].astype(jnp.float32))
    here = here.astype(jnp.bfloat16)
    for d, out in zip(steps, outs):
        first = lax.rem(lax.axis_index("tp") + d, tps) * share
        columns = pl.ds(pl.multiple_of(first, LANES), share)
        out[...] = jnp.dot(here, weight[:, columns], preferred_element_type=jnp.float32).astype(out.dtype)


def per_device(kv_pages, send_list, wanted, lengths, tables, queries, new_kv, out_weight):
    stored = kv_pages[0, 0, 0]
    slots = stored.shape[0]
    groups, tps = lax.axis_size("group"), lax.axis_size("tp")
    held = max(1, KVH // tps)
    rows, wide = queries.shape[1], queries.shape[2]
    heads = wide // HD
    per_held = heads // held
    maxp = tables.shape[2]
    send = jnp.transpose(send_list, (2, 0, 1))
    def place(block, at):
        return jnp.pad(block, ((0, rows - block.shape[0]), (at, wide + LANES - at - block.shape[1])))

    high = lax.shift_right_logical(place(lengths, wide + maxp), 3)
    low = jnp.bitwise_and(place(lengths, wide + maxp + rows), 7)
    integers = place(tables[0], wide) + high + low
    qa = place(queries[0], 0) + integers.astype(jnp.bfloat16)
    def paired(value, k, to_decode):
        first, second = (0, groups) if to_decode else (groups, 0)
        pairs = [pair for i in range(groups) for pair in ((first + i, second + (i ^ k)), (second + i, first + i))]
        return lax.ppermute(value, ("role", "group"), pairs)

    asked = [paired(qa, k, False) for k in range(1, groups)]
    part_shape = jax.ShapeDtypeStruct((heads * rows + STATS, HD), jnp.float32)
    sent_shape = jax.ShapeDtypeStruct(part_shape.shape, jnp.bfloat16)
    vmem = pl.BlockSpec(memory_space=pltpu.VMEM)
    hbm = pl.BlockSpec(memory_space=pltpu.HBM)
    page_shape = stored.shape[1:]
    chosen_count = groups * PARTS
    read_count = -(-rows * maxp // CHUNK) * CHUNK
    lists = [send, wanted, tables[0], lengths]
    pinned = [pltpu.with_memory_space_constraint(x, pltpu.HBM) for x in lists + [stored]]
    smem = [pltpu.SMEM(x.shape, jnp.int32) for x in lists]
    reading = [pltpu.SMEM((slots + 1,), jnp.int32), pltpu.SMEM((2, read_count), jnp.int32)]
    mine, mine_sent, chosen, entries = pl.pallas_call(
        functools.partial(first_kernel, held, per_held, groups, maxp),
        out_shape=[
            part_shape,
            sent_shape,
            jax.ShapeDtypeStruct((chosen_count,) + page_shape, jnp.bfloat16),
            jax.ShapeDtypeStruct((chosen_count, LANES), jnp.float32),
        ],
        in_specs=[vmem] + [hbm] * 5,
        out_specs=[vmem] * 4,
        scratch_shapes=[
            pltpu.VMEM((read_count,) + page_shape, jnp.bfloat16),
            *smem,
            *reading,
            pltpu.SMEM((chosen_count + 1,), jnp.int32),
            pltpu.SMEM((chosen_count + 1,), jnp.int32),
            pltpu.SemaphoreType.DMA((len(lists),)),
            pltpu.SemaphoreType.DMA((chosen_count,)),
            pltpu.SemaphoreType.DMA((read_count,)),
        ],
        compiler_params=pltpu.CompilerParams(vmem_limit_bytes=20 * MIB),
        name="resident",
    )(qa, *pinned)
    count = groups - 1
    theirs = pl.pallas_call(
        functools.partial(second_kernel, held, per_held, maxp, count),
        out_shape=[sent_shape] * count,
        in_specs=[vmem] * (2 + count),
        out_specs=[vmem] * count,
        compiler_params=pltpu.CompilerParams(vmem_limit_bytes=16 * MIB),
        cost_estimate=pl.CostEstimate(flops=4 * 10**10, bytes_accessed=8 * MIB, transcendentals=10**6),
        name="owned",
    )(chosen, entries, *reversed(asked))
    qa, mine_sent, theirs = lax.optimization_barrier((qa, mine_sent, theirs))
    fresh = pl.pallas_call(
        functools.partial(fresh_kernel, held, per_held),
        out_shape=part_shape,
        in_specs=[vmem] * 2,
        out_specs=vmem,
        compiler_params=pltpu.CompilerParams(vmem_limit_bytes=8 * MIB),
        cost_estimate=pl.CostEstimate(flops=10**9, bytes_accessed=MIB, transcendentals=10**4),
        name="fresh",
    )(qa, new_kv[0])
    parts = [mine, fresh] + [paired(part, k, True) for k, part in enumerate([mine_sent, *theirs])]
    attended = pl.pallas_call(
        functools.partial(merge_kernel, heads, rows),
        out_shape=jax.ShapeDtypeStruct((rows, wide), jnp.bfloat16),
        in_specs=[vmem] * len(parts),
        out_specs=vmem,
        compiler_params=pltpu.CompilerParams(vmem_limit_bytes=8 * MIB),
        name="merge",
    )(*parts)
    partner = lax.ppermute(attended, "role", [(0, 1), (1, 0)])
    share = out_weight.shape[1] // tps

    def project(steps, dtype, name):
        return pl.pallas_call(
            functools.partial(project_kernel, steps),
            out_shape=[jax.ShapeDtypeStruct((rows, share), dtype)] * len(steps),
            in_specs=[vmem] * 3,
            out_specs=[vmem] * len(steps),
            compiler_params=pltpu.CompilerParams(vmem_limit_bytes=24 * MIB),
            cost_estimate=pl.CostEstimate(
                flops=len(steps) * 32 * wide * share, bytes_accessed=len(steps) * 2 * wide * share, transcendentals=0
            ),
            name=name,
        )(attended, partner, out_weight)

    steps = list(range(1, tps))
    sent = project(steps, jnp.bfloat16, "project")
    arrived = [lax.ppermute(part, "tp", [(i, (i + d) % tps) for i in range(tps)]) for d, part in zip(steps, sent)]
    own = project([0], jnp.float32, "project_own")[0]
    total = functools.reduce(jnp.add, [part.astype(jnp.float32) for part in arrived], own)
    return total.astype(jnp.bfloat16)[None]


def solution(mesh):
    return jax.shard_map(
        per_device,
        mesh=mesh,
        in_specs=(
            P("role", "group", "tp", None, None, None),
            P(),
            P(),
            P("group", None),
            P("group", None, None),
            P("group", None, "tp"),
            P("group", None, "tp"),
            P("tp", "role"),
        ),
        out_specs=P("group", None, ("role", "tp")),
        check_vma=False,
    )
```

profile of v0, /device:TPU:0, one launch (start us, length us, event | category | flops | bytes accessed | tf_op | source)
XLA Modules:
  0.0 29.1 jit_solution(1736724789320082307)
XLA Ops:
  0.0 0.9 %fusion.qa = bf16[8,2176]{1,0:T(8,128)(2,1)S(1)} fusion(s32[1,8]{1,0:T(1,128)} %lengths_hbm.1, s32[8,8]{1,0:T(8,128)} %bitcast.12, bf16[8,2048]{1,0:T(8,128)(2,1)} %bitcast.11), kind=kLoop, calls=%fused_computation.1 | loop fusion | flops 156672 | bytes 67872 | tf_op jit(solution)/shard_map/add | solution.py:327
  0.9 0.5 %collective-permute-start.2 = (bf16[8,2176]{1,0:T(8,128)(2,1)S(1)}, bf16[8,2176]{1,0:T(8,128)(2,1)S(1)}, u32[]{:S(2)}, u32[]{:S(2)}) collective-permute-start(bf16[8,2176]{1,0:T(8,128)(2,1)S(1)} %fusion.qa), channel_id=1, source_target_pairs={{16,4},{0,16},{20,0},{4,20},{24,12},{8,24},{28,8},{12,28},{17,5},{... | collective-permute-start | bytes 104456 | tf_op jit(solution)/shard_map/ppermute | solution.py:331
  1.3 2.7 %collective-permute-start.1 = (bf16[8,2176]{1,0:T(8,128)(2,1)S(1)}, bf16[8,2176]{1,0:T(8,128)(2,1)S(1)}, u32[]{:S(2)}, u32[]{:S(2)}) collective-permute-start(bf16[8,2176]{1,0:T(8,128)(2,1)S(1)} %fusion.qa), channel_id=1, source_target_pairs={{16,8},{0,16},{20,12},{4,20},{24,0},{8,24},{28,4},{12,28},{17,9},{... | collective-permute-start | bytes 104456 | tf_op jit(solution)/shard_map/ppermute | solution.py:331
  4.0 1.1 %collective-permute-start = (bf16[8,2176]{1,0:T(8,128)(2,1)S(1)}, bf16[8,2176]{1,0:T(8,128)(2,1)S(1)}, u32[]{:S(2)}, u32[]{:S(2)}) collective-permute-start(bf16[8,2176]{1,0:T(8,128)(2,1)S(1)} %fusion.qa), channel_id=1, source_target_pairs={{16,12},{0,16},{20,8},{4,20},{24,4},{8,24},{28,0},{12,28},{17,13},... | collective-permute-start | bytes 104456 | tf_op jit(solution)/shard_map/ppermute | solution.py:331
  5.1 3.7 %resident.1 = (f32[144,128]{1,0:T(8,128)S(1)}, bf16[144,128]{1,0:T(8,128)(2,1)S(1)}, bf16[24,128,512]{2,1,0:T(8,128)(2,1)S(1)}, f32[24,128]{1,0:T(8,128)S(1)}) custom-call(bf16[8,2176]{1,0:T(8,128)(2,1)S(1)} %fusion.qa, s32[3,4,12]{2,1,0:T(4,128)} %bitcast.14, s32[4,6]{1,0:T(4,128)} %wanted_hbm.1, s32[8,8]{1,0:T(8,128)} %bitcast.13, s32[1,8]{1,0:T(1,128)} %lengths_hbm.1, ...), custom_call_target="tpu_custom_call" | custom-call | tf_op jit(solution)/shard_map/resident/pallas_call | solution.py:345
  8.9 0.3 %collective-permute-done.refs_0_ = bf16[8,2176]{1,0:T(8,128)(2,1)S(1)} collective-permute-done((bf16[8,2176]{1,0:T(8,128)(2,1)S(1)}, bf16[8,2176]{1,0:T(8,128)(2,1)S(1)}, u32[]{:S(2)}, u32[]{:S(2)}) %collective-permute-start) | collective-permute-done | bytes 34848 | tf_op jit(solution)/shard_map/ppermute | solution.py:331
  9.2 1.9 %owned.1 = (bf16[144,128]{1,0:T(8,128)(2,1)S(1)}, bf16[144,128]{1,0:T(8,128)(2,1)S(1)}, bf16[144,128]{1,0:T(8,128)(2,1)S(1)}) custom-call(bf16[24,128,512]{2,1,0:T(8,128)(2,1)S(1)} %get-tuple-element.22.chosen, f32[24,128]{1,0:T(8,128)S(1)} %get-tuple-element.23.entries, bf16[8,2176]{1,0:T(8,128)(2,1)S(1)} %collective-permute-done.refs_0_, ...), custom_call_target="tpu_custom_call" | custom-call | flops 40000000000 | bytes 8388608 | tf_op jit(solution)/shard_map/owned/pallas_call | solution.py:369
  11.1 1.0 %collective-permute-start.3 = (bf16[144,128]{1,0:T(8,128)(2,1)S(1)}, bf16[144,128]{1,0:T(8,128)(2,1)S(1)}, u32[]{:S(2)}, u32[]{:S(2)}) collective-permute-start(bf16[144,128]{1,0:T(8,128)(2,1)S(1)} %get-tuple-element.28), channel_id=1, source_target_pairs={{0,16},{16,0},{4,20},{20,4},{8,24},{24,8},{12,28},{28,12},{1,17},{... | collective-permute-start | bytes 110600 | tf_op jit(solution)/shard_map/ppermute | solution.py:331
  12.0 0.9 %collective-permute-start.4 = (bf16[144,128]{1,0:T(8,128)(2,1)S(1)}, bf16[144,128]{1,0:T(8,128)(2,1)S(1)}, u32[]{:S(2)}, u32[]{:S(2)}) collective-permute-start(bf16[144,128]{1,0:T(8,128)(2,1)S(1)} %get-tuple-element.29), channel_id=1, source_target_pairs={{0,20},{16,0},{4,16},{20,4},{8,28},{24,8},{12,24},{28,12},{1,21},{... | collective-permute-start | bytes 110600 | tf_op jit(solution)/shard_map/ppermute | solution.py:331
  13.0 1.1 %collective-permute-start.6 = (bf16[144,128]{1,0:T(8,128)(2,1)S(1)}, bf16[144,128]{1,0:T(8,128)(2,1)S(1)}, u32[]{:S(2)}, u32[]{:S(2)}) collective-permute-start(bf16[144,128]{1,0:T(8,128)(2,1)S(1)} %get-tuple-element.31), channel_id=1, source_target_pairs={{0,28},{16,0},{4,24},{20,4},{8,20},{24,8},{12,16},{28,12},{1,29},{... | collective-permute-start | bytes 110600 | tf_op jit(solution)/shard_map/ppermute | solution.py:331
  14.1 0.4 %fresh.1.refs_1_ = f32[144,128]{1,0:T(8,128)S(1)} custom-call(bf16[8,2176]{1,0:T(8,128)(2,1)S(1)} %fusion.qa, bf16[8,512]{1,0:T(8,128)(2,1)S(1)} %bitcast.9), custom_call_target="tpu_custom_call" | custom-call | flops 1000000000 | bytes 1048576 | tf_op jit(solution)/shard_map/fresh/pallas_call | solution.py:379
  14.4 0.1 collective-permute-done.4.refs_3_
  14.6 0.3 %collective-permute-done.5.refs_4_ = bf16[144,128]{1,0:T(8,128)(2,1)S(1)} collective-permute-done((bf16[144,128]{1,0:T(8,128)(2,1)S(1)}, bf16[144,128]{1,0:T(8,128)(2,1)S(1)}, u32[]{:S(2)}, u32[]{:S(2)}) %collective-permute-start.5) | collective-permute-done | bytes 36896 | tf_op jit(solution)/shard_map/ppermute | solution.py:331
  14.9 0.8 %collective-permute-done.6.refs_5_ = bf16[144,128]{1,0:T(8,128)(2,1)S(1)} collective-permute-done((bf16[144,128]{1,0:T(8,128)(2,1)S(1)}, bf16[144,128]{1,0:T(8,128)(2,1)S(1)}, u32[]{:S(2)}, u32[]{:S(2)}) %collective-permute-start.6) | collective-permute-done | bytes 36896 | tf_op jit(solution)/shard_map/ppermute | solution.py:331
  15.7 0.3 %merge.1.attended = bf16[8,2048]{1,0:T(8,128)(2,1)S(1)} custom-call(f32[144,128]{1,0:T(8,128)S(1)} %get-tuple-element.20.refs_0_, f32[144,128]{1,0:T(8,128)S(1)} %fresh.1.refs_1_, bf16[144,128]{1,0:T(8,128)(2,1)S(1)} %collective-permute-done.3.refs_2_, bf16[144,128]{1,0:T(8,128)(2,1)S(1)} %collective-permute-done.4.refs_3_, ...), custom_call_target="tpu_custom_call" | custom-call | tf_op jit(solution)/shard_map/merge/pallas_call | solution.py:389
  16.0 3.0 %collective-permute-start.7 = (bf16[8,2048]{1,0:T(8,128)(2,1)S(1)}, bf16[8,2048]{1,0:T(8,128)(2,1)S(1)}, u32[]{:S(2)}, u32[]{:S(2)}) collective-permute-start(bf16[8,2048]{1,0:T(8,128)(2,1)S(1)} %merge.1.attended), channel_id=1, source_target_pairs={{0,16},{16,0},{1,17},{17,1},{2,18},{18,2},{3,19},{19,3},{4,20},{20... | collective-permute-start | bytes 98312 | tf_op jit(solution)/shard_map/ppermute | solution.py:397
  19.1 0.9 %collective-permute-done.7.partner = bf16[8,2048]{1,0:T(8,128)(2,1)S(1)} collective-permute-done((bf16[8,2048]{1,0:T(8,128)(2,1)S(1)}, bf16[8,2048]{1,0:T(8,128)(2,1)S(1)}, u32[]{:S(2)}, u32[]{:S(2)}) %collective-permute-start.7) | collective-permute-done | bytes 32800 | tf_op jit(solution)/shard_map/ppermute | solution.py:397
  19.9 1.7 %project.1 = (bf16[8,1024]{1,0:T(8,128)(2,1)S(1)}, bf16[8,1024]{1,0:T(8,128)(2,1)S(1)}, bf16[8,1024]{1,0:T(8,128)(2,1)S(1)}) custom-call(bf16[8,2048]{1,0:T(8,128)(2,1)S(1)} %merge.1.attended, bf16[8,2048]{1,0:T(8,128)(2,1)S(1)} %collective-permute-done.7.partner, bf16[2048,4096]{1,0:T(8,128)(2,1)S(1)} %bitcast.8), custom_call_target="tpu_custom_call" | custom-call | flops 201326592 | bytes 12582912 | tf_op jit(solution)/shard_map/project/pallas_call | solution.py:401
  21.7 1.5 %collective-permute-start.8 = (bf16[8,1024]{1,0:T(8,128)(2,1)S(1)}, bf16[8,1024]{1,0:T(8,128)(2,1)S(1)}, u32[]{:S(2)}, u32[]{:S(2)}) collective-permute-start(bf16[8,1024]{1,0:T(8,128)(2,1)S(1)} %get-tuple-element.32), channel_id=1, source_target_pairs={{0,1},{1,2},{2,3},{3,0},{4,5},{5,6},{6,7},{7,4},{8,9},{9,10},{10,1... | collective-permute-start | bytes 49160 | tf_op jit(solution)/shard_map/ppermute | solution.py:415
  23.2 1.5 %collective-permute-start.9 = (bf16[8,1024]{1,0:T(8,128)(2,1)S(1)}, bf16[8,1024]{1,0:T(8,128)(2,1)S(1)}, u32[]{:S(2)}, u32[]{:S(2)}) collective-permute-start(bf16[8,1024]{1,0:T(8,128)(2,1)S(1)} %get-tuple-element.33), channel_id=1, source_target_pairs={{0,2},{1,3},{2,0},{3,1},{4,6},{5,7},{6,4},{7,5},{8,10},{9,11},{10,... | collective-permute-start | bytes 49160 | tf_op jit(solution)/shard_map/ppermute | solution.py:415
  24.7 1.4 %collective-permute-start.10 = (bf16[8,1024]{1,0:T(8,128)(2,1)S(1)}, bf16[8,1024]{1,0:T(8,128)(2,1)S(1)}, u32[]{:S(2)}, u32[]{:S(2)}) collective-permute-start(bf16[8,1024]{1,0:T(8,128)(2,1)S(1)} %get-tuple-element.34), channel_id=1, source_target_pairs={{0,3},{1,0},{2,1},{3,2},{4,7},{5,4},{6,5},{7,6},{8,11},{9,8},{10,9... | collective-permute-start | bytes 49160 | tf_op jit(solution)/shard_map/ppermute | solution.py:415
  26.1 0.6 %project_own.1 = f32[8,1024]{1,0:T(8,128)S(1)} custom-call(bf16[8,2048]{1,0:T(8,128)(2,1)S(1)} %merge.1.attended, bf16[8,2048]{1,0:T(8,128)(2,1)S(1)} %collective-permute-done.7.partner, bf16[2048,4096]{1,0:T(8,128)(2,1)S(1)} %bitcast.8), custom_call_target="tpu_custom_call" | custom-call | flops 67108864 | bytes 4194304 | tf_op jit(solution)/shard_map/project_own/pallas_call | solution.py:401
  26.9 1.5 %collective-permute-done.10 = bf16[8,1024]{1,0:T(8,128)(2,1)S(1)} collective-permute-done((bf16[8,1024]{1,0:T(8,128)(2,1)S(1)}, bf16[8,1024]{1,0:T(8,128)(2,1)S(1)}, u32[]{:S(2)}, u32[]{:S(2)}) %collective-permute-start.10) | collective-permute-done | bytes 16416 | tf_op jit(solution)/shard_map/ppermute | solution.py:415
  28.4 0.6 %fusion.1 = bf16[1,8,1024]{2,1,0:T(8,128)(2,1)} fusion(bf16[8,1024]{1,0:T(8,128)(2,1)S(1)} %collective-permute-done.10, bf16[8,1024]{1,0:T(8,128)(2,1)S(1)} %collective-permute-done.9, f32[8,1024]{1,0:T(8,128)S(1)} %project_own.1, bf16[8,1024]{1,0:T(8,128)(2,1)S(1)} %collective-permute-done.8), kind=kLoop, calls=%fused_computation.3 | loop fusion | flops 57344 | bytes 98304 | tf_op jit(solution)/shard_map/broadcast_in_dim | solution.py:418
  (17 shorter events, 0.2 us)
Async XLA Ops:
  0.9 8.0 %collective-permute-start.2 = (bf16[8,2176]{1,0:T(8,128)(2,1)S(1)}, bf16[8,2176]{1,0:T(8,128)(2,1)S(1)}, u32[]{:S(2)}, u32[]{:S(2)}) collective-permute-start(bf16[8,2176]{1,0:T(8,128)(2,1)S(1)} %fusion.qa), channel_id=1, source_target_pairs={{16,4},{0,16},{20,0},{4,20},{24,12},{8,24},{28,8},{12,28},{17,5},{... | collective-permute-start | bytes 104456 | tf_op jit(solution)/shard_map/ppermute | solution.py:331
  1.3 7.5 %collective-permute-start.1 = (bf16[8,2176]{1,0:T(8,128)(2,1)S(1)}, bf16[8,2176]{1,0:T(8,128)(2,1)S(1)}, u32[]{:S(2)}, u32[]{:S(2)}) collective-permute-start(bf16[8,2176]{1,0:T(8,128)(2,1)S(1)} %fusion.qa), channel_id=1, source_target_pairs={{16,8},{0,16},{20,12},{4,20},{24,0},{8,24},{28,4},{12,28},{17,9},{... | collective-permute-start | bytes 104456 | tf_op jit(solution)/shard_map/ppermute | solution.py:331
  4.0 5.2 %collective-permute-start = (bf16[8,2176]{1,0:T(8,128)(2,1)S(1)}, bf16[8,2176]{1,0:T(8,128)(2,1)S(1)}, u32[]{:S(2)}, u32[]{:S(2)}) collective-permute-start(bf16[8,2176]{1,0:T(8,128)(2,1)S(1)} %fusion.qa), channel_id=1, source_target_pairs={{16,12},{0,16},{20,8},{4,20},{24,4},{8,24},{28,0},{12,28},{17,13},... | collective-permute-start | bytes 104456 | tf_op jit(solution)/shard_map/ppermute | solution.py:331
  9.2 10.7 %slice-start = ((s8[16777216]{0:T(1024)(128)(4,1)}), s8[4194304]{0:T(1024)(128)(4,1)S(1)}, s32[]{:S(2)}) async-start(s8[16777216]{0:T(1024)(128)(4,1)} %bitcast.7), calls=%async_computation | async-start | bytes 8388608
  9.2 4.9 %copy-start = (bf16[1,8,512]{2,1,0:T(8,128)(2,1)S(1)}, bf16[1,8,512]{2,1,0:T(8,128)(2,1)}, u32[]{:S(2)}) copy-start(bf16[1,8,512]{2,1,0:T(8,128)(2,1)} %param.14) | copy-start | bytes 24580
  9.2 10.7 %slice-start.1 = ((s8[16777216]{0:T(1024)(128)(4,1)}), s8[4194304]{0:T(1024)(128)(4,1)S(1)}, s32[]{:S(2)}) async-start(s8[16777216]{0:T(1024)(128)(4,1)} %bitcast.7), calls=%async_computation.1 | async-start | bytes 8388608
  9.2 10.7 %slice-start.2 = ((s8[16777216]{0:T(1024)(128)(4,1)}), s8[4194304]{0:T(1024)(128)(4,1)S(1)}, s32[]{:S(2)}) async-start(s8[16777216]{0:T(1024)(128)(4,1)} %bitcast.7), calls=%async_computation.2 | async-start | bytes 8388608
  9.2 10.7 %slice-start.3 = ((s8[16777216]{0:T(1024)(128)(4,1)}), s8[4194304]{0:T(1024)(128)(4,1)S(1)}, s32[]{:S(2)}) async-start(s8[16777216]{0:T(1024)(128)(4,1)} %bitcast.7), calls=%async_computation.3 | async-start | bytes 8388608
  11.1 3.4 %collective-permute-start.3 = (bf16[144,128]{1,0:T(8,128)(2,1)S(1)}, bf16[144,128]{1,0:T(8,128)(2,1)S(1)}, u32[]{:S(2)}, u32[]{:S(2)}) collective-permute-start(bf16[144,128]{1,0:T(8,128)(2,1)S(1)} %get-tuple-element.28), channel_id=1, source_target_pairs={{0,16},{16,0},{4,20},{20,4},{8,24},{24,8},{12,28},{28,12},{1,17},{... | collective-permute-start | bytes 110600 | tf_op jit(solution)/shard_map/ppermute | solution.py:331
  12.0 2.6 %collective-permute-start.4 = (bf16[144,128]{1,0:T(8,128)(2,1)S(1)}, bf16[144,128]{1,0:T(8,128)(2,1)S(1)}, u32[]{:S(2)}, u32[]{:S(2)}) collective-permute-start(bf16[144,128]{1,0:T(8,128)(2,1)S(1)} %get-tuple-element.29), channel_id=1, source_target_pairs={{0,20},{16,0},{4,16},{20,4},{8,28},{24,8},{12,24},{28,12},{1,21},{... | collective-permute-start | bytes 110600 | tf_op jit(solution)/shard_map/ppermute | solution.py:331
  13.0 2.0 %collective-permute-start.5 = (bf16[144,128]{1,0:T(8,128)(2,1)S(1)}, bf16[144,128]{1,0:T(8,128)(2,1)S(1)}, u32[]{:S(2)}, u32[]{:S(2)}) collective-permute-start(bf16[144,128]{1,0:T(8,128)(2,1)S(1)} %get-tuple-element.30), channel_id=1, source_target_pairs={{0,24},{16,0},{4,28},{20,4},{8,16},{24,8},{12,20},{28,12},{1,25},{... | collective-permute-start | bytes 110600 | tf_op jit(solution)/shard_map/ppermute | solution.py:331
  13.0 2.8 %collective-permute-start.6 = (bf16[144,128]{1,0:T(8,128)(2,1)S(1)}, bf16[144,128]{1,0:T(8,128)(2,1)S(1)}, u32[]{:S(2)}, u32[]{:S(2)}) collective-permute-start(bf16[144,128]{1,0:T(8,128)(2,1)S(1)} %get-tuple-element.31), channel_id=1, source_target_pairs={{0,28},{16,0},{4,24},{20,4},{8,20},{24,8},{12,16},{28,12},{1,29},{... | collective-permute-start | bytes 110600 | tf_op jit(solution)/shard_map/ppermute | solution.py:331
  16.0 3.9 %collective-permute-start.7 = (bf16[8,2048]{1,0:T(8,128)(2,1)S(1)}, bf16[8,2048]{1,0:T(8,128)(2,1)S(1)}, u32[]{:S(2)}, u32[]{:S(2)}) collective-permute-start(bf16[8,2048]{1,0:T(8,128)(2,1)S(1)} %merge.1.attended), channel_id=1, source_target_pairs={{0,16},{16,0},{1,17},{17,1},{2,18},{18,2},{3,19},{19,3},{4,20},{20... | collective-permute-start | bytes 98312 | tf_op jit(solution)/shard_map/ppermute | solution.py:397
  21.7 5.1 %collective-permute-start.8 = (bf16[8,1024]{1,0:T(8,128)(2,1)S(1)}, bf16[8,1024]{1,0:T(8,128)(2,1)S(1)}, u32[]{:S(2)}, u32[]{:S(2)}) collective-permute-start(bf16[8,1024]{1,0:T(8,128)(2,1)S(1)} %get-tuple-element.32), channel_id=1, source_target_pairs={{0,1},{1,2},{2,3},{3,0},{4,5},{5,6},{6,7},{7,4},{8,9},{9,10},{10,1... | collective-permute-start | bytes 49160 | tf_op jit(solution)/shard_map/ppermute | solution.py:415
  23.2 3.7 %collective-permute-start.9 = (bf16[8,1024]{1,0:T(8,128)(2,1)S(1)}, bf16[8,1024]{1,0:T(8,128)(2,1)S(1)}, u32[]{:S(2)}, u32[]{:S(2)}) collective-permute-start(bf16[8,1024]{1,0:T(8,128)(2,1)S(1)} %get-tuple-element.33), channel_id=1, source_target_pairs={{0,2},{1,3},{2,0},{3,1},{4,6},{5,7},{6,4},{7,5},{8,10},{9,11},{10,... | collective-permute-start | bytes 49160 | tf_op jit(solution)/shard_map/ppermute | solution.py:415
  24.7 3.7 %collective-permute-start.10 = (bf16[8,1024]{1,0:T(8,128)(2,1)S(1)}, bf16[8,1024]{1,0:T(8,128)(2,1)S(1)}, u32[]{:S(2)}, u32[]{:S(2)}) collective-permute-start(bf16[8,1024]{1,0:T(8,128)(2,1)S(1)} %get-tuple-element.34), channel_id=1, source_target_pairs={{0,3},{1,0},{2,1},{3,2},{4,7},{5,4},{6,5},{7,6},{8,11},{9,8},{10,9... | collective-permute-start | bytes 49160 | tf_op jit(solution)/shard_map/ppermute | solution.py:415
where the time goes:
time: 29.1 us
  starting transfers between devices  14.7 us (51%)
  Pallas kernels  8.66 us (30%)
  waiting for transfers between devices  4.11 us (14%)
  other arithmetic  1.5 us (5%)
    ppermute x7, starting transfers between devices, paired(): return lax.ppermute(value, ('role', 'group'), pairs)  7.21 us
    ppermute x3, starting transfers between devices, per_device(): lax.ppermute(part, 'tp', [(i, (i + d) % tps) for i in range(tps)])  4.46 us
    pallas_call x1, Pallas kernels, per_device(): pl.pallas_call(functools.partial(first_kernel, held, per_held, groups, ma...  3.74 us
    ppermute x1, starting transfers between devices, per_device(): partner = lax.ppermute(attended, 'role', [(0, 1), (1, 0)])  3 us
    pallas_call x2, Pallas kernels, project(): pl.pallas_call(functools.partial(project_kernel, steps), out_shape=[jax.S...  2.38 us
    pallas_call x1, Pallas kernels, per_device(): pl.pallas_call(functools.partial(second_kernel, held, per_held, maxp, cou...  1.85 us
    ppermute x3, waiting for transfers between devices, per_device(): lax.ppermute(part, 'tp', [(i, (i + d) % tps) for i in range(tps)])  1.66 us
    ppermute x7, waiting for transfers between devices, paired(): return lax.ppermute(value, ('role', 'group'), pairs)  1.59 us
  transfers between devices with their start and end apart: 11, of which 7 were waited for; matrix products, arithmetic and copies ran while one was open for 0% of the time, Pallas kernels for 16%

commit v1 on v0

--- a/solution.py
+++ b/solution.py
@@ -19,8 +19,8 @@
 FLOOR = -1e29
 SCALE = 1.0 / math.sqrt(HD)
 PARTS = CAP + CAPP
-CHUNK = 4
-STATIC = (4, 5, 6, 7, 8)
+CHUNK = 8
+STATIC = (2, 3, 4, 5)
 STATS = 16
 MIB = 2**20
 
@@ -385,7 +385,7 @@
         cost_estimate=pl.CostEstimate(flops=10**9, bytes_accessed=MIB, transcendentals=10**4),
         name="fresh",
     )(qa, new_kv[0])
-    parts = [mine, fresh] + [paired(part, k, True) for k, part in enumerate([mine_sent, *theirs])]
+    parts = [mine, fresh] + [paired(part, k, True) for k, part in enumerate([mine_sent, *theirs])][::-1]
     attended = pl.pallas_call(
         functools.partial(merge_kernel, heads, rows),
         out_shape=jax.ShapeDtypeStruct((rows, wide), jnp.bfloat16),

time: 29.1 us -> 28.1 us (0.966); the launches traced: 29.1 us -> 27.7 us
  starting transfers between devices: 14.7 us -> 13.3 us
    ppermute x1, starting transfers between devices: 3 us -> 2.17 us  [per_device(): partner = lax.ppermute(attended, 'role', [(0, 1), (1, 0)])]
    ppermute x7, starting transfers between devices: 7.21 us -> 6.66 us  [paired(): return lax.ppermute(value, ('role', 'group'), pairs)]
  transfers between devices with their start and end apart: 11 -> 11, of which waited for: 7 -> 7; matrix products, arithmetic and copies ran while one was open for 0% -> 0% of each run, Pallas kernels for 16% -> 17%
where the time goes in v1:
time: 28.1 us; the launch traced here: 27.7 us
  starting transfers between devices  13.3 us (47%)
  Pallas kernels  8.48 us (30%)
  waiting for transfers between devices  4.3 us (15%)
  other arithmetic  1.5 us (5%)
    ppermute x7, starting transfers between devices, paired(): return lax.ppermute(value, ('role', 'group'), pairs)  6.66 us
    ppermute x3, starting transfers between devices, per_device(): lax.ppermute(part, 'tp', [(i, (i + d) % tps) for i in range(tps)])  4.46 us
    pallas_call x1, Pallas kernels, per_device(): pl.pallas_call(functools.partial(first_kernel, held, per_held, groups, ma...  3.74 us
    pallas_call x2, Pallas kernels, project(): pl.pallas_call(functools.partial(project_kernel, steps), out_shape=[jax.S...  2.38 us
    ppermute x1, starting transfers between devices, per_device(): partner = lax.ppermute(attended, 'role', [(0, 1), (1, 0)])  2.17 us
    ppermute x7, waiting for transfers between devices, paired(): return lax.ppermute(value, ('role', 'group'), pairs)  1.78 us
    pallas_call x1, Pallas kernels, per_device(): pl.pallas_call(functools.partial(second_kernel, held, per_held, maxp, cou...  1.67 us
    ppermute x3, waiting for transfers between devices, per_device(): lax.ppermute(part, 'tp', [(i, (i + d) % tps) for i in range(tps)])  1.66 us
  transfers between devices with their start and end apart: 11, of which 7 were waited for; matrix products, arithmetic and copies ran while one was open for 0% of the time, Pallas kernels for 17%

profile of v1, /device:TPU:0, one launch (start us, length us, event | category | flops | bytes accessed | tf_op | source)
XLA Modules:
  0.0 27.7 jit_solution(16926769414141778549)
XLA Ops:
  0.0 0.9 %fusion.qa = bf16[8,2176]{1,0:T(8,128)(2,1)S(1)} fusion(s32[1,8]{1,0:T(1,128)} %lengths_hbm.1, s32[8,8]{1,0:T(8,128)} %bitcast.12, bf16[8,2048]{1,0:T(8,128)(2,1)} %bitcast.11), kind=kLoop, calls=%fused_computation.1 | loop fusion | flops 156672 | bytes 67872 | tf_op jit(solution)/shard_map/add | solution.py:327
  0.9 0.5 %collective-permute-start.2 = (bf16[8,2176]{1,0:T(8,128)(2,1)S(1)}, bf16[8,2176]{1,0:T(8,128)(2,1)S(1)}, u32[]{:S(2)}, u32[]{:S(2)}) collective-permute-start(bf16[8,2176]{1,0:T(8,128)(2,1)S(1)} %fusion.qa), channel_id=1, source_target_pairs={{16,4},{0,16},{20,0},{4,20},{24,12},{8,24},{28,8},{12,28},{17,5},{... | collective-permute-start | bytes 104456 | tf_op jit(solution)/shard_map/ppermute | solution.py:331
  1.3 2.7 %collective-permute-start.1 = (bf16[8,2176]{1,0:T(8,128)(2,1)S(1)}, bf16[8,2176]{1,0:T(8,128)(2,1)S(1)}, u32[]{:S(2)}, u32[]{:S(2)}) collective-permute-start(bf16[8,2176]{1,0:T(8,128)(2,1)S(1)} %fusion.qa), channel_id=1, source_target_pairs={{16,8},{0,16},{20,12},{4,20},{24,0},{8,24},{28,4},{12,28},{17,9},{... | collective-permute-start | bytes 104456 | tf_op jit(solution)/shard_map/ppermute | solution.py:331
  4.0 1.1 %collective-permute-start = (bf16[8,2176]{1,0:T(8,128)(2,1)S(1)}, bf16[8,2176]{1,0:T(8,128)(2,1)S(1)}, u32[]{:S(2)}, u32[]{:S(2)}) collective-permute-start(bf16[8,2176]{1,0:T(8,128)(2,1)S(1)} %fusion.qa), channel_id=1, source_target_pairs={{16,12},{0,16},{20,8},{4,20},{24,4},{8,24},{28,0},{12,28},{17,13},... | collective-permute-start | bytes 104456 | tf_op jit(solution)/shard_map/ppermute | solution.py:331
  5.1 3.7 %resident.1 = (f32[144,128]{1,0:T(8,128)S(1)}, bf16[144,128]{1,0:T(8,128)(2,1)S(1)}, bf16[24,128,512]{2,1,0:T(8,128)(2,1)S(1)}, f32[24,128]{1,0:T(8,128)S(1)}) custom-call(bf16[8,2176]{1,0:T(8,128)(2,1)S(1)} %fusion.qa, s32[3,4,12]{2,1,0:T(4,128)} %bitcast.14, s32[4,6]{1,0:T(4,128)} %wanted_hbm.1, s32[8,8]{1,0:T(8,128)} %bitcast.13, s32[1,8]{1,0:T(1,128)} %lengths_hbm.1, ...), custom_call_target="tpu_custom_call" | custom-call | tf_op jit(solution)/shard_map/resident/pallas_call | solution.py:345
  8.9 0.3 %collective-permute-done.refs_0_ = bf16[8,2176]{1,0:T(8,128)(2,1)S(1)} collective-permute-done((bf16[8,2176]{1,0:T(8,128)(2,1)S(1)}, bf16[8,2176]{1,0:T(8,128)(2,1)S(1)}, u32[]{:S(2)}, u32[]{:S(2)}) %collective-permute-start) | collective-permute-done | bytes 34848 | tf_op jit(solution)/shard_map/ppermute | solution.py:331
  9.2 1.7 %owned.1 = (bf16[144,128]{1,0:T(8,128)(2,1)S(1)}, bf16[144,128]{1,0:T(8,128)(2,1)S(1)}, bf16[144,128]{1,0:T(8,128)(2,1)S(1)}) custom-call(bf16[24,128,512]{2,1,0:T(8,128)(2,1)S(1)} %get-tuple-element.22.chosen, f32[24,128]{1,0:T(8,128)S(1)} %get-tuple-element.23.entries, bf16[8,2176]{1,0:T(8,128)(2,1)S(1)} %collective-permute-done.refs_0_, ...), custom_call_target="tpu_custom_call" | custom-call | flops 40000000000 | bytes 8388608 | tf_op jit(solution)/shard_map/owned/pallas_call | solution.py:369
  10.9 1.9 %collective-permute-start.3 = (bf16[144,128]{1,0:T(8,128)(2,1)S(1)}, bf16[144,128]{1,0:T(8,128)(2,1)S(1)}, u32[]{:S(2)}, u32[]{:S(2)}) collective-permute-start(bf16[144,128]{1,0:T(8,128)(2,1)S(1)} %get-tuple-element.28), channel_id=1, source_target_pairs={{0,28},{16,0},{4,24},{20,4},{8,20},{24,8},{12,16},{28,12},{1,29},{... | collective-permute-start | bytes 110600 | tf_op jit(solution)/shard_map/ppermute | solution.py:331
  12.8 0.2 collective-permute-start.5
  13.0 0.3 %collective-permute-start.6 = (bf16[144,128]{1,0:T(8,128)(2,1)S(1)}, bf16[144,128]{1,0:T(8,128)(2,1)S(1)}, u32[]{:S(2)}, u32[]{:S(2)}) collective-permute-start(bf16[144,128]{1,0:T(8,128)(2,1)S(1)} %get-tuple-element.31), channel_id=1, source_target_pairs={{0,16},{16,0},{4,20},{20,4},{8,24},{24,8},{12,28},{28,12},{1,17},{... | collective-permute-start | bytes 110600 | tf_op jit(solution)/shard_map/ppermute | solution.py:331
  13.3 0.4 %fresh.1.refs_1_ = f32[144,128]{1,0:T(8,128)S(1)} custom-call(bf16[8,2176]{1,0:T(8,128)(2,1)S(1)} %fusion.qa, bf16[8,512]{1,0:T(8,128)(2,1)S(1)} %bitcast.9), custom_call_target="tpu_custom_call" | custom-call | flops 1000000000 | bytes 1048576 | tf_op jit(solution)/shard_map/fresh/pallas_call | solution.py:379
  13.7 0.8 %collective-permute-done.3.refs_2_ = bf16[144,128]{1,0:T(8,128)(2,1)S(1)} collective-permute-done((bf16[144,128]{1,0:T(8,128)(2,1)S(1)}, bf16[144,128]{1,0:T(8,128)(2,1)S(1)}, u32[]{:S(2)}, u32[]{:S(2)}) %collective-permute-start.3) | collective-permute-done | bytes 36896 | tf_op jit(solution)/shard_map/ppermute | solution.py:331
  14.5 0.3 %collective-permute-done.4.refs_3_ = bf16[144,128]{1,0:T(8,128)(2,1)S(1)} collective-permute-done((bf16[144,128]{1,0:T(8,128)(2,1)S(1)}, bf16[144,128]{1,0:T(8,128)(2,1)S(1)}, u32[]{:S(2)}, u32[]{:S(2)}) %collective-permute-start.4) | collective-permute-done | bytes 36896 | tf_op jit(solution)/shard_map/ppermute | solution.py:331
  14.8 0.3 %collective-permute-done.5.refs_4_ = bf16[144,128]{1,0:T(8,128)(2,1)S(1)} collective-permute-done((bf16[144,128]{1,0:T(8,128)(2,1)S(1)}, bf16[144,128]{1,0:T(8,128)(2,1)S(1)}, u32[]{:S(2)}, u32[]{:S(2)}) %collective-permute-start.5) | collective-permute-done | bytes 36896 | tf_op jit(solution)/shard_map/ppermute | solution.py:331
  15.2 0.3 %merge.1.attended = bf16[8,2048]{1,0:T(8,128)(2,1)S(1)} custom-call(f32[144,128]{1,0:T(8,128)S(1)} %get-tuple-element.20.refs_0_, f32[144,128]{1,0:T(8,128)S(1)} %fresh.1.refs_1_, bf16[144,128]{1,0:T(8,128)(2,1)S(1)} %collective-permute-done.3.refs_2_, bf16[144,128]{1,0:T(8,128)(2,1)S(1)} %collective-permute-done.4.refs_3_, ...), custom_call_target="tpu_custom_call" | custom-call | tf_op jit(solution)/shard_map/merge/pallas_call | solution.py:389
  15.5 2.2 %collective-permute-start.7 = (bf16[8,2048]{1,0:T(8,128)(2,1)S(1)}, bf16[8,2048]{1,0:T(8,128)(2,1)S(1)}, u32[]{:S(2)}, u32[]{:S(2)}) collective-permute-start(bf16[8,2048]{1,0:T(8,128)(2,1)S(1)} %merge.1.attended), channel_id=1, source_target_pairs={{0,16},{16,0},{1,17},{17,1},{2,18},{18,2},{3,19},{19,3},{4,20},{20... | collective-permute-start | bytes 98312 | tf_op jit(solution)/shard_map/ppermute | solution.py:397
  17.7 0.9 %collective-permute-done.7.partner = bf16[8,2048]{1,0:T(8,128)(2,1)S(1)} collective-permute-done((bf16[8,2048]{1,0:T(8,128)(2,1)S(1)}, bf16[8,2048]{1,0:T(8,128)(2,1)S(1)}, u32[]{:S(2)}, u32[]{:S(2)}) %collective-permute-start.7) | collective-permute-done | bytes 32800 | tf_op jit(solution)/shard_map/ppermute | solution.py:397
  18.6 1.7 %project.1 = (bf16[8,1024]{1,0:T(8,128)(2,1)S(1)}, bf16[8,1024]{1,0:T(8,128)(2,1)S(1)}, bf16[8,1024]{1,0:T(8,128)(2,1)S(1)}) custom-call(bf16[8,2048]{1,0:T(8,128)(2,1)S(1)} %merge.1.attended, bf16[8,2048]{1,0:T(8,128)(2,1)S(1)} %collective-permute-done.7.partner, bf16[2048,4096]{1,0:T(8,128)(2,1)S(1)} %bitcast.8), custom_call_target="tpu_custom_call" | custom-call | flops 201326592 | bytes 12582912 | tf_op jit(solution)/shard_map/project/pallas_call | solution.py:401
  20.3 1.5 %collective-permute-start.8 = (bf16[8,1024]{1,0:T(8,128)(2,1)S(1)}, bf16[8,1024]{1,0:T(8,128)(2,1)S(1)}, u32[]{:S(2)}, u32[]{:S(2)}) collective-permute-start(bf16[8,1024]{1,0:T(8,128)(2,1)S(1)} %get-tuple-element.32), channel_id=1, source_target_pairs={{0,1},{1,2},{2,3},{3,0},{4,5},{5,6},{6,7},{7,4},{8,9},{9,10},{10,1... | collective-permute-start | bytes 49160 | tf_op jit(solution)/shard_map/ppermute | solution.py:415
  21.8 1.5 %collective-permute-start.9 = (bf16[8,1024]{1,0:T(8,128)(2,1)S(1)}, bf16[8,1024]{1,0:T(8,128)(2,1)S(1)}, u32[]{:S(2)}, u32[]{:S(2)}) collective-permute-start(bf16[8,1024]{1,0:T(8,128)(2,1)S(1)} %get-tuple-element.33), channel_id=1, source_target_pairs={{0,2},{1,3},{2,0},{3,1},{4,6},{5,7},{6,4},{7,5},{8,10},{9,11},{10,... | collective-permute-start | bytes 49160 | tf_op jit(solution)/shard_map/ppermute | solution.py:415
  23.3 1.4 %collective-permute-start.10 = (bf16[8,1024]{1,0:T(8,128)(2,1)S(1)}, bf16[8,1024]{1,0:T(8,128)(2,1)S(1)}, u32[]{:S(2)}, u32[]{:S(2)}) collective-permute-start(bf16[8,1024]{1,0:T(8,128)(2,1)S(1)} %get-tuple-element.34), channel_id=1, source_target_pairs={{0,3},{1,0},{2,1},{3,2},{4,7},{5,4},{6,5},{7,6},{8,11},{9,8},{10,9... | collective-permute-start | bytes 49160 | tf_op jit(solution)/shard_map/ppermute | solution.py:415
  24.8 0.6 %project_own.1 = f32[8,1024]{1,0:T(8,128)S(1)} custom-call(bf16[8,2048]{1,0:T(8,128)(2,1)S(1)} %merge.1.attended, bf16[8,2048]{1,0:T(8,128)(2,1)S(1)} %collective-permute-done.7.partner, bf16[2048,4096]{1,0:T(8,128)(2,1)S(1)} %bitcast.8), custom_call_target="tpu_custom_call" | custom-call | flops 67108864 | bytes 4194304 | tf_op jit(solution)/shard_map/project_own/pallas_call | solution.py:401
  25.5 1.5 %collective-permute-done.10 = bf16[8,1024]{1,0:T(8,128)(2,1)S(1)} collective-permute-done((bf16[8,1024]{1,0:T(8,128)(2,1)S(1)}, bf16[8,1024]{1,0:T(8,128)(2,1)S(1)}, u32[]{:S(2)}, u32[]{:S(2)}) %collective-permute-start.10) | collective-permute-done | bytes 16416 | tf_op jit(solution)/shard_map/ppermute | solution.py:415
  27.1 0.6 %fusion.1 = bf16[1,8,1024]{2,1,0:T(8,128)(2,1)} fusion(bf16[8,1024]{1,0:T(8,128)(2,1)S(1)} %collective-permute-done.10, bf16[8,1024]{1,0:T(8,128)(2,1)S(1)} %collective-permute-done.9, f32[8,1024]{1,0:T(8,128)S(1)} %project_own.1, bf16[8,1024]{1,0:T(8,128)(2,1)S(1)} %collective-permute-done.8), kind=kLoop, calls=%fused_computation.3 | loop fusion | flops 57344 | bytes 98304 | tf_op jit(solution)/shard_map/broadcast_in_dim | solution.py:418
  (17 shorter events, 0.2 us)
Async XLA Ops:
  0.9 8.0 %collective-permute-start.2 = (bf16[8,2176]{1,0:T(8,128)(2,1)S(1)}, bf16[8,2176]{1,0:T(8,128)(2,1)S(1)}, u32[]{:S(2)}, u32[]{:S(2)}) collective-permute-start(bf16[8,2176]{1,0:T(8,128)(2,1)S(1)} %fusion.qa), channel_id=1, source_target_pairs={{16,4},{0,16},{20,0},{4,20},{24,12},{8,24},{28,8},{12,28},{17,5},{... | collective-permute-start | bytes 104456 | tf_op jit(solution)/shard_map/ppermute | solution.py:331
  1.3 7.5 %collective-permute-start.1 = (bf16[8,2176]{1,0:T(8,128)(2,1)S(1)}, bf16[8,2176]{1,0:T(8,128)(2,1)S(1)}, u32[]{:S(2)}, u32[]{:S(2)}) collective-permute-start(bf16[8,2176]{1,0:T(8,128)(2,1)S(1)} %fusion.qa), channel_id=1, source_target_pairs={{16,8},{0,16},{20,12},{4,20},{24,0},{8,24},{28,4},{12,28},{17,9},{... | collective-permute-start | bytes 104456 | tf_op jit(solution)/shard_map/ppermute | solution.py:331
  4.0 5.2 %collective-permute-start = (bf16[8,2176]{1,0:T(8,128)(2,1)S(1)}, bf16[8,2176]{1,0:T(8,128)(2,1)S(1)}, u32[]{:S(2)}, u32[]{:S(2)}) collective-permute-start(bf16[8,2176]{1,0:T(8,128)(2,1)S(1)} %fusion.qa), channel_id=1, source_target_pairs={{16,12},{0,16},{20,8},{4,20},{24,4},{8,24},{28,0},{12,28},{17,13},... | collective-permute-start | bytes 104456 | tf_op jit(solution)/shard_map/ppermute | solution.py:331
  9.2 9.4 %slice-start = ((s8[16777216]{0:T(1024)(128)(4,1)}), s8[4194304]{0:T(1024)(128)(4,1)S(1)}, s32[]{:S(2)}) async-start(s8[16777216]{0:T(1024)(128)(4,1)} %bitcast.7), calls=%async_computation | async-start | bytes 8388608
  9.2 4.2 %copy-start = (bf16[1,8,512]{2,1,0:T(8,128)(2,1)S(1)}, bf16[1,8,512]{2,1,0:T(8,128)(2,1)}, u32[]{:S(2)}) copy-start(bf16[1,8,512]{2,1,0:T(8,128)(2,1)} %param.14) | copy-start | bytes 24580
  9.2 9.4 %slice-start.1 = ((s8[16777216]{0:T(1024)(128)(4,1)}), s8[4194304]{0:T(1024)(128)(4,1)S(1)}, s32[]{:S(2)}) async-start(s8[16777216]{0:T(1024)(128)(4,1)} %bitcast.7), calls=%async_computation.1 | async-start | bytes 8388608
  9.2 9.4 %slice-start.2 = ((s8[16777216]{0:T(1024)(128)(4,1)}), s8[4194304]{0:T(1024)(128)(4,1)S(1)}, s32[]{:S(2)}) async-start(s8[16777216]{0:T(1024)(128)(4,1)} %bitcast.7), calls=%async_computation.2 | async-start | bytes 8388608
  9.2 9.3 %slice-start.3 = ((s8[16777216]{0:T(1024)(128)(4,1)}), s8[4194304]{0:T(1024)(128)(4,1)S(1)}, s32[]{:S(2)}) async-start(s8[16777216]{0:T(1024)(128)(4,1)} %bitcast.7), calls=%async_computation.3 | async-start | bytes 8388608
  10.9 3.6 %collective-permute-start.3 = (bf16[144,128]{1,0:T(8,128)(2,1)S(1)}, bf16[144,128]{1,0:T(8,128)(2,1)S(1)}, u32[]{:S(2)}, u32[]{:S(2)}) collective-permute-start(bf16[144,128]{1,0:T(8,128)(2,1)S(1)} %get-tuple-element.28), channel_id=1, source_target_pairs={{0,28},{16,0},{4,24},{20,4},{8,20},{24,8},{12,16},{28,12},{1,29},{... | collective-permute-start | bytes 110600 | tf_op jit(solution)/shard_map/ppermute | solution.py:331
  12.8 2.0 %collective-permute-start.4 = (bf16[144,128]{1,0:T(8,128)(2,1)S(1)}, bf16[144,128]{1,0:T(8,128)(2,1)S(1)}, u32[]{:S(2)}, u32[]{:S(2)}) collective-permute-start(bf16[144,128]{1,0:T(8,128)(2,1)S(1)} %get-tuple-element.29), channel_id=1, source_target_pairs={{0,24},{16,0},{4,28},{20,4},{8,16},{24,8},{12,20},{28,12},{1,25},{... | collective-permute-start | bytes 110600 | tf_op jit(solution)/shard_map/ppermute | solution.py:331
  12.8 2.3 %collective-permute-start.5 = (bf16[144,128]{1,0:T(8,128)(2,1)S(1)}, bf16[144,128]{1,0:T(8,128)(2,1)S(1)}, u32[]{:S(2)}, u32[]{:S(2)}) collective-permute-start(bf16[144,128]{1,0:T(8,128)(2,1)S(1)} %get-tuple-element.30), channel_id=1, source_target_pairs={{0,20},{16,0},{4,16},{20,4},{8,28},{24,8},{12,24},{28,12},{1,21},{... | collective-permute-start | bytes 110600 | tf_op jit(solution)/shard_map/ppermute | solution.py:331
  13.0 2.2 %collective-permute-start.6 = (bf16[144,128]{1,0:T(8,128)(2,1)S(1)}, bf16[144,128]{1,0:T(8,128)(2,1)S(1)}, u32[]{:S(2)}, u32[]{:S(2)}) collective-permute-start(bf16[144,128]{1,0:T(8,128)(2,1)S(1)} %get-tuple-element.31), channel_id=1, source_target_pairs={{0,16},{16,0},{4,20},{20,4},{8,24},{24,8},{12,28},{28,12},{1,17},{... | collective-permute-start | bytes 110600 | tf_op jit(solution)/shard_map/ppermute | solution.py:331
  15.5 3.0 %collective-permute-start.7 = (bf16[8,2048]{1,0:T(8,128)(2,1)S(1)}, bf16[8,2048]{1,0:T(8,128)(2,1)S(1)}, u32[]{:S(2)}, u32[]{:S(2)}) collective-permute-start(bf16[8,2048]{1,0:T(8,128)(2,1)S(1)} %merge.1.attended), channel_id=1, source_target_pairs={{0,16},{16,0},{1,17},{17,1},{2,18},{18,2},{3,19},{19,3},{4,20},{20... | collective-permute-start | bytes 98312 | tf_op jit(solution)/shard_map/ppermute | solution.py:397
  20.3 5.1 %collective-permute-start.8 = (bf16[8,1024]{1,0:T(8,128)(2,1)S(1)}, bf16[8,1024]{1,0:T(8,128)(2,1)S(1)}, u32[]{:S(2)}, u32[]{:S(2)}) collective-permute-start(bf16[8,1024]{1,0:T(8,128)(2,1)S(1)} %get-tuple-element.32), channel_id=1, source_target_pairs={{0,1},{1,2},{2,3},{3,0},{4,5},{5,6},{6,7},{7,4},{8,9},{9,10},{10,1... | collective-permute-start | bytes 49160 | tf_op jit(solution)/shard_map/ppermute | solution.py:415
  21.8 3.7 %collective-permute-start.9 = (bf16[8,1024]{1,0:T(8,128)(2,1)S(1)}, bf16[8,1024]{1,0:T(8,128)(2,1)S(1)}, u32[]{:S(2)}, u32[]{:S(2)}) collective-permute-start(bf16[8,1024]{1,0:T(8,128)(2,1)S(1)} %get-tuple-element.33), channel_id=1, source_target_pairs={{0,2},{1,3},{2,0},{3,1},{4,6},{5,7},{6,4},{7,5},{8,10},{9,11},{10,... | collective-permute-start | bytes 49160 | tf_op jit(solution)/shard_map/ppermute | solution.py:415
  23.3 3.7 %collective-permute-start.10 = (bf16[8,1024]{1,0:T(8,128)(2,1)S(1)}, bf16[8,1024]{1,0:T(8,128)(2,1)S(1)}, u32[]{:S(2)}, u32[]{:S(2)}) collective-permute-start(bf16[8,1024]{1,0:T(8,128)(2,1)S(1)} %get-tuple-element.34), channel_id=1, source_target_pairs={{0,3},{1,0},{2,1},{3,2},{4,7},{5,4},{6,5},{7,6},{8,11},{9,8},{10,9... | collective-permute-start | bytes 49160 | tf_op jit(solution)/shard_map/ppermute | solution.py:415

commit v2 on v1

--- a/solution.py
+++ b/solution.py
@@ -20,7 +20,7 @@
 SCALE = 1.0 / math.sqrt(HD)
 PARTS = CAP + CAPP
 CHUNK = 8
-STATIC = (2, 3, 4, 5)
+STATIC = (1, 2, 3)
 STATS = 16
 MIB = 2**20
 
@@ -97,7 +97,7 @@
     write_part(out, acc, top, total, held, per_held)
 
 
-def resident_part(qa, lists_ready, send, tables, lengths, maxp, group, kv, pages, flags, listed, sems, out, held, per_held):
+def resident_part(span, qa, lists_ready, send, tables, lengths, maxp, group, kv, pages, flags, listed, sems, out, held, per_held):
     rows = qa.shape[0]
     slots = kv.shape[0]
     q = query_block(qa, held, per_held)
@@ -116,7 +116,7 @@
         return pltpu.make_async_copy(kv.at[slot], pages.at[i], sems.at[i])
 
     listed_count = jnp.int32(0)
-    for r in range(rows):
+    for r in range(*span):
         length = lengths[0, r]
         for e in range(maxp):
             slot = tables[r, e]
@@ -220,7 +220,7 @@
     return ready
 
 
-def first_kernel(held, per_held, groups, maxp, qa, send_hbm, wanted_hbm, tables_hbm, lengths_hbm, kv, *refs):
+def first_kernel(span, held, per_held, groups, maxp, qa, send_hbm, wanted_hbm, tables_hbm, lengths_hbm, kv, *refs):
     out, sent, chosen, entries, pages, send, wanted, tables, lengths = refs[:9]
     flags, listed, page_list, slot_list, list_sems, chosen_sems, sems = refs[9:]
     group = lax.axis_index("group")
@@ -251,11 +251,11 @@
     @pl.when(jnp.logical_not(prefill))
     def _():
         resident_part(
-            qa, lists_ready, send, tables, lengths, maxp, group, kv, pages, flags, listed, sems, out, held, per_held
+            span, qa, lists_ready, send, tables, lengths, maxp, group, kv, pages, flags, listed, sems, out, held, per_held
         )
 
 
-def fresh_kernel(held, per_held, qa, new_kv, out):
+def fresh_part(qa, new_kv, out, held, per_held):
     rows = qa.shape[0]
     q = query_block(qa, held, per_held)
     count = q.shape[0]
@@ -268,6 +268,19 @@
     p = jnp.exp(s - top)
     acc = dot(p.astype(jnp.bfloat16), lanes_of(fresh, 1, held), 0, 0)
     write_part(out, acc, top, jnp.sum(p, 0, keepdims=True), held, per_held)
+
+
+def third_kernel(span, held, per_held, maxp, qa, new_kv, send_hbm, tables_hbm, lengths_hbm, kv, *refs):
+    out, fresh, pages, send, tables, lengths, flags, listed, list_sems, sems = refs
+    group = lax.axis_index("group")
+
+    @pl.when(lax.axis_index("role") == 1)
+    def _():
+        lists_ready = copy_lists(((send_hbm, send), (tables_hbm, tables), (lengths_hbm, lengths)), list_sems)
+        fresh_part(qa, new_kv, fresh, held, per_held)
+        resident_part(
+            span, qa, lists_ready, send, tables, lengths, maxp, group, kv, pages, flags, listed, sems, out, held, per_held
+        )
 
 
 def second_kernel(held, per_held, maxp, count, chosen, entries, *refs):
@@ -337,13 +350,14 @@
     hbm = pl.BlockSpec(memory_space=pltpu.HBM)
     page_shape = stored.shape[1:]
     chosen_count = groups * PARTS
-    read_count = -(-rows * maxp // CHUNK) * CHUNK
+    cut = (rows + 1) // 2
+    read_count = -(-cut * maxp // CHUNK) * CHUNK
     lists = [send, wanted, tables[0], lengths]
     pinned = [pltpu.with_memory_space_constraint(x, pltpu.HBM) for x in lists + [stored]]
     smem = [pltpu.SMEM(x.shape, jnp.int32) for x in lists]
     reading = [pltpu.SMEM((slots + 1,), jnp.int32), pltpu.SMEM((2, read_count), jnp.int32)]
     mine, mine_sent, chosen, entries = pl.pallas_call(
-        functools.partial(first_kernel, held, per_held, groups, maxp),
+        functools.partial(first_kernel, (0, cut), held, per_held, groups, maxp),
         out_shape=[
             part_shape,
             sent_shape,
@@ -372,20 +386,28 @@
         in_specs=[vmem] * (2 + count),
         out_specs=[vmem] * count,
         compiler_params=pltpu.CompilerParams(vmem_limit_bytes=16 * MIB),
-        cost_estimate=pl.CostEstimate(flops=4 * 10**10, bytes_accessed=8 * MIB, transcendentals=10**6),
+        cost_estimate=pl.CostEstimate(flops=4 * 10**9, bytes_accessed=8 * MIB, transcendentals=10**6),
         name="owned",
     )(chosen, entries, *reversed(asked))
     qa, mine_sent, theirs = lax.optimization_barrier((qa, mine_sent, theirs))
-    fresh = pl.pallas_call(
-        functools.partial(fresh_kernel, held, per_held),
-        out_shape=part_shape,
-        in_specs=[vmem] * 2,
-        out_specs=vmem,
-        compiler_params=pltpu.CompilerParams(vmem_limit_bytes=8 * MIB),
-        cost_estimate=pl.CostEstimate(flops=10**9, bytes_accessed=MIB, transcendentals=10**4),
-        name="fresh",
-    )(qa, new_kv[0])
-    parts = [mine, fresh] + [paired(part, k, True) for k, part in enumerate([mine_sent, *theirs])][::-1]
+    rest, fresh = pl.pallas_call(
+        functools.partial(third_kernel, (cut, rows), held, per_held, maxp),
+        out_shape=[part_shape] * 2,
+        in_specs=[vmem] * 2 + [hbm] * 4,
+        out_specs=[vmem] * 2,
+        scratch_shapes=[
+            pltpu.VMEM((read_count,) + page_shape, jnp.bfloat16),
+            smem[0],
+            smem[2],
+            smem[3],
+            *reading,
+            pltpu.SemaphoreType.DMA((3,)),
+            pltpu.SemaphoreType.DMA((read_count,)),
+        ],
+        compiler_params=pltpu.CompilerParams(vmem_limit_bytes=20 * MIB),
+        name="resident_rest",
+    )(qa, new_kv[0], pinned[0], *pinned[2:])
+    parts = [mine, rest, fresh] + [paired(part, k, True) for k, part in enumerate([mine_sent, *theirs])][::-1]
     attended = pl.pallas_call(
         functools.partial(merge_kernel, heads, rows),
         out_shape=jax.ShapeDtypeStruct((rows, wide), jnp.bfloat16),

time: 28.1 us -> 28.7 us (1.021)
  Pallas kernels: 8.48 us -> 9.06 us
  starting transfers between devices: 13.3 us -> 13.8 us
    pallas_call x2, Pallas kernels: 4.09 us -> 4.65 us  [the longest x1 4.34 us: per_device(): pl.pallas_call(functools.partial(first_kernel, (0, cut), held, per_held,...]
  transfers between devices with their start and end apart: 11 -> 11, of which waited for: 7 -> 6; matrix products, arithmetic and copies ran while one was open for 0% -> 0% of each run, Pallas kernels for 17% -> 19%
where the time goes in v2:
time: 28.7 us; the launch traced here: 28.5 us
  starting transfers between devices  13.8 us (48%)
  Pallas kernels  9.06 us (32%)
  waiting for transfers between devices  4.02 us (14%)
  other arithmetic  1.5 us (5%)
    ppermute x7, starting transfers between devices, paired(): return lax.ppermute(value, ('role', 'group'), pairs)  6.89 us
    ppermute x3, starting transfers between devices, per_device(): lax.ppermute(part, 'tp', [(i, (i + d) % tps) for i in range(tps)])  4.46 us
    pallas_call x1, Pallas kernels, per_device(): pl.pallas_call(functools.partial(first_kernel, (0, cut), held, per_held,...  4.34 us
    ppermute x1, starting transfers between devices, per_device(): partner = lax.ppermute(attended, 'role', [(0, 1), (1, 0)])  2.42 us
    pallas_call x2, Pallas kernels, project(): pl.pallas_call(functools.partial(project_kernel, steps), out_shape=[jax.S...  2.38 us
    pallas_call x1, Pallas kernels, per_device(): pl.pallas_call(functools.partial(second_kernel, held, per_held, maxp, cou...  1.67 us
    ppermute x3, waiting for transfers between devices, per_device(): lax.ppermute(part, 'tp', [(i, (i + d) % tps) for i in range(tps)])  1.66 us
    ppermute x7, waiting for transfers between devices, paired(): return lax.ppermute(value, ('role', 'group'), pairs)  1.5 us
  transfers between devices with their start and end apart: 11, of which 6 were waited for; matrix products, arithmetic and copies ran while one was open for 0% of the time, Pallas kernels for 19%

profile of v2, /device:TPU:0, one launch (start us, length us, event | category | flops | bytes accessed | tf_op | source)
XLA Modules:
  0.0 28.5 jit_solution(15823218914149998548)
XLA Ops:
  0.0 0.9 %fusion.qa = bf16[8,2176]{1,0:T(8,128)(2,1)S(1)} fusion(s32[1,8]{1,0:T(1,128)} %lengths_hbm.3, s32[8,8]{1,0:T(8,128)} %bitcast.12, bf16[8,2048]{1,0:T(8,128)(2,1)} %bitcast.15), kind=kLoop, calls=%fused_computation.1 | loop fusion | flops 156672 | bytes 67872 | tf_op jit(solution)/shard_map/add | solution.py:340
  0.9 0.5 %collective-permute-start.2 = (bf16[8,2176]{1,0:T(8,128)(2,1)S(1)}, bf16[8,2176]{1,0:T(8,128)(2,1)S(1)}, u32[]{:S(2)}, u32[]{:S(2)}) collective-permute-start(bf16[8,2176]{1,0:T(8,128)(2,1)S(1)} %fusion.qa), channel_id=1, source_target_pairs={{16,4},{0,16},{20,0},{4,20},{24,12},{8,24},{28,8},{12,28},{17,5},{... | collective-permute-start | bytes 104456 | tf_op jit(solution)/shard_map/ppermute | solution.py:344
  1.3 2.7 %collective-permute-start.1 = (bf16[8,2176]{1,0:T(8,128)(2,1)S(1)}, bf16[8,2176]{1,0:T(8,128)(2,1)S(1)}, u32[]{:S(2)}, u32[]{:S(2)}) collective-permute-start(bf16[8,2176]{1,0:T(8,128)(2,1)S(1)} %fusion.qa), channel_id=1, source_target_pairs={{16,8},{0,16},{20,12},{4,20},{24,0},{8,24},{28,4},{12,28},{17,9},{... | collective-permute-start | bytes 104456 | tf_op jit(solution)/shard_map/ppermute | solution.py:344
  4.0 1.1 %collective-permute-start = (bf16[8,2176]{1,0:T(8,128)(2,1)S(1)}, bf16[8,2176]{1,0:T(8,128)(2,1)S(1)}, u32[]{:S(2)}, u32[]{:S(2)}) collective-permute-start(bf16[8,2176]{1,0:T(8,128)(2,1)S(1)} %fusion.qa), channel_id=1, source_target_pairs={{16,12},{0,16},{20,8},{4,20},{24,4},{8,24},{28,0},{12,28},{17,13},... | collective-permute-start | bytes 104456 | tf_op jit(solution)/shard_map/ppermute | solution.py:344
  5.1 4.3 %resident.1 = (f32[144,128]{1,0:T(8,128)S(1)}, bf16[144,128]{1,0:T(8,128)(2,1)S(1)}, bf16[24,128,512]{2,1,0:T(8,128)(2,1)S(1)}, f32[24,128]{1,0:T(8,128)S(1)}) custom-call(bf16[8,2176]{1,0:T(8,128)(2,1)S(1)} %fusion.qa, s32[3,4,12]{2,1,0:T(4,128)} %bitcast.16, s32[4,6]{1,0:T(4,128)} %wanted_hbm.1, s32[8,8]{1,0:T(8,128)} %bitcast.13, s32[1,8]{1,0:T(1,128)} %lengths_hbm.3, ...), custom_call_target="tpu_custom_call" | custom-call | tf_op jit(solution)/shard_map/resident/pallas_call | solution.py:359
  9.5 0.0 slice-start.2
  9.5 1.7 %owned.1 = (bf16[144,128]{1,0:T(8,128)(2,1)S(1)}, bf16[144,128]{1,0:T(8,128)(2,1)S(1)}, bf16[144,128]{1,0:T(8,128)(2,1)S(1)}) custom-call(bf16[24,128,512]{2,1,0:T(8,128)(2,1)S(1)} %get-tuple-element.24.chosen, f32[24,128]{1,0:T(8,128)S(1)} %get-tuple-element.25.entries, bf16[8,2176]{1,0:T(8,128)(2,1)S(1)} %collective-permute-done.refs_0_, ...), custom_call_target="tpu_custom_call" | custom-call | flops 4000000000 | bytes 8388608 | tf_op jit(solution)/shard_map/owned/pallas_call | solution.py:383
  11.2 2.2 %collective-permute-start.3 = (bf16[144,128]{1,0:T(8,128)(2,1)S(1)}, bf16[144,128]{1,0:T(8,128)(2,1)S(1)}, u32[]{:S(2)}, u32[]{:S(2)}) collective-permute-start(bf16[144,128]{1,0:T(8,128)(2,1)S(1)} %get-tuple-element.32), channel_id=1, source_target_pairs={{0,28},{16,0},{4,24},{20,4},{8,20},{24,8},{12,16},{28,12},{1,29},{... | collective-permute-start | bytes 110600 | tf_op jit(solution)/shard_map/ppermute | solution.py:344
  13.4 0.5 %collective-permute-start.6 = (bf16[144,128]{1,0:T(8,128)(2,1)S(1)}, bf16[144,128]{1,0:T(8,128)(2,1)S(1)}, u32[]{:S(2)}, u32[]{:S(2)}) collective-permute-start(bf16[144,128]{1,0:T(8,128)(2,1)S(1)} %get-tuple-element.35), channel_id=1, source_target_pairs={{0,16},{16,0},{4,20},{20,4},{8,24},{24,8},{12,28},{28,12},{1,17},{... | collective-permute-start | bytes 110600 | tf_op jit(solution)/shard_map/ppermute | solution.py:344
  13.9 0.3 %resident_rest.1 = (f32[144,128]{1,0:T(8,128)S(1)}, f32[144,128]{1,0:T(8,128)S(1)}) custom-call(bf16[8,2176]{1,0:T(8,128)(2,1)S(1)} %fusion.qa, bf16[8,512]{1,0:T(8,128)(2,1)S(1)} %bitcast.9, s32[3,4,12]{2,1,0:T(4,128)} %bitcast.17, s32[8,8]{1,0:T(8,128)} %bitcast.14, s32[1,8]{1,0:T(1,128)} %lengths_hbm.3, bf16[64,128,512]{2,1,0:T(8,128)(2,1)} %bitcast.11), custom_call_target="tpu_custom_call" | custom-call | tf_op jit(solution)/shard_map/resident_rest/pallas_call | solution.py:393
  14.2 0.8 %collective-permute-done.3.refs_3_ = bf16[144,128]{1,0:T(8,128)(2,1)S(1)} collective-permute-done((bf16[144,128]{1,0:T(8,128)(2,1)S(1)}, bf16[144,128]{1,0:T(8,128)(2,1)S(1)}, u32[]{:S(2)}, u32[]{:S(2)}) %collective-permute-start.3) | collective-permute-done | bytes 36896 | tf_op jit(solution)/shard_map/ppermute | solution.py:344
  15.0 0.3 %collective-permute-done.4.refs_4_ = bf16[144,128]{1,0:T(8,128)(2,1)S(1)} collective-permute-done((bf16[144,128]{1,0:T(8,128)(2,1)S(1)}, bf16[144,128]{1,0:T(8,128)(2,1)S(1)}, u32[]{:S(2)}, u32[]{:S(2)}) %collective-permute-start.4) | collective-permute-done | bytes 36896 | tf_op jit(solution)/shard_map/ppermute | solution.py:344
  15.3 0.3 %collective-permute-done.5.refs_5_ = bf16[144,128]{1,0:T(8,128)(2,1)S(1)} collective-permute-done((bf16[144,128]{1,0:T(8,128)(2,1)S(1)}, bf16[144,128]{1,0:T(8,128)(2,1)S(1)}, u32[]{:S(2)}, u32[]{:S(2)}) %collective-permute-start.5) | collective-permute-done | bytes 36896 | tf_op jit(solution)/shard_map/ppermute | solution.py:344
  15.7 0.4 %merge.1.attended = bf16[8,2048]{1,0:T(8,128)(2,1)S(1)} custom-call(f32[144,128]{1,0:T(8,128)S(1)} %get-tuple-element.22.refs_0_, f32[144,128]{1,0:T(8,128)S(1)} %get-tuple-element.30.refs_1_, f32[144,128]{1,0:T(8,128)S(1)} %get-tuple-element.31.refs_2_, bf16[144,128]{1,0:T(8,128)(2,1)S(1)} %collective-permute-done.3.refs_3_, ...), custom_call_target="tpu_custom_call" | custom-call | tf_op jit(solution)/shard_map/merge/pallas_call | solution.py:411
  16.0 2.4 %collective-permute-start.7 = (bf16[8,2048]{1,0:T(8,128)(2,1)S(1)}, bf16[8,2048]{1,0:T(8,128)(2,1)S(1)}, u32[]{:S(2)}, u32[]{:S(2)}) collective-permute-start(bf16[8,2048]{1,0:T(8,128)(2,1)S(1)} %merge.1.attended), channel_id=1, source_target_pairs={{0,16},{16,0},{1,17},{17,1},{2,18},{18,2},{3,19},{19,3},{4,20},{20... | collective-permute-start | bytes 98312 | tf_op jit(solution)/shard_map/ppermute | solution.py:419
  18.5 0.9 %collective-permute-done.7.partner = bf16[8,2048]{1,0:T(8,128)(2,1)S(1)} collective-permute-done((bf16[8,2048]{1,0:T(8,128)(2,1)S(1)}, bf16[8,2048]{1,0:T(8,128)(2,1)S(1)}, u32[]{:S(2)}, u32[]{:S(2)}) %collective-permute-start.7) | collective-permute-done | bytes 32800 | tf_op jit(solution)/shard_map/ppermute | solution.py:419
  19.4 1.7 %project.1 = (bf16[8,1024]{1,0:T(8,128)(2,1)S(1)}, bf16[8,1024]{1,0:T(8,128)(2,1)S(1)}, bf16[8,1024]{1,0:T(8,128)(2,1)S(1)}) custom-call(bf16[8,2048]{1,0:T(8,128)(2,1)S(1)} %merge.1.attended, bf16[8,2048]{1,0:T(8,128)(2,1)S(1)} %collective-permute-done.7.partner, bf16[2048,4096]{1,0:T(8,128)(2,1)S(1)} %bitcast.8), custom_call_target="tpu_custom_call" | custom-call | flops 201326592 | bytes 12582912 | tf_op jit(solution)/shard_map/project/pallas_call | solution.py:423
  21.1 1.5 %collective-permute-start.8 = (bf16[8,1024]{1,0:T(8,128)(2,1)S(1)}, bf16[8,1024]{1,0:T(8,128)(2,1)S(1)}, u32[]{:S(2)}, u32[]{:S(2)}) collective-permute-start(bf16[8,1024]{1,0:T(8,128)(2,1)S(1)} %get-tuple-element.36), channel_id=1, source_target_pairs={{0,1},{1,2},{2,3},{3,0},{4,5},{5,6},{6,7},{7,4},{8,9},{9,10},{10,1... | collective-permute-start | bytes 49160 | tf_op jit(solution)/shard_map/ppermute | solution.py:437
  22.6 1.5 %collective-permute-start.9 = (bf16[8,1024]{1,0:T(8,128)(2,1)S(1)}, bf16[8,1024]{1,0:T(8,128)(2,1)S(1)}, u32[]{:S(2)}, u32[]{:S(2)}) collective-permute-start(bf16[8,1024]{1,0:T(8,128)(2,1)S(1)} %get-tuple-element.37), channel_id=1, source_target_pairs={{0,2},{1,3},{2,0},{3,1},{4,6},{5,7},{6,4},{7,5},{8,10},{9,11},{10,... | collective-permute-start | bytes 49160 | tf_op jit(solution)/shard_map/ppermute | solution.py:437
  24.1 1.4 %collective-permute-start.10 = (bf16[8,1024]{1,0:T(8,128)(2,1)S(1)}, bf16[8,1024]{1,0:T(8,128)(2,1)S(1)}, u32[]{:S(2)}, u32[]{:S(2)}) collective-permute-start(bf16[8,1024]{1,0:T(8,128)(2,1)S(1)} %get-tuple-element.38), channel_id=1, source_target_pairs={{0,3},{1,0},{2,1},{3,2},{4,7},{5,4},{6,5},{7,6},{8,11},{9,8},{10,9... | collective-permute-start | bytes 49160 | tf_op jit(solution)/shard_map/ppermute | solution.py:437
  25.6 0.6 %project_own.1 = f32[8,1024]{1,0:T(8,128)S(1)} custom-call(bf16[8,2048]{1,0:T(8,128)(2,1)S(1)} %merge.1.attended, bf16[8,2048]{1,0:T(8,128)(2,1)S(1)} %collective-permute-done.7.partner, bf16[2048,4096]{1,0:T(8,128)(2,1)S(1)} %bitcast.8), custom_call_target="tpu_custom_call" | custom-call | flops 67108864 | bytes 4194304 | tf_op jit(solution)/shard_map/project_own/pallas_call | solution.py:423
  26.2 0.1 collective-permute-done.9
  26.3 1.5 %collective-permute-done.10 = bf16[8,1024]{1,0:T(8,128)(2,1)S(1)} collective-permute-done((bf16[8,1024]{1,0:T(8,128)(2,1)S(1)}, bf16[8,1024]{1,0:T(8,128)(2,1)S(1)}, u32[]{:S(2)}, u32[]{:S(2)}) %collective-permute-start.10) | collective-permute-done | bytes 16416 | tf_op jit(solution)/shard_map/ppermute | solution.py:437
  27.9 0.6 %fusion.1 = bf16[1,8,1024]{2,1,0:T(8,128)(2,1)} fusion(bf16[8,1024]{1,0:T(8,128)(2,1)S(1)} %collective-permute-done.10, bf16[8,1024]{1,0:T(8,128)(2,1)S(1)} %collective-permute-done.9, f32[8,1024]{1,0:T(8,128)S(1)} %project_own.1, bf16[8,1024]{1,0:T(8,128)(2,1)S(1)} %collective-permute-done.8), kind=kLoop, calls=%fused_computation.3 | loop fusion | flops 57344 | bytes 98304 | tf_op jit(solution)/shard_map/broadcast_in_dim | solution.py:440
  (17 shorter events, 0.0 us)
Async XLA Ops:
  0.9 8.6 %collective-permute-start.2 = (bf16[8,2176]{1,0:T(8,128)(2,1)S(1)}, bf16[8,2176]{1,0:T(8,128)(2,1)S(1)}, u32[]{:S(2)}, u32[]{:S(2)}) collective-permute-start(bf16[8,2176]{1,0:T(8,128)(2,1)S(1)} %fusion.qa), channel_id=1, source_target_pairs={{16,4},{0,16},{20,0},{4,20},{24,12},{8,24},{28,8},{12,28},{17,5},{... | collective-permute-start | bytes 104456 | tf_op jit(solution)/shard_map/ppermute | solution.py:344
  1.3 8.1 %collective-permute-start.1 = (bf16[8,2176]{1,0:T(8,128)(2,1)S(1)}, bf16[8,2176]{1,0:T(8,128)(2,1)S(1)}, u32[]{:S(2)}, u32[]{:S(2)}) collective-permute-start(bf16[8,2176]{1,0:T(8,128)(2,1)S(1)} %fusion.qa), channel_id=1, source_target_pairs={{16,8},{0,16},{20,12},{4,20},{24,0},{8,24},{28,4},{12,28},{17,9},{... | collective-permute-start | bytes 104456 | tf_op jit(solution)/shard_map/ppermute | solution.py:344
  4.0 5.5 %collective-permute-start = (bf16[8,2176]{1,0:T(8,128)(2,1)S(1)}, bf16[8,2176]{1,0:T(8,128)(2,1)S(1)}, u32[]{:S(2)}, u32[]{:S(2)}) collective-permute-start(bf16[8,2176]{1,0:T(8,128)(2,1)S(1)} %fusion.qa), channel_id=1, source_target_pairs={{16,12},{0,16},{20,8},{4,20},{24,4},{8,24},{28,0},{12,28},{17,13},... | collective-permute-start | bytes 104456 | tf_op jit(solution)/shard_map/ppermute | solution.py:344
  5.1 14.2 %slice-start = ((s8[16777216]{0:T(1024)(128)(4,1)}), s8[4194304]{0:T(1024)(128)(4,1)S(1)}, s32[]{:S(2)}) async-start(s8[16777216]{0:T(1024)(128)(4,1)} %bitcast.7), calls=%async_computation | async-start | bytes 8388608
  5.1 14.2 %slice-start.1 = ((s8[16777216]{0:T(1024)(128)(4,1)}), s8[4194304]{0:T(1024)(128)(4,1)S(1)}, s32[]{:S(2)}) async-start(s8[16777216]{0:T(1024)(128)(4,1)} %bitcast.7), calls=%async_computation.1 | async-start | bytes 8388608
  9.4 4.4 %copy-start = (bf16[1,8,512]{2,1,0:T(8,128)(2,1)S(1)}, bf16[1,8,512]{2,1,0:T(8,128)(2,1)}, u32[]{:S(2)}) copy-start(bf16[1,8,512]{2,1,0:T(8,128)(2,1)} %param.14) | copy-start | bytes 24580
  9.5 9.8 %slice-start.2 = ((s8[16777216]{0:T(1024)(128)(4,1)}), s8[4194304]{0:T(1024)(128)(4,1)S(1)}, s32[]{:S(2)}) async-start(s8[16777216]{0:T(1024)(128)(4,1)} %bitcast.7), calls=%async_computation.2 | async-start | bytes 8388608
  11.2 3.8 %collective-permute-start.3 = (bf16[144,128]{1,0:T(8,128)(2,1)S(1)}, bf16[144,128]{1,0:T(8,128)(2,1)S(1)}, u32[]{:S(2)}, u32[]{:S(2)}) collective-permute-start(bf16[144,128]{1,0:T(8,128)(2,1)S(1)} %get-tuple-element.32), channel_id=1, source_target_pairs={{0,28},{16,0},{4,24},{20,4},{8,20},{24,8},{12,16},{28,12},{1,29},{... | collective-permute-start | bytes 110600 | tf_op jit(solution)/shard_map/ppermute | solution.py:344
  13.4 2.0 %collective-permute-start.4 = (bf16[144,128]{1,0:T(8,128)(2,1)S(1)}, bf16[144,128]{1,0:T(8,128)(2,1)S(1)}, u32[]{:S(2)}, u32[]{:S(2)}) collective-permute-start(bf16[144,128]{1,0:T(8,128)(2,1)S(1)} %get-tuple-element.33), channel_id=1, source_target_pairs={{0,24},{16,0},{4,28},{20,4},{8,16},{24,8},{12,20},{28,12},{1,25},{... | collective-permute-start | bytes 110600 | tf_op jit(solution)/shard_map/ppermute | solution.py:344
  13.4 2.3 %collective-permute-start.5 = (bf16[144,128]{1,0:T(8,128)(2,1)S(1)}, bf16[144,128]{1,0:T(8,128)(2,1)S(1)}, u32[]{:S(2)}, u32[]{:S(2)}) collective-permute-start(bf16[144,128]{1,0:T(8,128)(2,1)S(1)} %get-tuple-element.34), channel_id=1, source_target_pairs={{0,20},{16,0},{4,16},{20,4},{8,28},{24,8},{12,24},{28,12},{1,21},{... | collective-permute-start | bytes 110600 | tf_op jit(solution)/shard_map/ppermute | solution.py:344
  13.4 2.3 %collective-permute-start.6 = (bf16[144,128]{1,0:T(8,128)(2,1)S(1)}, bf16[144,128]{1,0:T(8,128)(2,1)S(1)}, u32[]{:S(2)}, u32[]{:S(2)}) collective-permute-start(bf16[144,128]{1,0:T(8,128)(2,1)S(1)} %get-tuple-element.35), channel_id=1, source_target_pairs={{0,16},{16,0},{4,20},{20,4},{8,24},{24,8},{12,28},{28,12},{1,17},{... | collective-permute-start | bytes 110600 | tf_op jit(solution)/shard_map/ppermute | solution.py:344
  13.9 5.5 %slice-start.3 = ((s8[16777216]{0:T(1024)(128)(4,1)}), s8[4194304]{0:T(1024)(128)(4,1)S(1)}, s32[]{:S(2)}) async-start(s8[16777216]{0:T(1024)(128)(4,1)} %bitcast.7), calls=%async_computation.3 | async-start | bytes 8388608
  16.0 3.3 %collective-permute-start.7 = (bf16[8,2048]{1,0:T(8,128)(2,1)S(1)}, bf16[8,2048]{1,0:T(8,128)(2,1)S(1)}, u32[]{:S(2)}, u32[]{:S(2)}) collective-permute-start(bf16[8,2048]{1,0:T(8,128)(2,1)S(1)} %merge.1.attended), channel_id=1, source_target_pairs={{0,16},{16,0},{1,17},{17,1},{2,18},{18,2},{3,19},{19,3},{4,20},{20... | collective-permute-start | bytes 98312 | tf_op jit(solution)/shard_map/ppermute | solution.py:419
  21.1 5.1 %collective-permute-start.8 = (bf16[8,1024]{1,0:T(8,128)(2,1)S(1)}, bf16[8,1024]{1,0:T(8,128)(2,1)S(1)}, u32[]{:S(2)}, u32[]{:S(2)}) collective-permute-start(bf16[8,1024]{1,0:T(8,128)(2,1)S(1)} %get-tuple-element.36), channel_id=1, source_target_pairs={{0,1},{1,2},{2,3},{3,0},{4,5},{5,6},{6,7},{7,4},{8,9},{9,10},{10,1... | collective-permute-start | bytes 49160 | tf_op jit(solution)/shard_map/ppermute | solution.py:437
  22.6 3.7 %collective-permute-start.9 = (bf16[8,1024]{1,0:T(8,128)(2,1)S(1)}, bf16[8,1024]{1,0:T(8,128)(2,1)S(1)}, u32[]{:S(2)}, u32[]{:S(2)}) collective-permute-start(bf16[8,1024]{1,0:T(8,128)(2,1)S(1)} %get-tuple-element.37), channel_id=1, source_target_pairs={{0,2},{1,3},{2,0},{3,1},{4,6},{5,7},{6,4},{7,5},{8,10},{9,11},{10,... | collective-permute-start | bytes 49160 | tf_op jit(solution)/shard_map/ppermute | solution.py:437
  24.1 3.7 %collective-permute-start.10 = (bf16[8,1024]{1,0:T(8,128)(2,1)S(1)}, bf16[8,1024]{1,0:T(8,128)(2,1)S(1)}, u32[]{:S(2)}, u32[]{:S(2)}) collective-permute-start(bf16[8,1024]{1,0:T(8,128)(2,1)S(1)} %get-tuple-element.38), channel_id=1, source_target_pairs={{0,3},{1,0},{2,1},{3,2},{4,7},{5,4},{6,5},{7,6},{8,11},{9,8},{10,9... | collective-permute-start | bytes 49160 | tf_op jit(solution)/shard_map/ppermute | solution.py:437

commit v3 on v1

--- a/solution.py
+++ b/solution.py
@@ -97,16 +97,11 @@
     write_part(out, acc, top, total, held, per_held)
 
 
-def resident_part(qa, lists_ready, send, tables, lengths, maxp, group, kv, pages, flags, listed, sems, out, held, per_held):
-    rows = qa.shape[0]
+def fetch_pages(rows, lists_ready, send, tables, lengths, maxp, group, kv, pages, valid, flags, sems):
     slots = kv.shape[0]
-    q = query_block(qa, held, per_held)
-    count = q.shape[0]
-    lane_row = lax.rem(lax.broadcasted_iota(jnp.int32, (1, count), 1), rows)
-    token = lax.broadcasted_iota(jnp.int32, (PAGE, count), 0)
+    lane_row = lax.rem(lax.broadcasted_iota(jnp.int32, (1, LANES), 1), rows)
     for i in range(slots):
         flags[i] = 0
-
     lists_ready()
     for o in range(send.shape[1]):
         for i in range(send.shape[2]):
@@ -115,7 +110,7 @@
     def page_copy(slot, i):
         return pltpu.make_async_copy(kv.at[slot], pages.at[i], sems.at[i])
 
-    listed_count = jnp.int32(0)
+    found = jnp.int32(0)
     for r in range(rows):
         length = lengths[0, r]
         for e in range(maxp):
@@ -123,31 +118,43 @@
             tokens = jnp.minimum(length - e * PAGE, PAGE)
             here = jnp.logical_and(slot < slots, flags[jnp.minimum(slot, slots - 1)] == 0)
             needed = jnp.logical_and(tokens > 0, here)
-            listed[0, listed_count] = r
-            listed[1, listed_count] = tokens
 
             @pl.when(needed)
-            def _(slot=slot, at=listed_count):
+            def _(slot=slot, r=r, at=found, tokens=tokens):
                 page_copy(slot, at).start()
-
-            listed_count = listed_count + needed.astype(jnp.int32)
-    chunks = jnp.maximum((listed_count + CHUNK - 1) // CHUNK, STATIC[0])
+                valid[pl.ds(at, 1), :] = jnp.where(lane_row == r, tokens.astype(jnp.float32), 0.0)
+
+            found = found + needed.astype(jnp.int32)
+    chunks = jnp.maximum((found + CHUNK - 1) // CHUNK, STATIC[0])
 
     def fill(i, _):
-        listed[0, i] = 0
-        listed[1, i] = 0
         page_copy(0, i).start()
+        valid[pl.ds(i, 1), :] = jnp.zeros((1, LANES), jnp.float32)
         return 0
 
-    lax.fori_loop(listed_count, chunks * CHUNK, fill, 0)
+    lax.fori_loop(found, chunks * CHUNK, fill, 0)
+    last = valid.shape[0] - 1
+    valid[last : last + 1, :] = jnp.full((1, LANES), chunks.astype(jnp.float32), jnp.float32)
+
+    def wait(c, _):
+        for i in range(CHUNK):
+            page_copy(0, c * CHUNK + i).wait()
+        return 0
+
+    lax.fori_loop(0, chunks, wait, 0)
+
+
+def resident_part(qa, pages, valid, out, held, per_held):
+    q = query_block(qa, held, per_held)
+    count = q.shape[0]
+    token = lax.broadcasted_iota(jnp.int32, (PAGE, count), 0).astype(jnp.float32)
+    floor = jnp.full((1, count), FLOOR, jnp.float32)
+    last = valid.shape[0] - 1
+    chunks = jnp.max(valid[last : last + 1, :]).astype(jnp.int32)
 
     def score(c):
         first = c * CHUNK
-        masks = []
-        for i in range(CHUNK):
-            masks.append(token < jnp.where(lane_row == listed[0, first + i], listed[1, first + i], 0))
-        for i in range(CHUNK):
-            page_copy(0, first + i).wait()
+        masks = [token < valid[pl.ds(first + i, 1), :][:, :count] for i in range(CHUNK)]
         keys = jnp.concatenate([lanes_of(pages.at[first + i], 0, held) for i in range(CHUNK)], 0)
         return jnp.where(jnp.concatenate(masks, 0), dot(keys, q, 1, 1) * SCALE, NEG)
 
@@ -155,8 +162,6 @@
         p = jnp.exp(s - top)
         values = jnp.concatenate([lanes_of(pages.at[c * CHUNK + i], 1, held) for i in range(CHUNK)], 0)
         return jnp.sum(p, 0, keepdims=True), dot(p.astype(jnp.bfloat16), values, 0, 0)
-
-    floor = jnp.full((1, count), FLOOR, jnp.float32)
 
     def straight(number):
         scores = [score(c) for c in range(number)]
@@ -221,8 +226,8 @@
 
 
 def first_kernel(held, per_held, groups, maxp, qa, send_hbm, wanted_hbm, tables_hbm, lengths_hbm, kv, *refs):
-    out, sent, chosen, entries, pages, send, wanted, tables, lengths = refs[:9]
-    flags, listed, page_list, slot_list, list_sems, chosen_sems, sems = refs[9:]
+    sent, chosen, entries, valid, send, wanted, tables, lengths = refs[:8]
+    flags, page_list, slot_list, list_sems, sems = refs[8:]
     group = lax.axis_index("group")
     prefill = lax.axis_index("role") == 0
     lists = ((send_hbm, send), (wanted_hbm, wanted), (tables_hbm, tables), (lengths_hbm, lengths))
@@ -237,7 +242,7 @@
             list_pages(send, wanted, group, target, kv.shape[0], page_list, slot_list, k * PARTS)
             for c in range(PARTS):
                 at = k * PARTS + c
-                copy = pltpu.make_async_copy(kv.at[page_list[at]], chosen.at[at], chosen_sems.at[at])
+                copy = pltpu.make_async_copy(kv.at[page_list[at]], chosen.at[at], sems.at[at])
                 copy.start()
                 copies.append(copy)
                 entry = slot_list[at].astype(jnp.float32)
@@ -250,12 +255,10 @@
 
     @pl.when(jnp.logical_not(prefill))
     def _():
-        resident_part(
-            qa, lists_ready, send, tables, lengths, maxp, group, kv, pages, flags, listed, sems, out, held, per_held
-        )
-
-
-def fresh_kernel(held, per_held, qa, new_kv, out):
+        fetch_pages(qa.shape[0], lists_ready, send, tables, lengths, maxp, group, kv, chosen, valid, flags, sems)
+
+
+def fresh_part(qa, new_kv, out, held, per_held):
     rows = qa.shape[0]
     q = query_block(qa, held, per_held)
     count = q.shape[0]
@@ -268,6 +271,13 @@
     p = jnp.exp(s - top)
     acc = dot(p.astype(jnp.bfloat16), lanes_of(fresh, 1, held), 0, 0)
     write_part(out, acc, top, jnp.sum(p, 0, keepdims=True), held, per_held)
+
+
+def third_kernel(held, per_held, qa, new_kv, pages, valid, out, fresh):
+    @pl.when(lax.axis_index("role") == 1)
+    def _():
+        fresh_part(qa, new_kv, fresh, held, per_held)
+        resident_part(qa, pages, valid, out, held, per_held)
 
 
 def second_kernel(held, per_held, maxp, count, chosen, entries, *refs):
@@ -338,29 +348,26 @@
     page_shape = stored.shape[1:]
     chosen_count = groups * PARTS
     read_count = -(-rows * maxp // CHUNK) * CHUNK
+    page_count = max(read_count, chosen_count)
     lists = [send, wanted, tables[0], lengths]
     pinned = [pltpu.with_memory_space_constraint(x, pltpu.HBM) for x in lists + [stored]]
-    smem = [pltpu.SMEM(x.shape, jnp.int32) for x in lists]
-    reading = [pltpu.SMEM((slots + 1,), jnp.int32), pltpu.SMEM((2, read_count), jnp.int32)]
-    mine, mine_sent, chosen, entries = pl.pallas_call(
+    mine_sent, chosen, entries, valid = pl.pallas_call(
         functools.partial(first_kernel, held, per_held, groups, maxp),
         out_shape=[
-            part_shape,
             sent_shape,
-            jax.ShapeDtypeStruct((chosen_count,) + page_shape, jnp.bfloat16),
+            jax.ShapeDtypeStruct((page_count,) + page_shape, jnp.bfloat16),
             jax.ShapeDtypeStruct((chosen_count, LANES), jnp.float32),
+            jax.ShapeDtypeStruct((read_count + 8, LANES), jnp.float32),
         ],
         in_specs=[vmem] + [hbm] * 5,
         out_specs=[vmem] * 4,
         scratch_shapes=[
-            pltpu.VMEM((read_count,) + page_shape, jnp.bfloat16),
-            *smem,
-            *reading,
+            *[pltpu.SMEM(x.shape, jnp.int32) for x in lists],
+            pltpu.SMEM((slots + 1,), jnp.int32),
             pltpu.SMEM((chosen_count + 1,), jnp.int32),
             pltpu.SMEM((chosen_count + 1,), jnp.int32),
             pltpu.SemaphoreType.DMA((len(lists),)),
-            pltpu.SemaphoreType.DMA((chosen_count,)),
-            pltpu.SemaphoreType.DMA((read_count,)),
+            pltpu.SemaphoreType.DMA((page_count,)),
         ],
         compiler_params=pltpu.CompilerParams(vmem_limit_bytes=20 * MIB),
         name="resident",
@@ -376,15 +383,14 @@
         name="owned",
     )(chosen, entries, *reversed(asked))
     qa, mine_sent, theirs = lax.optimization_barrier((qa, mine_sent, theirs))
-    fresh = pl.pallas_call(
-        functools.partial(fresh_kernel, held, per_held),
-        out_shape=part_shape,
-        in_specs=[vmem] * 2,
-        out_specs=vmem,
-        compiler_params=pltpu.CompilerParams(vmem_limit_bytes=8 * MIB),
-        cost_estimate=pl.CostEstimate(flops=10**9, bytes_accessed=MIB, transcendentals=10**4),
-        name="fresh",
-    )(qa, new_kv[0])
+    mine, fresh = pl.pallas_call(
+        functools.partial(third_kernel, held, per_held),
+        out_shape=[part_shape] * 2,
+        in_specs=[vmem] * 4,
+        out_specs=[vmem] * 2,
+        compiler_params=pltpu.CompilerParams(vmem_limit_bytes=16 * MIB),
+        name="attend",
+    )(qa, new_kv[0], chosen, valid)
     parts = [mine, fresh] + [paired(part, k, True) for k, part in enumerate([mine_sent, *theirs])][::-1]
     attended = pl.pallas_call(
         functools.partial(merge_kernel, heads, rows),

time: 28.1 us -> 27.2 us (0.968)
  Pallas kernels: 8.48 us -> 7.91 us
  starting transfers between devices: 13.3 us -> 12.9 us
    ppermute x7, starting transfers between devices: 6.66 us -> 5.92 us  [paired(): return lax.ppermute(value, ('role', 'group'), pairs)]
    pallas_call x1, Pallas kernels: 0.36 us -> 0.01 us  [per_device(): pl.pallas_call(functools.partial(third_kernel, held, per_held), out_shape...]
    ppermute x1, starting transfers between devices: 2.17 us -> 2.52 us  [per_device(): partner = lax.ppermute(attended, 'role', [(0, 1), (1, 0)])]
  transfers between devices with their start and end apart: 11 -> 11, of which waited for: 7 -> 7; matrix products, arithmetic and copies ran while one was open for 0% -> 0% of each run, Pallas kernels for 17% -> 15%
where the time goes in v3:
time: 27.2 us; the launch traced here: 26.9 us
  starting transfers between devices  12.9 us (47%)
  Pallas kernels  7.91 us (29%)
  waiting for transfers between devices  4.54 us (17%)
  other arithmetic  1.5 us (6%)
    ppermute x7, starting transfers between devices, paired(): return lax.ppermute(value, ('role', 'group'), pairs)  5.92 us
    ppermute x3, starting transfers between devices, per_device(): lax.ppermute(part, 'tp', [(i, (i + d) % tps) for i in range(tps)])  4.46 us
    pallas_call x1, Pallas kernels, per_device(): pl.pallas_call(functools.partial(first_kernel, held, per_held, groups, ma...  3.52 us
    ppermute x1, starting transfers between devices, per_device(): partner = lax.ppermute(attended, 'role', [(0, 1), (1, 0)])  2.52 us
    pallas_call x2, Pallas kernels, project(): pl.pallas_call(functools.partial(project_kernel, steps), out_shape=[jax.S...  2.38 us
    ppermute x7, waiting for transfers between devices, paired(): return lax.ppermute(value, ('role', 'group'), pairs)  2.02 us
    pallas_call x1, Pallas kernels, per_device(): pl.pallas_call(functools.partial(second_kernel, held, per_held, maxp, cou...  1.67 us
    ppermute x3, waiting for transfers between devices, per_device(): lax.ppermute(part, 'tp', [(i, (i + d) % tps) for i in range(tps)])  1.66 us
  transfers between devices with their start and end apart: 11, of which 7 were waited for; matrix products, arithmetic and copies ran while one was open for 0% of the time, Pallas kernels for 15%

profile of v3, /device:TPU:0, one launch (start us, length us, event | category | flops | bytes accessed | tf_op | source)
XLA Modules:
  0.0 26.9 jit_solution(14131286159025183982)
XLA Ops:
  0.0 0.9 %fusion.qa = bf16[8,2176]{1,0:T(8,128)(2,1)S(1)} fusion(s32[1,8]{1,0:T(1,128)} %lengths_hbm.1, s32[8,8]{1,0:T(8,128)} %bitcast.12, bf16[8,2048]{1,0:T(8,128)(2,1)} %bitcast.11), kind=kLoop, calls=%fused_computation.1 | loop fusion | flops 156672 | bytes 67872 | tf_op jit(solution)/shard_map/add | solution.py:337
  0.9 0.5 %collective-permute-start.2 = (bf16[8,2176]{1,0:T(8,128)(2,1)S(1)}, bf16[8,2176]{1,0:T(8,128)(2,1)S(1)}, u32[]{:S(2)}, u32[]{:S(2)}) collective-permute-start(bf16[8,2176]{1,0:T(8,128)(2,1)S(1)} %fusion.qa), channel_id=1, source_target_pairs={{16,4},{0,16},{20,0},{4,20},{24,12},{8,24},{28,8},{12,28},{17,5},{... | collective-permute-start | bytes 104456 | tf_op jit(solution)/shard_map/ppermute | solution.py:341
  1.3 2.7 %collective-permute-start.1 = (bf16[8,2176]{1,0:T(8,128)(2,1)S(1)}, bf16[8,2176]{1,0:T(8,128)(2,1)S(1)}, u32[]{:S(2)}, u32[]{:S(2)}) collective-permute-start(bf16[8,2176]{1,0:T(8,128)(2,1)S(1)} %fusion.qa), channel_id=1, source_target_pairs={{16,8},{0,16},{20,12},{4,20},{24,0},{8,24},{28,4},{12,28},{17,9},{... | collective-permute-start | bytes 104456 | tf_op jit(solution)/shard_map/ppermute | solution.py:341
  4.0 1.1 %collective-permute-start = (bf16[8,2176]{1,0:T(8,128)(2,1)S(1)}, bf16[8,2176]{1,0:T(8,128)(2,1)S(1)}, u32[]{:S(2)}, u32[]{:S(2)}) collective-permute-start(bf16[8,2176]{1,0:T(8,128)(2,1)S(1)} %fusion.qa), channel_id=1, source_target_pairs={{16,12},{0,16},{20,8},{4,20},{24,4},{8,24},{28,0},{12,28},{17,13},... | collective-permute-start | bytes 104456 | tf_op jit(solution)/shard_map/ppermute | solution.py:341
  5.1 3.5 %resident.1 = (bf16[144,128]{1,0:T(8,128)(2,1)S(1)}, bf16[64,128,512]{2,1,0:T(8,128)(2,1)S(1)}, f32[24,128]{1,0:T(8,128)S(1)}, f32[72,128]{1,0:T(8,128)S(1)}) custom-call(bf16[8,2176]{1,0:T(8,128)(2,1)S(1)} %fusion.qa, s32[3,4,12]{2,1,0:T(4,128)} %bitcast.14, s32[4,6]{1,0:T(4,128)} %wanted_hbm.1, s32[8,8]{1,0:T(8,128)} %bitcast.13, s32[1,8]{1,0:T(1,128)} %lengths_hbm.1, ...), custom_call_target="tpu_custom_call" | custom-call | tf_op jit(solution)/shard_map/resident/pallas_call | solution.py:354
  8.6 0.5 %collective-permute-done.refs_0_ = bf16[8,2176]{1,0:T(8,128)(2,1)S(1)} collective-permute-done((bf16[8,2176]{1,0:T(8,128)(2,1)S(1)}, bf16[8,2176]{1,0:T(8,128)(2,1)S(1)}, u32[]{:S(2)}, u32[]{:S(2)}) %collective-permute-start) | collective-permute-done | bytes 34848 | tf_op jit(solution)/shard_map/ppermute | solution.py:341
  9.2 1.7 %owned.1 = (bf16[144,128]{1,0:T(8,128)(2,1)S(1)}, bf16[144,128]{1,0:T(8,128)(2,1)S(1)}, bf16[144,128]{1,0:T(8,128)(2,1)S(1)}) custom-call(bf16[64,128,512]{2,1,0:T(8,128)(2,1)S(1)} %get-tuple-element.23.chosen.pages, f32[24,128]{1,0:T(8,128)S(1)} %get-tuple-element.24.entries, bf16[8,2176]{1,0:T(8,128)(2,1)S(1)} %collective-permute-done.refs_0_, ...), custom_call_target="tpu_custom_call" | custom-call | flops 40000000000 | bytes 8388608 | tf_op jit(solution)/shard_map/owned/pallas_call | solution.py:376
  10.9 0.8 %collective-permute-start.3 = (bf16[144,128]{1,0:T(8,128)(2,1)S(1)}, bf16[144,128]{1,0:T(8,128)(2,1)S(1)}, u32[]{:S(2)}, u32[]{:S(2)}) collective-permute-start(bf16[144,128]{1,0:T(8,128)(2,1)S(1)} %get-tuple-element.32), channel_id=1, source_target_pairs={{0,28},{16,0},{4,24},{20,4},{8,20},{24,8},{12,16},{28,12},{1,29},{... | collective-permute-start | bytes 110600 | tf_op jit(solution)/shard_map/ppermute | solution.py:341
  11.7 0.4 %collective-permute-start.4 = (bf16[144,128]{1,0:T(8,128)(2,1)S(1)}, bf16[144,128]{1,0:T(8,128)(2,1)S(1)}, u32[]{:S(2)}, u32[]{:S(2)}) collective-permute-start(bf16[144,128]{1,0:T(8,128)(2,1)S(1)} %get-tuple-element.33), channel_id=1, source_target_pairs={{0,24},{16,0},{4,28},{20,4},{8,16},{24,8},{12,20},{28,12},{1,25},{... | collective-permute-start | bytes 110600 | tf_op jit(solution)/shard_map/ppermute | solution.py:341
  12.2 0.4 %collective-permute-start.6 = (bf16[144,128]{1,0:T(8,128)(2,1)S(1)}, bf16[144,128]{1,0:T(8,128)(2,1)S(1)}, u32[]{:S(2)}, u32[]{:S(2)}) collective-permute-start(bf16[144,128]{1,0:T(8,128)(2,1)S(1)} %get-tuple-element.35), channel_id=1, source_target_pairs={{0,16},{16,0},{4,20},{20,4},{8,24},{24,8},{12,28},{28,12},{1,17},{... | collective-permute-start | bytes 110600 | tf_op jit(solution)/shard_map/ppermute | solution.py:341
  12.6 0.8 %collective-permute-done.3.refs_2_ = bf16[144,128]{1,0:T(8,128)(2,1)S(1)} collective-permute-done((bf16[144,128]{1,0:T(8,128)(2,1)S(1)}, bf16[144,128]{1,0:T(8,128)(2,1)S(1)}, u32[]{:S(2)}, u32[]{:S(2)}) %collective-permute-start.3) | collective-permute-done | bytes 36896 | tf_op jit(solution)/shard_map/ppermute | solution.py:341
  13.4 0.4 %collective-permute-done.4.refs_3_ = bf16[144,128]{1,0:T(8,128)(2,1)S(1)} collective-permute-done((bf16[144,128]{1,0:T(8,128)(2,1)S(1)}, bf16[144,128]{1,0:T(8,128)(2,1)S(1)}, u32[]{:S(2)}, u32[]{:S(2)}) %collective-permute-start.4) | collective-permute-done | bytes 36896 | tf_op jit(solution)/shard_map/ppermute | solution.py:341
  13.7 0.3 %collective-permute-done.5.refs_4_ = bf16[144,128]{1,0:T(8,128)(2,1)S(1)} collective-permute-done((bf16[144,128]{1,0:T(8,128)(2,1)S(1)}, bf16[144,128]{1,0:T(8,128)(2,1)S(1)}, u32[]{:S(2)}, u32[]{:S(2)}) %collective-permute-start.5) | collective-permute-done | bytes 36896 | tf_op jit(solution)/shard_map/ppermute | solution.py:341
  14.1 0.3 %merge.1.attended = bf16[8,2048]{1,0:T(8,128)(2,1)S(1)} custom-call(f32[144,128]{1,0:T(8,128)S(1)} %get-tuple-element.30.refs_0_, f32[144,128]{1,0:T(8,128)S(1)} %get-tuple-element.31.refs_1_, bf16[144,128]{1,0:T(8,128)(2,1)S(1)} %collective-permute-done.3.refs_2_, bf16[144,128]{1,0:T(8,128)(2,1)S(1)} %collective-permute-done.4.refs_3_, ...), custom_call_target="tpu_custom_call" | custom-call | tf_op jit(solution)/shard_map/merge/pallas_call | solution.py:395
  14.4 2.5 %collective-permute-start.7 = (bf16[8,2048]{1,0:T(8,128)(2,1)S(1)}, bf16[8,2048]{1,0:T(8,128)(2,1)S(1)}, u32[]{:S(2)}, u32[]{:S(2)}) collective-permute-start(bf16[8,2048]{1,0:T(8,128)(2,1)S(1)} %merge.1.attended), channel_id=1, source_target_pairs={{0,16},{16,0},{1,17},{17,1},{2,18},{18,2},{3,19},{19,3},{4,20},{20... | collective-permute-start | bytes 98312 | tf_op jit(solution)/shard_map/ppermute | solution.py:403
  16.9 0.9 %collective-permute-done.7.partner = bf16[8,2048]{1,0:T(8,128)(2,1)S(1)} collective-permute-done((bf16[8,2048]{1,0:T(8,128)(2,1)S(1)}, bf16[8,2048]{1,0:T(8,128)(2,1)S(1)}, u32[]{:S(2)}, u32[]{:S(2)}) %collective-permute-start.7) | collective-permute-done | bytes 32800 | tf_op jit(solution)/shard_map/ppermute | solution.py:403
  17.8 1.7 %project.1 = (bf16[8,1024]{1,0:T(8,128)(2,1)S(1)}, bf16[8,1024]{1,0:T(8,128)(2,1)S(1)}, bf16[8,1024]{1,0:T(8,128)(2,1)S(1)}) custom-call(bf16[8,2048]{1,0:T(8,128)(2,1)S(1)} %merge.1.attended, bf16[8,2048]{1,0:T(8,128)(2,1)S(1)} %collective-permute-done.7.partner, bf16[2048,4096]{1,0:T(8,128)(2,1)S(1)} %bitcast.8), custom_call_target="tpu_custom_call" | custom-call | flops 201326592 | bytes 12582912 | tf_op jit(solution)/shard_map/project/pallas_call | solution.py:407
  19.6 1.5 %collective-permute-start.8 = (bf16[8,1024]{1,0:T(8,128)(2,1)S(1)}, bf16[8,1024]{1,0:T(8,128)(2,1)S(1)}, u32[]{:S(2)}, u32[]{:S(2)}) collective-permute-start(bf16[8,1024]{1,0:T(8,128)(2,1)S(1)} %get-tuple-element.36), channel_id=1, source_target_pairs={{0,1},{1,2},{2,3},{3,0},{4,5},{5,6},{6,7},{7,4},{8,9},{9,10},{10,1... | collective-permute-start | bytes 49160 | tf_op jit(solution)/shard_map/ppermute | solution.py:421
  21.1 1.5 %collective-permute-start.9 = (bf16[8,1024]{1,0:T(8,128)(2,1)S(1)}, bf16[8,1024]{1,0:T(8,128)(2,1)S(1)}, u32[]{:S(2)}, u32[]{:S(2)}) collective-permute-start(bf16[8,1024]{1,0:T(8,128)(2,1)S(1)} %get-tuple-element.37), channel_id=1, source_target_pairs={{0,2},{1,3},{2,0},{3,1},{4,6},{5,7},{6,4},{7,5},{8,10},{9,11},{10,... | collective-permute-start | bytes 49160 | tf_op jit(solution)/shard_map/ppermute | solution.py:421
  22.6 1.4 %collective-permute-start.10 = (bf16[8,1024]{1,0:T(8,128)(2,1)S(1)}, bf16[8,1024]{1,0:T(8,128)(2,1)S(1)}, u32[]{:S(2)}, u32[]{:S(2)}) collective-permute-start(bf16[8,1024]{1,0:T(8,128)(2,1)S(1)} %get-tuple-element.38), channel_id=1, source_target_pairs={{0,3},{1,0},{2,1},{3,2},{4,7},{5,4},{6,5},{7,6},{8,11},{9,8},{10,9... | collective-permute-start | bytes 49160 | tf_op jit(solution)/shard_map/ppermute | solution.py:421
  24.0 0.6 %project_own.1 = f32[8,1024]{1,0:T(8,128)S(1)} custom-call(bf16[8,2048]{1,0:T(8,128)(2,1)S(1)} %merge.1.attended, bf16[8,2048]{1,0:T(8,128)(2,1)S(1)} %collective-permute-done.7.partner, bf16[2048,4096]{1,0:T(8,128)(2,1)S(1)} %bitcast.8), custom_call_target="tpu_custom_call" | custom-call | flops 67108864 | bytes 4194304 | tf_op jit(solution)/shard_map/project_own/pallas_call | solution.py:407
  24.7 0.1 collective-permute-done.9
  24.8 1.5 %collective-permute-done.10 = bf16[8,1024]{1,0:T(8,128)(2,1)S(1)} collective-permute-done((bf16[8,1024]{1,0:T(8,128)(2,1)S(1)}, bf16[8,1024]{1,0:T(8,128)(2,1)S(1)}, u32[]{:S(2)}, u32[]{:S(2)}) %collective-permute-start.10) | collective-permute-done | bytes 16416 | tf_op jit(solution)/shard_map/ppermute | solution.py:421
  26.3 0.6 %fusion.1 = bf16[1,8,1024]{2,1,0:T(8,128)(2,1)} fusion(bf16[8,1024]{1,0:T(8,128)(2,1)S(1)} %collective-permute-done.10, bf16[8,1024]{1,0:T(8,128)(2,1)S(1)} %collective-permute-done.9, f32[8,1024]{1,0:T(8,128)S(1)} %project_own.1, bf16[8,1024]{1,0:T(8,128)(2,1)S(1)} %collective-permute-done.8), kind=kLoop, calls=%fused_computation.3 | loop fusion | flops 57344 | bytes 98304 | tf_op jit(solution)/shard_map/broadcast_in_dim | solution.py:424
  (17 shorter events, 0.1 us)
Async XLA Ops:
  0.9 7.7 %collective-permute-start.2 = (bf16[8,2176]{1,0:T(8,128)(2,1)S(1)}, bf16[8,2176]{1,0:T(8,128)(2,1)S(1)}, u32[]{:S(2)}, u32[]{:S(2)}) collective-permute-start(bf16[8,2176]{1,0:T(8,128)(2,1)S(1)} %fusion.qa), channel_id=1, source_target_pairs={{16,4},{0,16},{20,0},{4,20},{24,12},{8,24},{28,8},{12,28},{17,5},{... | collective-permute-start | bytes 104456 | tf_op jit(solution)/shard_map/ppermute | solution.py:341
  1.3 7.3 %collective-permute-start.1 = (bf16[8,2176]{1,0:T(8,128)(2,1)S(1)}, bf16[8,2176]{1,0:T(8,128)(2,1)S(1)}, u32[]{:S(2)}, u32[]{:S(2)}) collective-permute-start(bf16[8,2176]{1,0:T(8,128)(2,1)S(1)} %fusion.qa), channel_id=1, source_target_pairs={{16,8},{0,16},{20,12},{4,20},{24,0},{8,24},{28,4},{12,28},{17,9},{... | collective-permute-start | bytes 104456 | tf_op jit(solution)/shard_map/ppermute | solution.py:341
  4.0 5.2 %collective-permute-start = (bf16[8,2176]{1,0:T(8,128)(2,1)S(1)}, bf16[8,2176]{1,0:T(8,128)(2,1)S(1)}, u32[]{:S(2)}, u32[]{:S(2)}) collective-permute-start(bf16[8,2176]{1,0:T(8,128)(2,1)S(1)} %fusion.qa), channel_id=1, source_target_pairs={{16,12},{0,16},{20,8},{4,20},{24,4},{8,24},{28,0},{12,28},{17,13},... | collective-permute-start | bytes 104456 | tf_op jit(solution)/shard_map/ppermute | solution.py:341
  9.2 8.6 %slice-start = ((s8[16777216]{0:T(1024)(128)(4,1)}), s8[4194304]{0:T(1024)(128)(4,1)S(1)}, s32[]{:S(2)}) async-start(s8[16777216]{0:T(1024)(128)(4,1)} %bitcast.7), calls=%async_computation | async-start | bytes 8388608
  9.2 3.4 %copy-start = (bf16[1,8,512]{2,1,0:T(8,128)(2,1)S(1)}, bf16[1,8,512]{2,1,0:T(8,128)(2,1)}, u32[]{:S(2)}) copy-start(bf16[1,8,512]{2,1,0:T(8,128)(2,1)} %param.14) | copy-start | bytes 24580
  9.2 8.6 %slice-start.1 = ((s8[16777216]{0:T(1024)(128)(4,1)}), s8[4194304]{0:T(1024)(128)(4,1)S(1)}, s32[]{:S(2)}) async-start(s8[16777216]{0:T(1024)(128)(4,1)} %bitcast.7), calls=%async_computation.1 | async-start | bytes 8388608
  9.2 8.6 %slice-start.2 = ((s8[16777216]{0:T(1024)(128)(4,1)}), s8[4194304]{0:T(1024)(128)(4,1)S(1)}, s32[]{:S(2)}) async-start(s8[16777216]{0:T(1024)(128)(4,1)} %bitcast.7), calls=%async_computation.2 | async-start | bytes 8388608
  9.2 8.6 %slice-start.3 = ((s8[16777216]{0:T(1024)(128)(4,1)}), s8[4194304]{0:T(1024)(128)(4,1)S(1)}, s32[]{:S(2)}) async-start(s8[16777216]{0:T(1024)(128)(4,1)} %bitcast.7), calls=%async_computation.3 | async-start | bytes 8388608
  10.9 2.5 %collective-permute-start.3 = (bf16[144,128]{1,0:T(8,128)(2,1)S(1)}, bf16[144,128]{1,0:T(8,128)(2,1)S(1)}, u32[]{:S(2)}, u32[]{:S(2)}) collective-permute-start(bf16[144,128]{1,0:T(8,128)(2,1)S(1)} %get-tuple-element.32), channel_id=1, source_target_pairs={{0,28},{16,0},{4,24},{20,4},{8,20},{24,8},{12,16},{28,12},{1,29},{... | collective-permute-start | bytes 110600 | tf_op jit(solution)/shard_map/ppermute | solution.py:341
  11.7 2.0 %collective-permute-start.4 = (bf16[144,128]{1,0:T(8,128)(2,1)S(1)}, bf16[144,128]{1,0:T(8,128)(2,1)S(1)}, u32[]{:S(2)}, u32[]{:S(2)}) collective-permute-start(bf16[144,128]{1,0:T(8,128)(2,1)S(1)} %get-tuple-element.33), channel_id=1, source_target_pairs={{0,24},{16,0},{4,28},{20,4},{8,16},{24,8},{12,20},{28,12},{1,25},{... | collective-permute-start | bytes 110600 | tf_op jit(solution)/shard_map/ppermute | solution.py:341
  12.1 2.0 %collective-permute-start.5 = (bf16[144,128]{1,0:T(8,128)(2,1)S(1)}, bf16[144,128]{1,0:T(8,128)(2,1)S(1)}, u32[]{:S(2)}, u32[]{:S(2)}) collective-permute-start(bf16[144,128]{1,0:T(8,128)(2,1)S(1)} %get-tuple-element.34), channel_id=1, source_target_pairs={{0,20},{16,0},{4,16},{20,4},{8,28},{24,8},{12,24},{28,12},{1,21},{... | collective-permute-start | bytes 110600 | tf_op jit(solution)/shard_map/ppermute | solution.py:341
  12.2 1.9 %collective-permute-start.6 = (bf16[144,128]{1,0:T(8,128)(2,1)S(1)}, bf16[144,128]{1,0:T(8,128)(2,1)S(1)}, u32[]{:S(2)}, u32[]{:S(2)}) collective-permute-start(bf16[144,128]{1,0:T(8,128)(2,1)S(1)} %get-tuple-element.35), channel_id=1, source_target_pairs={{0,16},{16,0},{4,20},{20,4},{8,24},{24,8},{12,28},{28,12},{1,17},{... | collective-permute-start | bytes 110600 | tf_op jit(solution)/shard_map/ppermute | solution.py:341
  14.4 3.4 %collective-permute-start.7 = (bf16[8,2048]{1,0:T(8,128)(2,1)S(1)}, bf16[8,2048]{1,0:T(8,128)(2,1)S(1)}, u32[]{:S(2)}, u32[]{:S(2)}) collective-permute-start(bf16[8,2048]{1,0:T(8,128)(2,1)S(1)} %merge.1.attended), channel_id=1, source_target_pairs={{0,16},{16,0},{1,17},{17,1},{2,18},{18,2},{3,19},{19,3},{4,20},{20... | collective-permute-start | bytes 98312 | tf_op jit(solution)/shard_map/ppermute | solution.py:403
  19.6 5.1 %collective-permute-start.8 = (bf16[8,1024]{1,0:T(8,128)(2,1)S(1)}, bf16[8,1024]{1,0:T(8,128)(2,1)S(1)}, u32[]{:S(2)}, u32[]{:S(2)}) collective-permute-start(bf16[8,1024]{1,0:T(8,128)(2,1)S(1)} %get-tuple-element.36), channel_id=1, source_target_pairs={{0,1},{1,2},{2,3},{3,0},{4,5},{5,6},{6,7},{7,4},{8,9},{9,10},{10,1... | collective-permute-start | bytes 49160 | tf_op jit(solution)/shard_map/ppermute | solution.py:421
  21.1 3.7 %collective-permute-start.9 = (bf16[8,1024]{1,0:T(8,128)(2,1)S(1)}, bf16[8,1024]{1,0:T(8,128)(2,1)S(1)}, u32[]{:S(2)}, u32[]{:S(2)}) collective-permute-start(bf16[8,1024]{1,0:T(8,128)(2,1)S(1)} %get-tuple-element.37), channel_id=1, source_target_pairs={{0,2},{1,3},{2,0},{3,1},{4,6},{5,7},{6,4},{7,5},{8,10},{9,11},{10,... | collective-permute-start | bytes 49160 | tf_op jit(solution)/shard_map/ppermute | solution.py:421
  22.6 3.7 %collective-permute-start.10 = (bf16[8,1024]{1,0:T(8,128)(2,1)S(1)}, bf16[8,1024]{1,0:T(8,128)(2,1)S(1)}, u32[]{:S(2)}, u32[]{:S(2)}) collective-permute-start(bf16[8,1024]{1,0:T(8,128)(2,1)S(1)} %get-tuple-element.38), channel_id=1, source_target_pairs={{0,3},{1,0},{2,1},{3,2},{4,7},{5,4},{6,5},{7,6},{8,11},{9,8},{10,9... | collective-permute-start | bytes 49160 | tf_op jit(solution)/shard_map/ppermute | solution.py:421

commit v4 on v3

--- a/solution.py
+++ b/solution.py
@@ -280,13 +280,13 @@
         resident_part(qa, pages, valid, out, held, per_held)
 
 
-def second_kernel(held, per_held, maxp, count, chosen, entries, *refs):
-    qas, outs = refs[:count][::-1], refs[count:]
+def second_kernel(held, per_held, maxp, first, count, chosen, entries, *refs):
+    qas, outs = refs[:count][::-1], refs[len(refs) - count :]
 
     @pl.when(lax.axis_index("role") == 0)
     def _():
         for k in range(count):
-            at = (k + 1) * PARTS
+            at = (first + k) * PARTS
             owner_part(
                 qas[k], chosen.at[pl.ds(at, PARTS)], entries[at : at + PARTS, :], outs[k], held, per_held, maxp
             )
@@ -372,16 +372,17 @@
         compiler_params=pltpu.CompilerParams(vmem_limit_bytes=20 * MIB),
         name="resident",
     )(qa, *pinned)
-    count = groups - 1
-    theirs = pl.pallas_call(
-        functools.partial(second_kernel, held, per_held, maxp, count),
-        out_shape=[sent_shape] * count,
-        in_specs=[vmem] * (2 + count),
-        out_specs=[vmem] * count,
-        compiler_params=pltpu.CompilerParams(vmem_limit_bytes=16 * MIB),
-        cost_estimate=pl.CostEstimate(flops=4 * 10**10, bytes_accessed=8 * MIB, transcendentals=10**6),
-        name="owned",
-    )(chosen, entries, *reversed(asked))
+    theirs = []
+    for first, messages in ((1, asked[:-1]), (groups - 1, asked[-1:])):
+        theirs += pl.pallas_call(
+            functools.partial(second_kernel, held, per_held, maxp, first, len(messages)),
+            out_shape=[sent_shape] * len(messages),
+            in_specs=[vmem] * (2 + len(messages) + len(theirs)),
+            out_specs=[vmem] * len(messages),
+            compiler_params=pltpu.CompilerParams(vmem_limit_bytes=16 * MIB),
+            cost_estimate=pl.CostEstimate(flops=2 * 10**10, bytes_accessed=8 * MIB, transcendentals=10**6),
+            name="owned",
+        )(chosen, entries, *reversed(messages), *theirs)
     qa, mine_sent, theirs = lax.optimization_barrier((qa, mine_sent, theirs))
     mine, fresh = pl.pallas_call(
         functools.partial(third_kernel, held, per_held),

time: 27.2 us -> 26.9 us (0.989)
  waiting for transfers between devices: 4.54 us -> 3.99 us
    ppermute x7, waiting for transfers between devices: 2.02 us -> 1.48 us  [paired(): return lax.ppermute(value, ('role', 'group'), pairs)]
    ppermute x1, starting transfers between devices: 2.52 us -> 2.03 us  [per_device(): partner = lax.ppermute(attended, 'role', [(0, 1), (1, 0)])]
    ppermute x7, starting transfers between devices: 5.92 us -> 6.41 us  [paired(): return lax.ppermute(value, ('role', 'group'), pairs)]
    pallas_call x1 -> x2, Pallas kernels: 1.67 us -> 1.83 us  [per_device(): pl.pallas_call(functools.partial(second_kernel, held, per_held, maxp, fir...]
  transfers between devices with their start and end apart: 11 -> 11, of which waited for: 7 -> 6; matrix products, arithmetic and copies ran while one was open for 0% -> 0% of each run, Pallas kernels for 15% -> 20%
where the time goes in v4:
time: 26.9 us; the launch traced here: 26.6 us
  starting transfers between devices  12.9 us (48%)
  Pallas kernels  8.08 us (30%)
  waiting for transfers between devices  3.99 us (15%)
  other arithmetic  1.5 us (6%)
    ppermute x7, starting transfers between devices, paired(): return lax.ppermute(value, ('role', 'group'), pairs)  6.41 us
    ppermute x3, starting transfers between devices, per_device(): lax.ppermute(part, 'tp', [(i, (i + d) % tps) for i in range(tps)])  4.46 us
    pallas_call x1, Pallas kernels, per_device(): pl.pallas_call(functools.partial(first_kernel, held, per_held, groups, ma...  3.52 us
    pallas_call x2, Pallas kernels, project(): pl.pallas_call(functools.partial(project_kernel, steps), out_shape=[jax.S...  2.38 us
    ppermute x1, starting transfers between devices, per_device(): partner = lax.ppermute(attended, 'role', [(0, 1), (1, 0)])  2.03 us
    pallas_call x2, Pallas kernels, per_device(): pl.pallas_call(functools.partial(second_kernel, held, per_held, maxp, fir...  1.83 us
    ppermute x3, waiting for transfers between devices, per_device(): lax.ppermute(part, 'tp', [(i, (i + d) % tps) for i in range(tps)])  1.66 us
    ppermute x7, waiting for transfers between devices, paired(): return lax.ppermute(value, ('role', 'group'), pairs)  1.48 us
  transfers between devices with their start and end apart: 11, of which 6 were waited for; matrix products, arithmetic and copies ran while one was open for 0% of the time, Pallas kernels for 20%

profile of v4, /device:TPU:0, one launch (start us, length us, event | category | flops | bytes accessed | tf_op | source)
XLA Modules:
  0.0 26.6 jit_solution(3414899646835297048)
XLA Ops:
  0.0 0.9 %fusion.qa = bf16[8,2176]{1,0:T(8,128)(2,1)S(1)} fusion(s32[1,8]{1,0:T(1,128)} %lengths_hbm.1, s32[8,8]{1,0:T(8,128)} %bitcast.12, bf16[8,2048]{1,0:T(8,128)(2,1)} %bitcast.11), kind=kLoop, calls=%fused_computation.1 | loop fusion | flops 156672 | bytes 67872 | tf_op jit(solution)/shard_map/add | solution.py:337
  0.9 0.5 %collective-permute-start.1 = (bf16[8,2176]{1,0:T(8,128)(2,1)S(1)}, bf16[8,2176]{1,0:T(8,128)(2,1)S(1)}, u32[]{:S(2)}, u32[]{:S(2)}) collective-permute-start(bf16[8,2176]{1,0:T(8,128)(2,1)S(1)} %fusion.qa), channel_id=1, source_target_pairs={{16,4},{0,16},{20,0},{4,20},{24,12},{8,24},{28,8},{12,28},{17,5},{... | collective-permute-start | bytes 104456 | tf_op jit(solution)/shard_map/ppermute | solution.py:341
  1.3 2.7 %collective-permute-start = (bf16[8,2176]{1,0:T(8,128)(2,1)S(1)}, bf16[8,2176]{1,0:T(8,128)(2,1)S(1)}, u32[]{:S(2)}, u32[]{:S(2)}) collective-permute-start(bf16[8,2176]{1,0:T(8,128)(2,1)S(1)} %fusion.qa), channel_id=1, source_target_pairs={{16,8},{0,16},{20,12},{4,20},{24,0},{8,24},{28,4},{12,28},{17,9},{... | collective-permute-start | bytes 104456 | tf_op jit(solution)/shard_map/ppermute | solution.py:341
  4.0 1.1 %collective-permute-start.2 = (bf16[8,2176]{1,0:T(8,128)(2,1)S(1)}, bf16[8,2176]{1,0:T(8,128)(2,1)S(1)}, u32[]{:S(2)}, u32[]{:S(2)}) collective-permute-start(bf16[8,2176]{1,0:T(8,128)(2,1)S(1)} %fusion.qa), channel_id=1, source_target_pairs={{16,12},{0,16},{20,8},{4,20},{24,4},{8,24},{28,0},{12,28},{17,13},... | collective-permute-start | bytes 104456 | tf_op jit(solution)/shard_map/ppermute | solution.py:341
  5.1 3.5 %resident.1 = (bf16[144,128]{1,0:T(8,128)(2,1)S(1)}, bf16[64,128,512]{2,1,0:T(8,128)(2,1)S(1)}, f32[24,128]{1,0:T(8,128)S(1)}, f32[72,128]{1,0:T(8,128)S(1)}) custom-call(bf16[8,2176]{1,0:T(8,128)(2,1)S(1)} %fusion.qa, s32[3,4,12]{2,1,0:T(4,128)} %bitcast.14, s32[4,6]{1,0:T(4,128)} %wanted_hbm.1, s32[8,8]{1,0:T(8,128)} %bitcast.13, s32[1,8]{1,0:T(1,128)} %lengths_hbm.1, ...), custom_call_target="tpu_custom_call" | custom-call | tf_op jit(solution)/shard_map/resident/pallas_call | solution.py:354
  8.6 1.2 %owned.2 = (bf16[144,128]{1,0:T(8,128)(2,1)S(1)}, bf16[144,128]{1,0:T(8,128)(2,1)S(1)}) custom-call(bf16[64,128,512]{2,1,0:T(8,128)(2,1)S(1)} %get-tuple-element.22.chosen.pages, f32[24,128]{1,0:T(8,128)S(1)} %get-tuple-element.23.entries, bf16[8,2176]{1,0:T(8,128)(2,1)S(1)} %collective-permute-done.refs_0_, bf16[8,2176]{1,0:T(8,128)(2,1)S(1)} %collective-permute-done.1.refs_1_), custom_call_target="tpu_custom_call" | custom-call | flops 20000000000 | bytes 8388608 | tf_op jit(solution)/shard_map/owned/pallas_call | solution.py:377
  9.9 0.6 %owned.3 = bf16[144,128]{1,0:T(8,128)(2,1)S(1)} custom-call(bf16[64,128,512]{2,1,0:T(8,128)(2,1)S(1)} %get-tuple-element.22.chosen.pages, f32[24,128]{1,0:T(8,128)S(1)} %get-tuple-element.23.entries, bf16[8,2176]{1,0:T(8,128)(2,1)S(1)} %collective-permute-done.2.refs_0_, bf16[144,128]{1,0:T(8,128)(2,1)S(1)} %get-tuple-element.32.refs_1_, ...), custom_call_target="tpu_custom_call" | custom-call | flops 20000000000 | bytes 8388608 | tf_op jit(solution)/shard_map/owned/pallas_call | solution.py:377
  10.6 1.0 %collective-permute-start.3 = (bf16[144,128]{1,0:T(8,128)(2,1)S(1)}, bf16[144,128]{1,0:T(8,128)(2,1)S(1)}, u32[]{:S(2)}, u32[]{:S(2)}) collective-permute-start(bf16[144,128]{1,0:T(8,128)(2,1)S(1)} %owned.3), channel_id=1, source_target_pairs={{0,28},{16,0},{4,24},{20,4},{8,20},{24,8},{12,16},{28,12},{1,29},{... | collective-permute-start | bytes 110600 | tf_op jit(solution)/shard_map/ppermute | solution.py:341
  11.6 0.7 %collective-permute-start.4 = (bf16[144,128]{1,0:T(8,128)(2,1)S(1)}, bf16[144,128]{1,0:T(8,128)(2,1)S(1)}, u32[]{:S(2)}, u32[]{:S(2)}) collective-permute-start(bf16[144,128]{1,0:T(8,128)(2,1)S(1)} %get-tuple-element.31.refs_2_), channel_id=1, source_target_pairs={{0,24},{16,0},{4,28},{20,4},{8,16},{24,8},{12,20},{28,12},{1,25},{... | collective-permute-start | bytes 110600 | tf_op jit(solution)/shard_map/ppermute | solution.py:341
  12.4 0.4 %collective-permute-start.6 = (bf16[144,128]{1,0:T(8,128)(2,1)S(1)}, bf16[144,128]{1,0:T(8,128)(2,1)S(1)}, u32[]{:S(2)}, u32[]{:S(2)}) collective-permute-start(bf16[144,128]{1,0:T(8,128)(2,1)S(1)} %get-tuple-element.33), channel_id=1, source_target_pairs={{0,16},{16,0},{4,20},{20,4},{8,24},{24,8},{12,28},{28,12},{1,17},{... | collective-permute-start | bytes 110600 | tf_op jit(solution)/shard_map/ppermute | solution.py:341
  12.8 0.5 %collective-permute-done.3.refs_2_ = bf16[144,128]{1,0:T(8,128)(2,1)S(1)} collective-permute-done((bf16[144,128]{1,0:T(8,128)(2,1)S(1)}, bf16[144,128]{1,0:T(8,128)(2,1)S(1)}, u32[]{:S(2)}, u32[]{:S(2)}) %collective-permute-start.3) | collective-permute-done | bytes 36896 | tf_op jit(solution)/shard_map/ppermute | solution.py:341
  13.2 0.7 %collective-permute-done.4.refs_3_ = bf16[144,128]{1,0:T(8,128)(2,1)S(1)} collective-permute-done((bf16[144,128]{1,0:T(8,128)(2,1)S(1)}, bf16[144,128]{1,0:T(8,128)(2,1)S(1)}, u32[]{:S(2)}, u32[]{:S(2)}) %collective-permute-start.4) | collective-permute-done | bytes 36896 | tf_op jit(solution)/shard_map/ppermute | solution.py:341
  13.9 0.3 %collective-permute-done.5.refs_4_ = bf16[144,128]{1,0:T(8,128)(2,1)S(1)} collective-permute-done((bf16[144,128]{1,0:T(8,128)(2,1)S(1)}, bf16[144,128]{1,0:T(8,128)(2,1)S(1)}, u32[]{:S(2)}, u32[]{:S(2)}) %collective-permute-start.5) | collective-permute-done | bytes 36896 | tf_op jit(solution)/shard_map/ppermute | solution.py:341
  14.2 0.3 %merge.1.attended = bf16[8,2048]{1,0:T(8,128)(2,1)S(1)} custom-call(f32[144,128]{1,0:T(8,128)S(1)} %get-tuple-element.28.refs_0_, f32[144,128]{1,0:T(8,128)S(1)} %get-tuple-element.29.refs_1_, bf16[144,128]{1,0:T(8,128)(2,1)S(1)} %collective-permute-done.3.refs_2_, bf16[144,128]{1,0:T(8,128)(2,1)S(1)} %collective-permute-done.4.refs_3_, ...), custom_call_target="tpu_custom_call" | custom-call | tf_op jit(solution)/shard_map/merge/pallas_call | solution.py:396
  14.6 2.0 %collective-permute-start.7 = (bf16[8,2048]{1,0:T(8,128)(2,1)S(1)}, bf16[8,2048]{1,0:T(8,128)(2,1)S(1)}, u32[]{:S(2)}, u32[]{:S(2)}) collective-permute-start(bf16[8,2048]{1,0:T(8,128)(2,1)S(1)} %merge.1.attended), channel_id=1, source_target_pairs={{0,16},{16,0},{1,17},{17,1},{2,18},{18,2},{3,19},{19,3},{4,20},{20... | collective-permute-start | bytes 98312 | tf_op jit(solution)/shard_map/ppermute | solution.py:404
  16.6 0.9 %collective-permute-done.7.partner = bf16[8,2048]{1,0:T(8,128)(2,1)S(1)} collective-permute-done((bf16[8,2048]{1,0:T(8,128)(2,1)S(1)}, bf16[8,2048]{1,0:T(8,128)(2,1)S(1)}, u32[]{:S(2)}, u32[]{:S(2)}) %collective-permute-start.7) | collective-permute-done | bytes 32800 | tf_op jit(solution)/shard_map/ppermute | solution.py:404
  17.5 1.7 %project.1 = (bf16[8,1024]{1,0:T(8,128)(2,1)S(1)}, bf16[8,1024]{1,0:T(8,128)(2,1)S(1)}, bf16[8,1024]{1,0:T(8,128)(2,1)S(1)}) custom-call(bf16[8,2048]{1,0:T(8,128)(2,1)S(1)} %merge.1.attended, bf16[8,2048]{1,0:T(8,128)(2,1)S(1)} %collective-permute-done.7.partner, bf16[2048,4096]{1,0:T(8,128)(2,1)S(1)} %bitcast.8), custom_call_target="tpu_custom_call" | custom-call | flops 201326592 | bytes 12582912 | tf_op jit(solution)/shard_map/project/pallas_call | solution.py:408
  19.2 1.5 %collective-permute-start.8 = (bf16[8,1024]{1,0:T(8,128)(2,1)S(1)}, bf16[8,1024]{1,0:T(8,128)(2,1)S(1)}, u32[]{:S(2)}, u32[]{:S(2)}) collective-permute-start(bf16[8,1024]{1,0:T(8,128)(2,1)S(1)} %get-tuple-element.34), channel_id=1, source_target_pairs={{0,1},{1,2},{2,3},{3,0},{4,5},{5,6},{6,7},{7,4},{8,9},{9,10},{10,1... | collective-permute-start | bytes 49160 | tf_op jit(solution)/shard_map/ppermute | solution.py:422
  20.7 1.5 %collective-permute-start.9 = (bf16[8,1024]{1,0:T(8,128)(2,1)S(1)}, bf16[8,1024]{1,0:T(8,128)(2,1)S(1)}, u32[]{:S(2)}, u32[]{:S(2)}) collective-permute-start(bf16[8,1024]{1,0:T(8,128)(2,1)S(1)} %get-tuple-element.35), channel_id=1, source_target_pairs={{0,2},{1,3},{2,0},{3,1},{4,6},{5,7},{6,4},{7,5},{8,10},{9,11},{10,... | collective-permute-start | bytes 49160 | tf_op jit(solution)/shard_map/ppermute | solution.py:422
  22.3 1.4 %collective-permute-start.10 = (bf16[8,1024]{1,0:T(8,128)(2,1)S(1)}, bf16[8,1024]{1,0:T(8,128)(2,1)S(1)}, u32[]{:S(2)}, u32[]{:S(2)}) collective-permute-start(bf16[8,1024]{1,0:T(8,128)(2,1)S(1)} %get-tuple-element.36), channel_id=1, source_target_pairs={{0,3},{1,0},{2,1},{3,2},{4,7},{5,4},{6,5},{7,6},{8,11},{9,8},{10,9... | collective-permute-start | bytes 49160 | tf_op jit(solution)/shard_map/ppermute | solution.py:422
  23.7 0.6 %project_own.1 = f32[8,1024]{1,0:T(8,128)S(1)} custom-call(bf16[8,2048]{1,0:T(8,128)(2,1)S(1)} %merge.1.attended, bf16[8,2048]{1,0:T(8,128)(2,1)S(1)} %collective-permute-done.7.partner, bf16[2048,4096]{1,0:T(8,128)(2,1)S(1)} %bitcast.8), custom_call_target="tpu_custom_call" | custom-call | flops 67108864 | bytes 4194304 | tf_op jit(solution)/shard_map/project_own/pallas_call | solution.py:408
  24.3 0.1 collective-permute-done.9
  24.5 1.5 %collective-permute-done.10 = bf16[8,1024]{1,0:T(8,128)(2,1)S(1)} collective-permute-done((bf16[8,1024]{1,0:T(8,128)(2,1)S(1)}, bf16[8,1024]{1,0:T(8,128)(2,1)S(1)}, u32[]{:S(2)}, u32[]{:S(2)}) %collective-permute-start.10) | collective-permute-done | bytes 16416 | tf_op jit(solution)/shard_map/ppermute | solution.py:422
  26.0 0.6 %fusion.1 = bf16[1,8,1024]{2,1,0:T(8,128)(2,1)} fusion(bf16[8,1024]{1,0:T(8,128)(2,1)S(1)} %collective-permute-done.10, bf16[8,1024]{1,0:T(8,128)(2,1)S(1)} %collective-permute-done.9, f32[8,1024]{1,0:T(8,128)S(1)} %project_own.1, bf16[8,1024]{1,0:T(8,128)(2,1)S(1)} %collective-permute-done.8), kind=kLoop, calls=%fused_computation.3 | loop fusion | flops 57344 | bytes 98304 | tf_op jit(solution)/shard_map/broadcast_in_dim | solution.py:425
  (18 shorter events, 0.2 us)
Async XLA Ops:
  0.9 7.7 %collective-permute-start.1 = (bf16[8,2176]{1,0:T(8,128)(2,1)S(1)}, bf16[8,2176]{1,0:T(8,128)(2,1)S(1)}, u32[]{:S(2)}, u32[]{:S(2)}) collective-permute-start(bf16[8,2176]{1,0:T(8,128)(2,1)S(1)} %fusion.qa), channel_id=1, source_target_pairs={{16,4},{0,16},{20,0},{4,20},{24,12},{8,24},{28,8},{12,28},{17,5},{... | collective-permute-start | bytes 104456 | tf_op jit(solution)/shard_map/ppermute | solution.py:341
  1.3 7.3 %collective-permute-start = (bf16[8,2176]{1,0:T(8,128)(2,1)S(1)}, bf16[8,2176]{1,0:T(8,128)(2,1)S(1)}, u32[]{:S(2)}, u32[]{:S(2)}) collective-permute-start(bf16[8,2176]{1,0:T(8,128)(2,1)S(1)} %fusion.qa), channel_id=1, source_target_pairs={{16,8},{0,16},{20,12},{4,20},{24,0},{8,24},{28,4},{12,28},{17,9},{... | collective-permute-start | bytes 104456 | tf_op jit(solution)/shard_map/ppermute | solution.py:341
  4.0 5.8 %collective-permute-start.2 = (bf16[8,2176]{1,0:T(8,128)(2,1)S(1)}, bf16[8,2176]{1,0:T(8,128)(2,1)S(1)}, u32[]{:S(2)}, u32[]{:S(2)}) collective-permute-start(bf16[8,2176]{1,0:T(8,128)(2,1)S(1)} %fusion.qa), channel_id=1, source_target_pairs={{16,12},{0,16},{20,8},{4,20},{24,4},{8,24},{28,0},{12,28},{17,13},... | collective-permute-start | bytes 104456 | tf_op jit(solution)/shard_map/ppermute | solution.py:341
  9.9 7.6 %slice-start = ((s8[16777216]{0:T(1024)(128)(4,1)}), s8[4194304]{0:T(1024)(128)(4,1)S(1)}, s32[]{:S(2)}) async-start(s8[16777216]{0:T(1024)(128)(4,1)} %bitcast.7), calls=%async_computation | async-start | bytes 8388608
  9.9 2.9 %copy-start = (bf16[1,8,512]{2,1,0:T(8,128)(2,1)S(1)}, bf16[1,8,512]{2,1,0:T(8,128)(2,1)}, u32[]{:S(2)}) copy-start(bf16[1,8,512]{2,1,0:T(8,128)(2,1)} %param.14) | copy-start | bytes 24580
  9.9 7.6 %slice-start.1 = ((s8[16777216]{0:T(1024)(128)(4,1)}), s8[4194304]{0:T(1024)(128)(4,1)S(1)}, s32[]{:S(2)}) async-start(s8[16777216]{0:T(1024)(128)(4,1)} %bitcast.7), calls=%async_computation.1 | async-start | bytes 8388608
  9.9 7.6 %slice-start.2 = ((s8[16777216]{0:T(1024)(128)(4,1)}), s8[4194304]{0:T(1024)(128)(4,1)S(1)}, s32[]{:S(2)}) async-start(s8[16777216]{0:T(1024)(128)(4,1)} %bitcast.7), calls=%async_computation.2 | async-start | bytes 8388608
  9.9 7.6 %slice-start.3 = ((s8[16777216]{0:T(1024)(128)(4,1)}), s8[4194304]{0:T(1024)(128)(4,1)S(1)}, s32[]{:S(2)}) async-start(s8[16777216]{0:T(1024)(128)(4,1)} %bitcast.7), calls=%async_computation.3 | async-start | bytes 8388608
  10.6 2.7 %collective-permute-start.3 = (bf16[144,128]{1,0:T(8,128)(2,1)S(1)}, bf16[144,128]{1,0:T(8,128)(2,1)S(1)}, u32[]{:S(2)}, u32[]{:S(2)}) collective-permute-start(bf16[144,128]{1,0:T(8,128)(2,1)S(1)} %owned.3), channel_id=1, source_target_pairs={{0,28},{16,0},{4,24},{20,4},{8,20},{24,8},{12,16},{28,12},{1,29},{... | collective-permute-start | bytes 110600 | tf_op jit(solution)/shard_map/ppermute | solution.py:341
  11.6 2.3 %collective-permute-start.4 = (bf16[144,128]{1,0:T(8,128)(2,1)S(1)}, bf16[144,128]{1,0:T(8,128)(2,1)S(1)}, u32[]{:S(2)}, u32[]{:S(2)}) collective-permute-start(bf16[144,128]{1,0:T(8,128)(2,1)S(1)} %get-tuple-element.31.refs_2_), channel_id=1, source_target_pairs={{0,24},{16,0},{4,28},{20,4},{8,16},{24,8},{12,20},{28,12},{1,25},{... | collective-permute-start | bytes 110600 | tf_op jit(solution)/shard_map/ppermute | solution.py:341
  12.3 2.0 %collective-permute-start.5 = (bf16[144,128]{1,0:T(8,128)(2,1)S(1)}, bf16[144,128]{1,0:T(8,128)(2,1)S(1)}, u32[]{:S(2)}, u32[]{:S(2)}) collective-permute-start(bf16[144,128]{1,0:T(8,128)(2,1)S(1)} %get-tuple-element.32.refs_1_), channel_id=1, source_target_pairs={{0,20},{16,0},{4,16},{20,4},{8,28},{24,8},{12,24},{28,12},{1,21},{... | collective-permute-start | bytes 110600 | tf_op jit(solution)/shard_map/ppermute | solution.py:341
  12.4 1.9 %collective-permute-start.6 = (bf16[144,128]{1,0:T(8,128)(2,1)S(1)}, bf16[144,128]{1,0:T(8,128)(2,1)S(1)}, u32[]{:S(2)}, u32[]{:S(2)}) collective-permute-start(bf16[144,128]{1,0:T(8,128)(2,1)S(1)} %get-tuple-element.33), channel_id=1, source_target_pairs={{0,16},{16,0},{4,20},{20,4},{8,24},{24,8},{12,28},{28,12},{1,17},{... | collective-permute-start | bytes 110600 | tf_op jit(solution)/shard_map/ppermute | solution.py:341
  14.6 2.9 %collective-permute-start.7 = (bf16[8,2048]{1,0:T(8,128)(2,1)S(1)}, bf16[8,2048]{1,0:T(8,128)(2,1)S(1)}, u32[]{:S(2)}, u32[]{:S(2)}) collective-permute-start(bf16[8,2048]{1,0:T(8,128)(2,1)S(1)} %merge.1.attended), channel_id=1, source_target_pairs={{0,16},{16,0},{1,17},{17,1},{2,18},{18,2},{3,19},{19,3},{4,20},{20... | collective-permute-start | bytes 98312 | tf_op jit(solution)/shard_map/ppermute | solution.py:404
  19.2 5.1 %collective-permute-start.8 = (bf16[8,1024]{1,0:T(8,128)(2,1)S(1)}, bf16[8,1024]{1,0:T(8,128)(2,1)S(1)}, u32[]{:S(2)}, u32[]{:S(2)}) collective-permute-start(bf16[8,1024]{1,0:T(8,128)(2,1)S(1)} %get-tuple-element.34), channel_id=1, source_target_pairs={{0,1},{1,2},{2,3},{3,0},{4,5},{5,6},{6,7},{7,4},{8,9},{9,10},{10,1... | collective-permute-start | bytes 49160 | tf_op jit(solution)/shard_map/ppermute | solution.py:422
  20.7 3.7 %collective-permute-start.9 = (bf16[8,1024]{1,0:T(8,128)(2,1)S(1)}, bf16[8,1024]{1,0:T(8,128)(2,1)S(1)}, u32[]{:S(2)}, u32[]{:S(2)}) collective-permute-start(bf16[8,1024]{1,0:T(8,128)(2,1)S(1)} %get-tuple-element.35), channel_id=1, source_target_pairs={{0,2},{1,3},{2,0},{3,1},{4,6},{5,7},{6,4},{7,5},{8,10},{9,11},{10,... | collective-permute-start | bytes 49160 | tf_op jit(solution)/shard_map/ppermute | solution.py:422
  22.3 3.7 %collective-permute-start.10 = (bf16[8,1024]{1,0:T(8,128)(2,1)S(1)}, bf16[8,1024]{1,0:T(8,128)(2,1)S(1)}, u32[]{:S(2)}, u32[]{:S(2)}) collective-permute-start(bf16[8,1024]{1,0:T(8,128)(2,1)S(1)} %get-tuple-element.36), channel_id=1, source_target_pairs={{0,3},{1,0},{2,1},{3,2},{4,7},{5,4},{6,5},{7,6},{8,11},{9,8},{10,9... | collective-permute-start | bytes 49160 | tf_op jit(solution)/shard_map/ppermute | solution.py:422

commit v5 on v4

--- a/solution.py
+++ b/solution.py
@@ -97,7 +97,7 @@
     write_part(out, acc, top, total, held, per_held)
 
 
-def fetch_pages(rows, lists_ready, send, tables, lengths, maxp, group, kv, pages, valid, flags, sems):
+def fetch_pages(rows, lists_ready, send, tables, lengths, maxp, group, kv, pages, valid, flags, listed, sems):
     slots = kv.shape[0]
     lane_row = lax.rem(lax.broadcasted_iota(jnp.int32, (1, LANES), 1), rows)
     for i in range(slots):
@@ -119,22 +119,34 @@
             here = jnp.logical_and(slot < slots, flags[jnp.minimum(slot, slots - 1)] == 0)
             needed = jnp.logical_and(tokens > 0, here)
 
+            listed[0, found] = r
+            listed[1, found] = tokens
+
             @pl.when(needed)
-            def _(slot=slot, r=r, at=found, tokens=tokens):
+            def _(slot=slot, at=found):
                 page_copy(slot, at).start()
-                valid[pl.ds(at, 1), :] = jnp.where(lane_row == r, tokens.astype(jnp.float32), 0.0)
 
             found = found + needed.astype(jnp.int32)
     chunks = jnp.maximum((found + CHUNK - 1) // CHUNK, STATIC[0])
 
     def fill(i, _):
         page_copy(0, i).start()
-        valid[pl.ds(i, 1), :] = jnp.zeros((1, LANES), jnp.float32)
+        listed[0, i] = 0
+        listed[1, i] = 0
         return 0
 
     lax.fori_loop(found, chunks * CHUNK, fill, 0)
     last = valid.shape[0] - 1
     valid[last : last + 1, :] = jnp.full((1, LANES), chunks.astype(jnp.float32), jnp.float32)
+
+    def describe(c, _):
+        for i in range(CHUNK):
+            at = c * CHUNK + i
+            tokens = listed[1, at].astype(jnp.float32)
+            valid[pl.ds(at, 1), :] = jnp.where(lane_row == listed[0, at], tokens, 0.0)
+        return 0
+
+    lax.fori_loop(0, chunks, describe, 0)
 
     def wait(c, _):
         for i in range(CHUNK):
@@ -227,7 +239,7 @@
 
 def first_kernel(held, per_held, groups, maxp, qa, send_hbm, wanted_hbm, tables_hbm, lengths_hbm, kv, *refs):
     sent, chosen, entries, valid, send, wanted, tables, lengths = refs[:8]
-    flags, page_list, slot_list, list_sems, sems = refs[8:]
+    flags, listed, page_list, slot_list, list_sems, sems = refs[8:]
     group = lax.axis_index("group")
     prefill = lax.axis_index("role") == 0
     lists = ((send_hbm, send), (wanted_hbm, wanted), (tables_hbm, tables), (lengths_hbm, lengths))
@@ -255,7 +267,7 @@
 
     @pl.when(jnp.logical_not(prefill))
     def _():
-        fetch_pages(qa.shape[0], lists_ready, send, tables, lengths, maxp, group, kv, chosen, valid, flags, sems)
+        fetch_pages(qa.shape[0], lists_ready, send, tables, lengths, maxp, group, kv, chosen, valid, flags, listed, sems)
 
 
 def fresh_part(qa, new_kv, out, held, per_held):
@@ -308,12 +320,11 @@
 
 
 def project_kernel(steps, attended, partner, weight, *outs):
-    tps = lax.axis_size("tp")
     share = outs[0].shape[1]
     here = jnp.where(lax.axis_index("role") == 0, partner[...].astype(jnp.float32), attended[...].astype(jnp.float32))
     here = here.astype(jnp.bfloat16)
     for d, out in zip(steps, outs):
-        first = lax.rem(lax.axis_index("tp") + d, tps) * share
+        first = lax.bitwise_xor(lax.axis_index("tp"), d) * share
         columns = pl.ds(pl.multiple_of(first, LANES), share)
         out[...] = jnp.dot(here, weight[:, columns], preferred_element_type=jnp.float32).astype(out.dtype)
 
@@ -364,6 +375,7 @@
         scratch_shapes=[
             *[pltpu.SMEM(x.shape, jnp.int32) for x in lists],
             pltpu.SMEM((slots + 1,), jnp.int32),
+            pltpu.SMEM((2, read_count), jnp.int32),
             pltpu.SMEM((chosen_count + 1,), jnp.int32),
             pltpu.SMEM((chosen_count + 1,), jnp.int32),
             pltpu.SemaphoreType.DMA((len(lists),)),
@@ -417,9 +429,9 @@
             name=name,
         )(attended, partner, out_weight)
 
-    steps = list(range(1, tps))
+    steps = sorted(range(1, tps), key=lambda d: -d.bit_count())
     sent = project(steps, jnp.bfloat16, "project")
-    arrived = [lax.ppermute(part, "tp", [(i, (i + d) % tps) for i in range(tps)]) for d, part in zip(steps, sent)]
+    arrived = [lax.ppermute(part, "tp", [(i, i ^ d) for i in range(tps)]) for d, part in zip(steps, sent)]
     own = project([0], jnp.float32, "project_own")[0]
     total = functools.reduce(jnp.add, [part.astype(jnp.float32) for part in arrived], own)
     return total.astype(jnp.bfloat16)[None]

time: 26.9 us -> 26.6 us (0.989)
  starting transfers between devices: 12.9 us -> 11.8 us
  waiting for transfers between devices: 3.99 us -> 4.92 us
    ppermute x3, starting transfers between devices: 4.46 us -> 3.5 us  [per_device(): lax.ppermute(part, 'tp', [(i, i ^ d) for i in range(tps)])]
    ppermute x3, waiting for transfers between devices: 1.66 us -> 2.59 us  [per_device(): lax.ppermute(part, 'tp', [(i, i ^ d) for i in range(tps)])]
  transfers between devices with their start and end apart: 11 -> 11, of which waited for: 6 -> 7; matrix products, arithmetic and copies ran while one was open for 0% -> 0% of each run, Pallas kernels for 20% -> 20%
where the time goes in v5:
time: 26.6 us; the launch traced here: 26.5 us
  starting transfers between devices  11.8 us (44%)
  Pallas kernels  8.07 us (30%)
  waiting for transfers between devices  4.92 us (18%)
  other arithmetic  1.5 us (6%)
    ppermute x7, starting transfers between devices, paired(): return lax.ppermute(value, ('role', 'group'), pairs)  6.41 us
    pallas_call x1, Pallas kernels, per_device(): pl.pallas_call(functools.partial(first_kernel, held, per_held, groups, ma...  3.52 us
    ppermute x3, starting transfers between devices, per_device(): lax.ppermute(part, 'tp', [(i, i ^ d) for i in range(tps)])  3.5 us
    ppermute x3, waiting for transfers between devices, per_device(): lax.ppermute(part, 'tp', [(i, i ^ d) for i in range(tps)])  2.59 us
    pallas_call x2, Pallas kernels, project(): pl.pallas_call(functools.partial(project_kernel, steps), out_shape=[jax.S...  2.38 us
    ppermute x1, starting transfers between devices, per_device(): partner = lax.ppermute(attended, 'role', [(0, 1), (1, 0)])  1.92 us
    pallas_call x2, Pallas kernels, per_device(): pl.pallas_call(functools.partial(second_kernel, held, per_held, maxp, fir...  1.83 us
    ppermute x7, waiting for transfers between devices, paired(): return lax.ppermute(value, ('role', 'group'), pairs)  1.48 us
  transfers between devices with their start and end apart: 11, of which 7 were waited for; matrix products, arithmetic and copies ran while one was open for 0% of the time, Pallas kernels for 20%

profile of v5, /device:TPU:0, one launch (start us, length us, event | category | flops | bytes accessed | tf_op | source)
XLA Modules:
  0.0 26.5 jit_solution(5260076657480309957)
XLA Ops:
  0.0 0.9 %fusion.qa = bf16[8,2176]{1,0:T(8,128)(2,1)S(1)} fusion(s32[1,8]{1,0:T(1,128)} %lengths_hbm.1, s32[8,8]{1,0:T(8,128)} %bitcast.12, bf16[8,2048]{1,0:T(8,128)(2,1)} %bitcast.11), kind=kLoop, calls=%fused_computation.1 | loop fusion | flops 156672 | bytes 67872 | tf_op jit(solution)/shard_map/add | solution.py:348
  0.9 0.5 %collective-permute-start.1 = (bf16[8,2176]{1,0:T(8,128)(2,1)S(1)}, bf16[8,2176]{1,0:T(8,128)(2,1)S(1)}, u32[]{:S(2)}, u32[]{:S(2)}) collective-permute-start(bf16[8,2176]{1,0:T(8,128)(2,1)S(1)} %fusion.qa), channel_id=1, source_target_pairs={{16,4},{0,16},{20,0},{4,20},{24,12},{8,24},{28,8},{12,28},{17,5},{... | collective-permute-start | bytes 104456 | tf_op jit(solution)/shard_map/ppermute | solution.py:352
  1.3 2.7 %collective-permute-start = (bf16[8,2176]{1,0:T(8,128)(2,1)S(1)}, bf16[8,2176]{1,0:T(8,128)(2,1)S(1)}, u32[]{:S(2)}, u32[]{:S(2)}) collective-permute-start(bf16[8,2176]{1,0:T(8,128)(2,1)S(1)} %fusion.qa), channel_id=1, source_target_pairs={{16,8},{0,16},{20,12},{4,20},{24,0},{8,24},{28,4},{12,28},{17,9},{... | collective-permute-start | bytes 104456 | tf_op jit(solution)/shard_map/ppermute | solution.py:352
  4.0 1.1 %collective-permute-start.2 = (bf16[8,2176]{1,0:T(8,128)(2,1)S(1)}, bf16[8,2176]{1,0:T(8,128)(2,1)S(1)}, u32[]{:S(2)}, u32[]{:S(2)}) collective-permute-start(bf16[8,2176]{1,0:T(8,128)(2,1)S(1)} %fusion.qa), channel_id=1, source_target_pairs={{16,12},{0,16},{20,8},{4,20},{24,4},{8,24},{28,0},{12,28},{17,13},... | collective-permute-start | bytes 104456 | tf_op jit(solution)/shard_map/ppermute | solution.py:352
  5.1 3.5 %resident.1 = (bf16[144,128]{1,0:T(8,128)(2,1)S(1)}, bf16[64,128,512]{2,1,0:T(8,128)(2,1)S(1)}, f32[24,128]{1,0:T(8,128)S(1)}, f32[72,128]{1,0:T(8,128)S(1)}) custom-call(bf16[8,2176]{1,0:T(8,128)(2,1)S(1)} %fusion.qa, s32[3,4,12]{2,1,0:T(4,128)} %bitcast.14, s32[4,6]{1,0:T(4,128)} %wanted_hbm.1, s32[8,8]{1,0:T(8,128)} %bitcast.13, s32[1,8]{1,0:T(1,128)} %lengths_hbm.1, ...), custom_call_target="tpu_custom_call" | custom-call | tf_op jit(solution)/shard_map/resident/pallas_call | solution.py:365
  8.6 1.2 %owned.2 = (bf16[144,128]{1,0:T(8,128)(2,1)S(1)}, bf16[144,128]{1,0:T(8,128)(2,1)S(1)}) custom-call(bf16[64,128,512]{2,1,0:T(8,128)(2,1)S(1)} %get-tuple-element.22.chosen.pages, f32[24,128]{1,0:T(8,128)S(1)} %get-tuple-element.23.entries, bf16[8,2176]{1,0:T(8,128)(2,1)S(1)} %collective-permute-done.refs_0_, bf16[8,2176]{1,0:T(8,128)(2,1)S(1)} %collective-permute-done.1.refs_1_), custom_call_target="tpu_custom_call" | custom-call | flops 20000000000 | bytes 8388608 | tf_op jit(solution)/shard_map/owned/pallas_call | solution.py:389
  9.9 0.6 %owned.3 = bf16[144,128]{1,0:T(8,128)(2,1)S(1)} custom-call(bf16[64,128,512]{2,1,0:T(8,128)(2,1)S(1)} %get-tuple-element.22.chosen.pages, f32[24,128]{1,0:T(8,128)S(1)} %get-tuple-element.23.entries, bf16[8,2176]{1,0:T(8,128)(2,1)S(1)} %collective-permute-done.2.refs_0_, bf16[144,128]{1,0:T(8,128)(2,1)S(1)} %get-tuple-element.32.refs_1_, ...), custom_call_target="tpu_custom_call" | custom-call | flops 20000000000 | bytes 8388608 | tf_op jit(solution)/shard_map/owned/pallas_call | solution.py:389
  10.6 0.8 %collective-permute-start.3 = (bf16[144,128]{1,0:T(8,128)(2,1)S(1)}, bf16[144,128]{1,0:T(8,128)(2,1)S(1)}, u32[]{:S(2)}, u32[]{:S(2)}) collective-permute-start(bf16[144,128]{1,0:T(8,128)(2,1)S(1)} %owned.3), channel_id=1, source_target_pairs={{0,28},{16,0},{4,24},{20,4},{8,20},{24,8},{12,16},{28,12},{1,29},{... | collective-permute-start | bytes 110600 | tf_op jit(solution)/shard_map/ppermute | solution.py:352
  11.4 0.8 %collective-permute-start.4 = (bf16[144,128]{1,0:T(8,128)(2,1)S(1)}, bf16[144,128]{1,0:T(8,128)(2,1)S(1)}, u32[]{:S(2)}, u32[]{:S(2)}) collective-permute-start(bf16[144,128]{1,0:T(8,128)(2,1)S(1)} %get-tuple-element.31.refs_2_), channel_id=1, source_target_pairs={{0,24},{16,0},{4,28},{20,4},{8,16},{24,8},{12,20},{28,12},{1,25},{... | collective-permute-start | bytes 110600 | tf_op jit(solution)/shard_map/ppermute | solution.py:352
  12.4 0.4 %collective-permute-start.6 = (bf16[144,128]{1,0:T(8,128)(2,1)S(1)}, bf16[144,128]{1,0:T(8,128)(2,1)S(1)}, u32[]{:S(2)}, u32[]{:S(2)}) collective-permute-start(bf16[144,128]{1,0:T(8,128)(2,1)S(1)} %get-tuple-element.33), channel_id=1, source_target_pairs={{0,16},{16,0},{4,20},{20,4},{8,24},{24,8},{12,28},{28,12},{1,17},{... | collective-permute-start | bytes 110600 | tf_op jit(solution)/shard_map/ppermute | solution.py:352
  13.0 0.8 %collective-permute-done.4.refs_3_ = bf16[144,128]{1,0:T(8,128)(2,1)S(1)} collective-permute-done((bf16[144,128]{1,0:T(8,128)(2,1)S(1)}, bf16[144,128]{1,0:T(8,128)(2,1)S(1)}, u32[]{:S(2)}, u32[]{:S(2)}) %collective-permute-start.4) | collective-permute-done | bytes 36896 | tf_op jit(solution)/shard_map/ppermute | solution.py:352
  13.9 0.3 %collective-permute-done.5.refs_4_ = bf16[144,128]{1,0:T(8,128)(2,1)S(1)} collective-permute-done((bf16[144,128]{1,0:T(8,128)(2,1)S(1)}, bf16[144,128]{1,0:T(8,128)(2,1)S(1)}, u32[]{:S(2)}, u32[]{:S(2)}) %collective-permute-start.5) | collective-permute-done | bytes 36896 | tf_op jit(solution)/shard_map/ppermute | solution.py:352
  14.2 0.3 %merge.1.attended = bf16[8,2048]{1,0:T(8,128)(2,1)S(1)} custom-call(f32[144,128]{1,0:T(8,128)S(1)} %get-tuple-element.28.refs_0_, f32[144,128]{1,0:T(8,128)S(1)} %get-tuple-element.29.refs_1_, bf16[144,128]{1,0:T(8,128)(2,1)S(1)} %collective-permute-done.3.refs_2_, bf16[144,128]{1,0:T(8,128)(2,1)S(1)} %collective-permute-done.4.refs_3_, ...), custom_call_target="tpu_custom_call" | custom-call | tf_op jit(solution)/shard_map/merge/pallas_call | solution.py:408
  14.6 1.9 %collective-permute-start.7 = (bf16[8,2048]{1,0:T(8,128)(2,1)S(1)}, bf16[8,2048]{1,0:T(8,128)(2,1)S(1)}, u32[]{:S(2)}, u32[]{:S(2)}) collective-permute-start(bf16[8,2048]{1,0:T(8,128)(2,1)S(1)} %merge.1.attended), channel_id=1, source_target_pairs={{0,16},{16,0},{1,17},{17,1},{2,18},{18,2},{3,19},{19,3},{4,20},{20... | collective-permute-start | bytes 98312 | tf_op jit(solution)/shard_map/ppermute | solution.py:416
  16.5 0.9 %collective-permute-done.7.partner = bf16[8,2048]{1,0:T(8,128)(2,1)S(1)} collective-permute-done((bf16[8,2048]{1,0:T(8,128)(2,1)S(1)}, bf16[8,2048]{1,0:T(8,128)(2,1)S(1)}, u32[]{:S(2)}, u32[]{:S(2)}) %collective-permute-start.7) | collective-permute-done | bytes 32800 | tf_op jit(solution)/shard_map/ppermute | solution.py:416
  17.4 1.7 %project.1 = (bf16[8,1024]{1,0:T(8,128)(2,1)S(1)}, bf16[8,1024]{1,0:T(8,128)(2,1)S(1)}, bf16[8,1024]{1,0:T(8,128)(2,1)S(1)}) custom-call(bf16[8,2048]{1,0:T(8,128)(2,1)S(1)} %merge.1.attended, bf16[8,2048]{1,0:T(8,128)(2,1)S(1)} %collective-permute-done.7.partner, bf16[2048,4096]{1,0:T(8,128)(2,1)S(1)} %bitcast.8), custom_call_target="tpu_custom_call" | custom-call | flops 201326592 | bytes 12582912 | tf_op jit(solution)/shard_map/project/pallas_call | solution.py:420
  19.1 2.5 %collective-permute-start.8 = (bf16[8,1024]{1,0:T(8,128)(2,1)S(1)}, bf16[8,1024]{1,0:T(8,128)(2,1)S(1)}, u32[]{:S(2)}, u32[]{:S(2)}) collective-permute-start(bf16[8,1024]{1,0:T(8,128)(2,1)S(1)} %get-tuple-element.34), channel_id=1, source_target_pairs={{0,3},{1,2},{2,1},{3,0},{4,7},{5,6},{6,5},{7,4},{8,11},{9,10},{10,... | collective-permute-start | bytes 49160 | tf_op jit(solution)/shard_map/ppermute | solution.py:434
  21.6 0.5 %collective-permute-start.9 = (bf16[8,1024]{1,0:T(8,128)(2,1)S(1)}, bf16[8,1024]{1,0:T(8,128)(2,1)S(1)}, u32[]{:S(2)}, u32[]{:S(2)}) collective-permute-start(bf16[8,1024]{1,0:T(8,128)(2,1)S(1)} %get-tuple-element.35), channel_id=1, source_target_pairs={{0,1},{1,0},{2,3},{3,2},{4,5},{5,4},{6,7},{7,6},{8,9},{9,8},{10,11... | collective-permute-start | bytes 49160 | tf_op jit(solution)/shard_map/ppermute | solution.py:434
  22.1 0.5 %collective-permute-start.10 = (bf16[8,1024]{1,0:T(8,128)(2,1)S(1)}, bf16[8,1024]{1,0:T(8,128)(2,1)S(1)}, u32[]{:S(2)}, u32[]{:S(2)}) collective-permute-start(bf16[8,1024]{1,0:T(8,128)(2,1)S(1)} %get-tuple-element.36), channel_id=1, source_target_pairs={{0,2},{1,3},{2,0},{3,1},{4,6},{5,7},{6,4},{7,5},{8,10},{9,11},{10,... | collective-permute-start | bytes 49160 | tf_op jit(solution)/shard_map/ppermute | solution.py:434
  22.6 0.6 %project_own.1 = f32[8,1024]{1,0:T(8,128)S(1)} custom-call(bf16[8,2048]{1,0:T(8,128)(2,1)S(1)} %merge.1.attended, bf16[8,2048]{1,0:T(8,128)(2,1)S(1)} %collective-permute-done.7.partner, bf16[2048,4096]{1,0:T(8,128)(2,1)S(1)} %bitcast.8), custom_call_target="tpu_custom_call" | custom-call | flops 67108864 | bytes 4194304 | tf_op jit(solution)/shard_map/project_own/pallas_call | solution.py:420
  23.3 0.5 %collective-permute-done.8 = bf16[8,1024]{1,0:T(8,128)(2,1)S(1)} collective-permute-done((bf16[8,1024]{1,0:T(8,128)(2,1)S(1)}, bf16[8,1024]{1,0:T(8,128)(2,1)S(1)}, u32[]{:S(2)}, u32[]{:S(2)}) %collective-permute-start.8) | collective-permute-done | bytes 16416 | tf_op jit(solution)/shard_map/ppermute | solution.py:434
  23.8 1.5 %collective-permute-done.9 = bf16[8,1024]{1,0:T(8,128)(2,1)S(1)} collective-permute-done((bf16[8,1024]{1,0:T(8,128)(2,1)S(1)}, bf16[8,1024]{1,0:T(8,128)(2,1)S(1)}, u32[]{:S(2)}, u32[]{:S(2)}) %collective-permute-start.9) | collective-permute-done | bytes 16416 | tf_op jit(solution)/shard_map/ppermute | solution.py:434
  25.3 0.5 %collective-permute-done.10 = bf16[8,1024]{1,0:T(8,128)(2,1)S(1)} collective-permute-done((bf16[8,1024]{1,0:T(8,128)(2,1)S(1)}, bf16[8,1024]{1,0:T(8,128)(2,1)S(1)}, u32[]{:S(2)}, u32[]{:S(2)}) %collective-permute-start.10) | collective-permute-done | bytes 16416 | tf_op jit(solution)/shard_map/ppermute | solution.py:434
  25.9 0.6 %fusion.1 = bf16[1,8,1024]{2,1,0:T(8,128)(2,1)} fusion(bf16[8,1024]{1,0:T(8,128)(2,1)S(1)} %collective-permute-done.10, bf16[8,1024]{1,0:T(8,128)(2,1)S(1)} %collective-permute-done.9, f32[8,1024]{1,0:T(8,128)S(1)} %project_own.1, bf16[8,1024]{1,0:T(8,128)(2,1)S(1)} %collective-permute-done.8), kind=kLoop, calls=%fused_computation.3 | loop fusion | flops 57344 | bytes 98304 | tf_op jit(solution)/shard_map/broadcast_in_dim | solution.py:437
  (18 shorter events, 0.4 us)
Async XLA Ops:
  0.9 7.7 %collective-permute-start.1 = (bf16[8,2176]{1,0:T(8,128)(2,1)S(1)}, bf16[8,2176]{1,0:T(8,128)(2,1)S(1)}, u32[]{:S(2)}, u32[]{:S(2)}) collective-permute-start(bf16[8,2176]{1,0:T(8,128)(2,1)S(1)} %fusion.qa), channel_id=1, source_target_pairs={{16,4},{0,16},{20,0},{4,20},{24,12},{8,24},{28,8},{12,28},{17,5},{... | collective-permute-start | bytes 104456 | tf_op jit(solution)/shard_map/ppermute | solution.py:352
  1.3 7.3 %collective-permute-start = (bf16[8,2176]{1,0:T(8,128)(2,1)S(1)}, bf16[8,2176]{1,0:T(8,128)(2,1)S(1)}, u32[]{:S(2)}, u32[]{:S(2)}) collective-permute-start(bf16[8,2176]{1,0:T(8,128)(2,1)S(1)} %fusion.qa), channel_id=1, source_target_pairs={{16,8},{0,16},{20,12},{4,20},{24,0},{8,24},{28,4},{12,28},{17,9},{... | collective-permute-start | bytes 104456 | tf_op jit(solution)/shard_map/ppermute | solution.py:352
  4.0 5.8 %collective-permute-start.2 = (bf16[8,2176]{1,0:T(8,128)(2,1)S(1)}, bf16[8,2176]{1,0:T(8,128)(2,1)S(1)}, u32[]{:S(2)}, u32[]{:S(2)}) collective-permute-start(bf16[8,2176]{1,0:T(8,128)(2,1)S(1)} %fusion.qa), channel_id=1, source_target_pairs={{16,12},{0,16},{20,8},{4,20},{24,4},{8,24},{28,0},{12,28},{17,13},... | collective-permute-start | bytes 104456 | tf_op jit(solution)/shard_map/ppermute | solution.py:352
  9.9 7.5 %slice-start = ((s8[16777216]{0:T(1024)(128)(4,1)}), s8[4194304]{0:T(1024)(128)(4,1)S(1)}, s32[]{:S(2)}) async-start(s8[16777216]{0:T(1024)(128)(4,1)} %bitcast.7), calls=%async_computation | async-start | bytes 8388608
  9.9 2.9 %copy-start = (bf16[1,8,512]{2,1,0:T(8,128)(2,1)S(1)}, bf16[1,8,512]{2,1,0:T(8,128)(2,1)}, u32[]{:S(2)}) copy-start(bf16[1,8,512]{2,1,0:T(8,128)(2,1)} %param.14) | copy-start | bytes 24580
  9.9 7.5 %slice-start.1 = ((s8[16777216]{0:T(1024)(128)(4,1)}), s8[4194304]{0:T(1024)(128)(4,1)S(1)}, s32[]{:S(2)}) async-start(s8[16777216]{0:T(1024)(128)(4,1)} %bitcast.7), calls=%async_computation.1 | async-start | bytes 8388608
  9.9 7.5 %slice-start.2 = ((s8[16777216]{0:T(1024)(128)(4,1)}), s8[4194304]{0:T(1024)(128)(4,1)S(1)}, s32[]{:S(2)}) async-start(s8[16777216]{0:T(1024)(128)(4,1)} %bitcast.7), calls=%async_computation.2 | async-start | bytes 8388608
  9.9 7.5 %slice-start.3 = ((s8[16777216]{0:T(1024)(128)(4,1)}), s8[4194304]{0:T(1024)(128)(4,1)S(1)}, s32[]{:S(2)}) async-start(s8[16777216]{0:T(1024)(128)(4,1)} %bitcast.7), calls=%async_computation.3 | async-start | bytes 8388608
  10.6 2.5 %collective-permute-start.3 = (bf16[144,128]{1,0:T(8,128)(2,1)S(1)}, bf16[144,128]{1,0:T(8,128)(2,1)S(1)}, u32[]{:S(2)}, u32[]{:S(2)}) collective-permute-start(bf16[144,128]{1,0:T(8,128)(2,1)S(1)} %owned.3), channel_id=1, source_target_pairs={{0,28},{16,0},{4,24},{20,4},{8,20},{24,8},{12,16},{28,12},{1,29},{... | collective-permute-start | bytes 110600 | tf_op jit(solution)/shard_map/ppermute | solution.py:352
  11.4 2.5 %collective-permute-start.4 = (bf16[144,128]{1,0:T(8,128)(2,1)S(1)}, bf16[144,128]{1,0:T(8,128)(2,1)S(1)}, u32[]{:S(2)}, u32[]{:S(2)}) collective-permute-start(bf16[144,128]{1,0:T(8,128)(2,1)S(1)} %get-tuple-element.31.refs_2_), channel_id=1, source_target_pairs={{0,24},{16,0},{4,28},{20,4},{8,16},{24,8},{12,20},{28,12},{1,25},{... | collective-permute-start | bytes 110600 | tf_op jit(solution)/shard_map/ppermute | solution.py:352
  12.3 2.0 %collective-permute-start.5 = (bf16[144,128]{1,0:T(8,128)(2,1)S(1)}, bf16[144,128]{1,0:T(8,128)(2,1)S(1)}, u32[]{:S(2)}, u32[]{:S(2)}) collective-permute-start(bf16[144,128]{1,0:T(8,128)(2,1)S(1)} %get-tuple-element.32.refs_1_), channel_id=1, source_target_pairs={{0,20},{16,0},{4,16},{20,4},{8,28},{24,8},{12,24},{28,12},{1,21},{... | collective-permute-start | bytes 110600 | tf_op jit(solution)/shard_map/ppermute | solution.py:352
  12.4 1.9 %collective-permute-start.6 = (bf16[144,128]{1,0:T(8,128)(2,1)S(1)}, bf16[144,128]{1,0:T(8,128)(2,1)S(1)}, u32[]{:S(2)}, u32[]{:S(2)}) collective-permute-start(bf16[144,128]{1,0:T(8,128)(2,1)S(1)} %get-tuple-element.33), channel_id=1, source_target_pairs={{0,16},{16,0},{4,20},{20,4},{8,24},{24,8},{12,28},{28,12},{1,17},{... | collective-permute-start | bytes 110600 | tf_op jit(solution)/shard_map/ppermute | solution.py:352
  14.6 2.8 %collective-permute-start.7 = (bf16[8,2048]{1,0:T(8,128)(2,1)S(1)}, bf16[8,2048]{1,0:T(8,128)(2,1)S(1)}, u32[]{:S(2)}, u32[]{:S(2)}) collective-permute-start(bf16[8,2048]{1,0:T(8,128)(2,1)S(1)} %merge.1.attended), channel_id=1, source_target_pairs={{0,16},{16,0},{1,17},{17,1},{2,18},{18,2},{3,19},{19,3},{4,20},{20... | collective-permute-start | bytes 98312 | tf_op jit(solution)/shard_map/ppermute | solution.py:416
  19.1 4.7 %collective-permute-start.8 = (bf16[8,1024]{1,0:T(8,128)(2,1)S(1)}, bf16[8,1024]{1,0:T(8,128)(2,1)S(1)}, u32[]{:S(2)}, u32[]{:S(2)}) collective-permute-start(bf16[8,1024]{1,0:T(8,128)(2,1)S(1)} %get-tuple-element.34), channel_id=1, source_target_pairs={{0,3},{1,2},{2,1},{3,0},{4,7},{5,6},{6,5},{7,4},{8,11},{9,10},{10,... | collective-permute-start | bytes 49160 | tf_op jit(solution)/shard_map/ppermute | solution.py:434
  21.6 3.7 %collective-permute-start.9 = (bf16[8,1024]{1,0:T(8,128)(2,1)S(1)}, bf16[8,1024]{1,0:T(8,128)(2,1)S(1)}, u32[]{:S(2)}, u32[]{:S(2)}) collective-permute-start(bf16[8,1024]{1,0:T(8,128)(2,1)S(1)} %get-tuple-element.35), channel_id=1, source_target_pairs={{0,1},{1,0},{2,3},{3,2},{4,5},{5,4},{6,7},{7,6},{8,9},{9,8},{10,11... | collective-permute-start | bytes 49160 | tf_op jit(solution)/shard_map/ppermute | solution.py:434
  22.1 3.7 %collective-permute-start.10 = (bf16[8,1024]{1,0:T(8,128)(2,1)S(1)}, bf16[8,1024]{1,0:T(8,128)(2,1)S(1)}, u32[]{:S(2)}, u32[]{:S(2)}) collective-permute-start(bf16[8,1024]{1,0:T(8,128)(2,1)S(1)} %get-tuple-element.36), channel_id=1, source_target_pairs={{0,2},{1,3},{2,0},{3,1},{4,6},{5,7},{6,4},{7,5},{8,10},{9,11},{10,... | collective-permute-start | bytes 49160 | tf_op jit(solution)/shard_map/ppermute | solution.py:434

commit v6 on v5

--- a/solution.py
+++ b/solution.py
@@ -319,7 +319,8 @@
     out[...] = jnp.concatenate([merged[h * rows : (h + 1) * rows] for h in range(heads)], 1).astype(out.dtype)
 
 
-def project_kernel(steps, attended, partner, weight, *outs):
+def project_kernel(steps, attended, partner, weight, *refs):
+    outs = refs[len(refs) - len(steps) :]
     share = outs[0].shape[1]
     here = jnp.where(lax.axis_index("role") == 0, partner[...].astype(jnp.float32), attended[...].astype(jnp.float32))
     here = here.astype(jnp.bfloat16)
@@ -416,21 +417,22 @@
     partner = lax.ppermute(attended, "role", [(0, 1), (1, 0)])
     share = out_weight.shape[1] // tps
 
-    def project(steps, dtype, name):
+    def project(steps, dtype, name, after=()):
         return pl.pallas_call(
             functools.partial(project_kernel, steps),
             out_shape=[jax.ShapeDtypeStruct((rows, share), dtype)] * len(steps),
-            in_specs=[vmem] * 3,
+            in_specs=[vmem] * (3 + len(after)),
             out_specs=[vmem] * len(steps),
             compiler_params=pltpu.CompilerParams(vmem_limit_bytes=24 * MIB),
             cost_estimate=pl.CostEstimate(
                 flops=len(steps) * 32 * wide * share, bytes_accessed=len(steps) * 2 * wide * share, transcendentals=0
             ),
             name=name,
-        )(attended, partner, out_weight)
+        )(attended, partner, out_weight, *after)
 
     steps = sorted(range(1, tps), key=lambda d: -d.bit_count())
-    sent = project(steps, jnp.bfloat16, "project")
+    sent = list(project(steps[:1], jnp.bfloat16, "project_far"))
+    sent += project(steps[1:], jnp.bfloat16, "project_near", sent)
     arrived = [lax.ppermute(part, "tp", [(i, i ^ d) for i in range(tps)]) for d, part in zip(steps, sent)]
     own = project([0], jnp.float32, "project_own")[0]
     total = functools.reduce(jnp.add, [part.astype(jnp.float32) for part in arrived], own)

time: 26.6 us -> 26.9 us (1.011)
    pallas_call x2 -> x3, Pallas kernels: 2.38 us -> 2.48 us  [project(): pl.pallas_call(functools.partial(project_kernel, steps), out_shape=[jax.S...]
  transfers between devices with their start and end apart: 11 -> 11, of which waited for: 7 -> 6; matrix products, arithmetic and copies ran while one was open for 0% -> 0% of each run, Pallas kernels for 20% -> 25%
where the time goes in v6:
time: 26.9 us; the launch traced here: 26.6 us
  starting transfers between devices  11.8 us (44%)
  Pallas kernels  8.17 us (30%)
  waiting for transfers between devices  4.92 us (18%)
  other arithmetic  1.5 us (6%)
    ppermute x7, starting transfers between devices, paired(): return lax.ppermute(value, ('role', 'group'), pairs)  6.41 us
    pallas_call x1, Pallas kernels, per_device(): pl.pallas_call(functools.partial(first_kernel, held, per_held, groups, ma...  3.52 us
    ppermute x3, starting transfers between devices, per_device(): lax.ppermute(part, 'tp', [(i, i ^ d) for i in range(tps)])  3.52 us
    ppermute x3, waiting for transfers between devices, per_device(): lax.ppermute(part, 'tp', [(i, i ^ d) for i in range(tps)])  2.59 us
    pallas_call x3, Pallas kernels, project(): pl.pallas_call(functools.partial(project_kernel, steps), out_shape=[jax.S...  2.48 us
    ppermute x1, starting transfers between devices, per_device(): partner = lax.ppermute(attended, 'role', [(0, 1), (1, 0)])  1.91 us
    pallas_call x2, Pallas kernels, per_device(): pl.pallas_call(functools.partial(second_kernel, held, per_held, maxp, fir...  1.83 us
    ppermute x7, waiting for transfers between devices, paired(): return lax.ppermute(value, ('role', 'group'), pairs)  1.48 us
  transfers between devices with their start and end apart: 11, of which 6 were waited for; matrix products, arithmetic and copies ran while one was open for 0% of the time, Pallas kernels for 25%

profile of v6, /device:TPU:0, one launch (start us, length us, event | category | flops | bytes accessed | tf_op | source)
XLA Modules:
  0.0 26.6 jit_solution(13398249758668186018)
XLA Ops:
  0.0 0.9 %fusion.qa = bf16[8,2176]{1,0:T(8,128)(2,1)S(1)} fusion(s32[1,8]{1,0:T(1,128)} %lengths_hbm.1, s32[8,8]{1,0:T(8,128)} %bitcast.12, bf16[8,2048]{1,0:T(8,128)(2,1)} %bitcast.11), kind=kLoop, calls=%fused_computation.1 | loop fusion | flops 156672 | bytes 67872 | tf_op jit(solution)/shard_map/add | solution.py:349
  0.9 0.5 %collective-permute-start.1 = (bf16[8,2176]{1,0:T(8,128)(2,1)S(1)}, bf16[8,2176]{1,0:T(8,128)(2,1)S(1)}, u32[]{:S(2)}, u32[]{:S(2)}) collective-permute-start(bf16[8,2176]{1,0:T(8,128)(2,1)S(1)} %fusion.qa), channel_id=1, source_target_pairs={{16,4},{0,16},{20,0},{4,20},{24,12},{8,24},{28,8},{12,28},{17,5},{... | collective-permute-start | bytes 104456 | tf_op jit(solution)/shard_map/ppermute | solution.py:353
  1.3 2.7 %collective-permute-start = (bf16[8,2176]{1,0:T(8,128)(2,1)S(1)}, bf16[8,2176]{1,0:T(8,128)(2,1)S(1)}, u32[]{:S(2)}, u32[]{:S(2)}) collective-permute-start(bf16[8,2176]{1,0:T(8,128)(2,1)S(1)} %fusion.qa), channel_id=1, source_target_pairs={{16,8},{0,16},{20,12},{4,20},{24,0},{8,24},{28,4},{12,28},{17,9},{... | collective-permute-start | bytes 104456 | tf_op jit(solution)/shard_map/ppermute | solution.py:353
  4.0 1.1 %collective-permute-start.2 = (bf16[8,2176]{1,0:T(8,128)(2,1)S(1)}, bf16[8,2176]{1,0:T(8,128)(2,1)S(1)}, u32[]{:S(2)}, u32[]{:S(2)}) collective-permute-start(bf16[8,2176]{1,0:T(8,128)(2,1)S(1)} %fusion.qa), channel_id=1, source_target_pairs={{16,12},{0,16},{20,8},{4,20},{24,4},{8,24},{28,0},{12,28},{17,13},... | collective-permute-start | bytes 104456 | tf_op jit(solution)/shard_map/ppermute | solution.py:353
  5.1 3.5 %resident.1 = (bf16[144,128]{1,0:T(8,128)(2,1)S(1)}, bf16[64,128,512]{2,1,0:T(8,128)(2,1)S(1)}, f32[24,128]{1,0:T(8,128)S(1)}, f32[72,128]{1,0:T(8,128)S(1)}) custom-call(bf16[8,2176]{1,0:T(8,128)(2,1)S(1)} %fusion.qa, s32[3,4,12]{2,1,0:T(4,128)} %bitcast.14, s32[4,6]{1,0:T(4,128)} %wanted_hbm.1, s32[8,8]{1,0:T(8,128)} %bitcast.13, s32[1,8]{1,0:T(1,128)} %lengths_hbm.1, ...), custom_call_target="tpu_custom_call" | custom-call | tf_op jit(solution)/shard_map/resident/pallas_call | solution.py:366
  8.6 1.2 %owned.2 = (bf16[144,128]{1,0:T(8,128)(2,1)S(1)}, bf16[144,128]{1,0:T(8,128)(2,1)S(1)}) custom-call(bf16[64,128,512]{2,1,0:T(8,128)(2,1)S(1)} %get-tuple-element.21.chosen.pages, f32[24,128]{1,0:T(8,128)S(1)} %get-tuple-element.22.entries, bf16[8,2176]{1,0:T(8,128)(2,1)S(1)} %collective-permute-done.refs_0_, bf16[8,2176]{1,0:T(8,128)(2,1)S(1)} %collective-permute-done.1.refs_1_), custom_call_target="tpu_custom_call" | custom-call | flops 20000000000 | bytes 8388608 | tf_op jit(solution)/shard_map/owned/pallas_call | solution.py:390
  9.9 0.6 %owned.3 = bf16[144,128]{1,0:T(8,128)(2,1)S(1)} custom-call(bf16[64,128,512]{2,1,0:T(8,128)(2,1)S(1)} %get-tuple-element.21.chosen.pages, f32[24,128]{1,0:T(8,128)S(1)} %get-tuple-element.22.entries, bf16[8,2176]{1,0:T(8,128)(2,1)S(1)} %collective-permute-done.2.refs_0_, bf16[144,128]{1,0:T(8,128)(2,1)S(1)} %get-tuple-element.31.refs_1_, ...), custom_call_target="tpu_custom_call" | custom-call | flops 20000000000 | bytes 8388608 | tf_op jit(solution)/shard_map/owned/pallas_call | solution.py:390
  10.6 0.8 %collective-permute-start.3 = (bf16[144,128]{1,0:T(8,128)(2,1)S(1)}, bf16[144,128]{1,0:T(8,128)(2,1)S(1)}, u32[]{:S(2)}, u32[]{:S(2)}) collective-permute-start(bf16[144,128]{1,0:T(8,128)(2,1)S(1)} %owned.3), channel_id=1, source_target_pairs={{0,28},{16,0},{4,24},{20,4},{8,20},{24,8},{12,16},{28,12},{1,29},{... | collective-permute-start | bytes 110600 | tf_op jit(solution)/shard_map/ppermute | solution.py:353
  11.4 0.9 %collective-permute-start.4 = (bf16[144,128]{1,0:T(8,128)(2,1)S(1)}, bf16[144,128]{1,0:T(8,128)(2,1)S(1)}, u32[]{:S(2)}, u32[]{:S(2)}) collective-permute-start(bf16[144,128]{1,0:T(8,128)(2,1)S(1)} %get-tuple-element.30.refs_2_), channel_id=1, source_target_pairs={{0,24},{16,0},{4,28},{20,4},{8,16},{24,8},{12,20},{28,12},{1,25},{... | collective-permute-start | bytes 110600 | tf_op jit(solution)/shard_map/ppermute | solution.py:353
  12.4 0.4 %collective-permute-start.6 = (bf16[144,128]{1,0:T(8,128)(2,1)S(1)}, bf16[144,128]{1,0:T(8,128)(2,1)S(1)}, u32[]{:S(2)}, u32[]{:S(2)}) collective-permute-start(bf16[144,128]{1,0:T(8,128)(2,1)S(1)} %get-tuple-element.32), channel_id=1, source_target_pairs={{0,16},{16,0},{4,20},{20,4},{8,24},{24,8},{12,28},{28,12},{1,17},{... | collective-permute-start | bytes 110600 | tf_op jit(solution)/shard_map/ppermute | solution.py:353
  13.0 0.9 %collective-permute-done.4.refs_3_ = bf16[144,128]{1,0:T(8,128)(2,1)S(1)} collective-permute-done((bf16[144,128]{1,0:T(8,128)(2,1)S(1)}, bf16[144,128]{1,0:T(8,128)(2,1)S(1)}, u32[]{:S(2)}, u32[]{:S(2)}) %collective-permute-start.4) | collective-permute-done | bytes 36896 | tf_op jit(solution)/shard_map/ppermute | solution.py:353
  13.9 0.3 %collective-permute-done.5.refs_4_ = bf16[144,128]{1,0:T(8,128)(2,1)S(1)} collective-permute-done((bf16[144,128]{1,0:T(8,128)(2,1)S(1)}, bf16[144,128]{1,0:T(8,128)(2,1)S(1)}, u32[]{:S(2)}, u32[]{:S(2)}) %collective-permute-start.5) | collective-permute-done | bytes 36896 | tf_op jit(solution)/shard_map/ppermute | solution.py:353
  14.2 0.3 %merge.1.attended = bf16[8,2048]{1,0:T(8,128)(2,1)S(1)} custom-call(f32[144,128]{1,0:T(8,128)S(1)} %get-tuple-element.27.refs_0_, f32[144,128]{1,0:T(8,128)S(1)} %get-tuple-element.28.refs_1_, bf16[144,128]{1,0:T(8,128)(2,1)S(1)} %collective-permute-done.3.refs_2_, bf16[144,128]{1,0:T(8,128)(2,1)S(1)} %collective-permute-done.4.refs_3_, ...), custom_call_target="tpu_custom_call" | custom-call | tf_op jit(solution)/shard_map/merge/pallas_call | solution.py:409
  14.6 1.9 %collective-permute-start.7 = (bf16[8,2048]{1,0:T(8,128)(2,1)S(1)}, bf16[8,2048]{1,0:T(8,128)(2,1)S(1)}, u32[]{:S(2)}, u32[]{:S(2)}) collective-permute-start(bf16[8,2048]{1,0:T(8,128)(2,1)S(1)} %merge.1.attended), channel_id=1, source_target_pairs={{0,16},{16,0},{1,17},{17,1},{2,18},{18,2},{3,19},{19,3},{4,20},{20... | collective-permute-start | bytes 98312 | tf_op jit(solution)/shard_map/ppermute | solution.py:417
  16.5 0.9 %collective-permute-done.7.partner = bf16[8,2048]{1,0:T(8,128)(2,1)S(1)} collective-permute-done((bf16[8,2048]{1,0:T(8,128)(2,1)S(1)}, bf16[8,2048]{1,0:T(8,128)(2,1)S(1)}, u32[]{:S(2)}, u32[]{:S(2)}) %collective-permute-start.7) | collective-permute-done | bytes 32800 | tf_op jit(solution)/shard_map/ppermute | solution.py:417
  17.4 0.7 %project_far.1.refs_0_ = bf16[8,1024]{1,0:T(8,128)(2,1)S(1)} custom-call(bf16[8,2048]{1,0:T(8,128)(2,1)S(1)} %merge.1.attended, bf16[8,2048]{1,0:T(8,128)(2,1)S(1)} %collective-permute-done.7.partner, bf16[2048,4096]{1,0:T(8,128)(2,1)S(1)} %bitcast.8), custom_call_target="tpu_custom_call" | custom-call | flops 67108864 | bytes 4194304 | tf_op jit(solution)/shard_map/project_far/pallas_call | solution.py:421
  18.0 2.5 %collective-permute-start.8 = (bf16[8,1024]{1,0:T(8,128)(2,1)S(1)}, bf16[8,1024]{1,0:T(8,128)(2,1)S(1)}, u32[]{:S(2)}, u32[]{:S(2)}) collective-permute-start(bf16[8,1024]{1,0:T(8,128)(2,1)S(1)} %project_far.1.refs_0_), channel_id=1, source_target_pairs={{0,3},{1,2},{2,1},{3,0},{4,7},{5,6},{6,5},{7,4},{8,11},{9,10},{10,... | collective-permute-start | bytes 49160 | tf_op jit(solution)/shard_map/ppermute | solution.py:436
  20.5 1.2 %project_near.1 = (bf16[8,1024]{1,0:T(8,128)(2,1)S(1)}, bf16[8,1024]{1,0:T(8,128)(2,1)S(1)}) custom-call(bf16[8,2048]{1,0:T(8,128)(2,1)S(1)} %merge.1.attended, bf16[8,2048]{1,0:T(8,128)(2,1)S(1)} %collective-permute-done.7.partner, bf16[2048,4096]{1,0:T(8,128)(2,1)S(1)} %bitcast.8, bf16[8,1024]{1,0:T(8,128)(2,1)S(1)} %project_far.1.refs_0_), custom_call_target="tpu_custom_call" | custom-call | flops 134217728 | bytes 8388608 | tf_op jit(solution)/shard_map/project_near/pallas_call | solution.py:421
  21.7 0.6 %collective-permute-start.9 = (bf16[8,1024]{1,0:T(8,128)(2,1)S(1)}, bf16[8,1024]{1,0:T(8,128)(2,1)S(1)}, u32[]{:S(2)}, u32[]{:S(2)}) collective-permute-start(bf16[8,1024]{1,0:T(8,128)(2,1)S(1)} %get-tuple-element.33), channel_id=1, source_target_pairs={{0,1},{1,0},{2,3},{3,2},{4,5},{5,4},{6,7},{7,6},{8,9},{9,8},{10,11... | collective-permute-start | bytes 49160 | tf_op jit(solution)/shard_map/ppermute | solution.py:436
  22.2 0.5 %collective-permute-start.10 = (bf16[8,1024]{1,0:T(8,128)(2,1)S(1)}, bf16[8,1024]{1,0:T(8,128)(2,1)S(1)}, u32[]{:S(2)}, u32[]{:S(2)}) collective-permute-start(bf16[8,1024]{1,0:T(8,128)(2,1)S(1)} %get-tuple-element.34), channel_id=1, source_target_pairs={{0,2},{1,3},{2,0},{3,1},{4,6},{5,7},{6,4},{7,5},{8,10},{9,11},{10,... | collective-permute-start | bytes 49160 | tf_op jit(solution)/shard_map/ppermute | solution.py:436
  22.7 0.6 %project_own.1 = f32[8,1024]{1,0:T(8,128)S(1)} custom-call(bf16[8,2048]{1,0:T(8,128)(2,1)S(1)} %merge.1.attended, bf16[8,2048]{1,0:T(8,128)(2,1)S(1)} %collective-permute-done.7.partner, bf16[2048,4096]{1,0:T(8,128)(2,1)S(1)} %bitcast.8), custom_call_target="tpu_custom_call" | custom-call | flops 67108864 | bytes 4194304 | tf_op jit(solution)/shard_map/project_own/pallas_call | solution.py:421
  23.4 2.0 %collective-permute-done.9 = bf16[8,1024]{1,0:T(8,128)(2,1)S(1)} collective-permute-done((bf16[8,1024]{1,0:T(8,128)(2,1)S(1)}, bf16[8,1024]{1,0:T(8,128)(2,1)S(1)}, u32[]{:S(2)}, u32[]{:S(2)}) %collective-permute-start.9) | collective-permute-done | bytes 16416 | tf_op jit(solution)/shard_map/ppermute | solution.py:436
  25.4 0.5 %collective-permute-done.10 = bf16[8,1024]{1,0:T(8,128)(2,1)S(1)} collective-permute-done((bf16[8,1024]{1,0:T(8,128)(2,1)S(1)}, bf16[8,1024]{1,0:T(8,128)(2,1)S(1)}, u32[]{:S(2)}, u32[]{:S(2)}) %collective-permute-start.10) | collective-permute-done | bytes 16416 | tf_op jit(solution)/shard_map/ppermute | solution.py:436
  26.0 0.6 %fusion.1 = bf16[1,8,1024]{2,1,0:T(8,128)(2,1)} fusion(bf16[8,1024]{1,0:T(8,128)(2,1)S(1)} %collective-permute-done.10, bf16[8,1024]{1,0:T(8,128)(2,1)S(1)} %collective-permute-done.9, f32[8,1024]{1,0:T(8,128)S(1)} %project_own.1, bf16[8,1024]{1,0:T(8,128)(2,1)S(1)} %collective-permute-done.8), kind=kLoop, calls=%fused_computation.3 | loop fusion | flops 57344 | bytes 98304 | tf_op jit(solution)/shard_map/broadcast_in_dim | solution.py:439
  (19 shorter events, 0.4 us)
Async XLA Ops:
  0.9 7.7 %collective-permute-start.1 = (bf16[8,2176]{1,0:T(8,128)(2,1)S(1)}, bf16[8,2176]{1,0:T(8,128)(2,1)S(1)}, u32[]{:S(2)}, u32[]{:S(2)}) collective-permute-start(bf16[8,2176]{1,0:T(8,128)(2,1)S(1)} %fusion.qa), channel_id=1, source_target_pairs={{16,4},{0,16},{20,0},{4,20},{24,12},{8,24},{28,8},{12,28},{17,5},{... | collective-permute-start | bytes 104456 | tf_op jit(solution)/shard_map/ppermute | solution.py:353
  1.3 7.3 %collective-permute-start = (bf16[8,2176]{1,0:T(8,128)(2,1)S(1)}, bf16[8,2176]{1,0:T(8,128)(2,1)S(1)}, u32[]{:S(2)}, u32[]{:S(2)}) collective-permute-start(bf16[8,2176]{1,0:T(8,128)(2,1)S(1)} %fusion.qa), channel_id=1, source_target_pairs={{16,8},{0,16},{20,12},{4,20},{24,0},{8,24},{28,4},{12,28},{17,9},{... | collective-permute-start | bytes 104456 | tf_op jit(solution)/shard_map/ppermute | solution.py:353
  4.0 5.8 %collective-permute-start.2 = (bf16[8,2176]{1,0:T(8,128)(2,1)S(1)}, bf16[8,2176]{1,0:T(8,128)(2,1)S(1)}, u32[]{:S(2)}, u32[]{:S(2)}) collective-permute-start(bf16[8,2176]{1,0:T(8,128)(2,1)S(1)} %fusion.qa), channel_id=1, source_target_pairs={{16,12},{0,16},{20,8},{4,20},{24,4},{8,24},{28,0},{12,28},{17,13},... | collective-permute-start | bytes 104456 | tf_op jit(solution)/shard_map/ppermute | solution.py:353
  9.9 7.5 %slice-start = ((s8[16777216]{0:T(1024)(128)(4,1)}), s8[4194304]{0:T(1024)(128)(4,1)S(1)}, s32[]{:S(2)}) async-start(s8[16777216]{0:T(1024)(128)(4,1)} %bitcast.7), calls=%async_computation | async-start | bytes 8388608
  9.9 2.9 %copy-start = (bf16[1,8,512]{2,1,0:T(8,128)(2,1)S(1)}, bf16[1,8,512]{2,1,0:T(8,128)(2,1)}, u32[]{:S(2)}) copy-start(bf16[1,8,512]{2,1,0:T(8,128)(2,1)} %param.14) | copy-start | bytes 24580
  9.9 7.5 %slice-start.1 = ((s8[16777216]{0:T(1024)(128)(4,1)}), s8[4194304]{0:T(1024)(128)(4,1)S(1)}, s32[]{:S(2)}) async-start(s8[16777216]{0:T(1024)(128)(4,1)} %bitcast.7), calls=%async_computation.1 | async-start | bytes 8388608
  9.9 7.5 %slice-start.2 = ((s8[16777216]{0:T(1024)(128)(4,1)}), s8[4194304]{0:T(1024)(128)(4,1)S(1)}, s32[]{:S(2)}) async-start(s8[16777216]{0:T(1024)(128)(4,1)} %bitcast.7), calls=%async_computation.2 | async-start | bytes 8388608
  9.9 7.5 %slice-start.3 = ((s8[16777216]{0:T(1024)(128)(4,1)}), s8[4194304]{0:T(1024)(128)(4,1)S(1)}, s32[]{:S(2)}) async-start(s8[16777216]{0:T(1024)(128)(4,1)} %bitcast.7), calls=%async_computation.3 | async-start | bytes 8388608
  10.6 2.5 %collective-permute-start.3 = (bf16[144,128]{1,0:T(8,128)(2,1)S(1)}, bf16[144,128]{1,0:T(8,128)(2,1)S(1)}, u32[]{:S(2)}, u32[]{:S(2)}) collective-permute-start(bf16[144,128]{1,0:T(8,128)(2,1)S(1)} %owned.3), channel_id=1, source_target_pairs={{0,28},{16,0},{4,24},{20,4},{8,20},{24,8},{12,16},{28,12},{1,29},{... | collective-permute-start | bytes 110600 | tf_op jit(solution)/shard_map/ppermute | solution.py:353
  11.4 2.5 %collective-permute-start.4 = (bf16[144,128]{1,0:T(8,128)(2,1)S(1)}, bf16[144,128]{1,0:T(8,128)(2,1)S(1)}, u32[]{:S(2)}, u32[]{:S(2)}) collective-permute-start(bf16[144,128]{1,0:T(8,128)(2,1)S(1)} %get-tuple-element.30.refs_2_), channel_id=1, source_target_pairs={{0,24},{16,0},{4,28},{20,4},{8,16},{24,8},{12,20},{28,12},{1,25},{... | collective-permute-start | bytes 110600 | tf_op jit(solution)/shard_map/ppermute | solution.py:353
  12.3 2.0 %collective-permute-start.5 = (bf16[144,128]{1,0:T(8,128)(2,1)S(1)}, bf16[144,128]{1,0:T(8,128)(2,1)S(1)}, u32[]{:S(2)}, u32[]{:S(2)}) collective-permute-start(bf16[144,128]{1,0:T(8,128)(2,1)S(1)} %get-tuple-element.31.refs_1_), channel_id=1, source_target_pairs={{0,20},{16,0},{4,16},{20,4},{8,28},{24,8},{12,24},{28,12},{1,21},{... | collective-permute-start | bytes 110600 | tf_op jit(solution)/shard_map/ppermute | solution.py:353
  12.4 1.9 %collective-permute-start.6 = (bf16[144,128]{1,0:T(8,128)(2,1)S(1)}, bf16[144,128]{1,0:T(8,128)(2,1)S(1)}, u32[]{:S(2)}, u32[]{:S(2)}) collective-permute-start(bf16[144,128]{1,0:T(8,128)(2,1)S(1)} %get-tuple-element.32), channel_id=1, source_target_pairs={{0,16},{16,0},{4,20},{20,4},{8,24},{24,8},{12,28},{28,12},{1,17},{... | collective-permute-start | bytes 110600 | tf_op jit(solution)/shard_map/ppermute | solution.py:353
  14.6 2.8 %collective-permute-start.7 = (bf16[8,2048]{1,0:T(8,128)(2,1)S(1)}, bf16[8,2048]{1,0:T(8,128)(2,1)S(1)}, u32[]{:S(2)}, u32[]{:S(2)}) collective-permute-start(bf16[8,2048]{1,0:T(8,128)(2,1)S(1)} %merge.1.attended), channel_id=1, source_target_pairs={{0,16},{16,0},{1,17},{17,1},{2,18},{18,2},{3,19},{19,3},{4,20},{20... | collective-permute-start | bytes 98312 | tf_op jit(solution)/shard_map/ppermute | solution.py:417
  18.0 5.4 %collective-permute-start.8 = (bf16[8,1024]{1,0:T(8,128)(2,1)S(1)}, bf16[8,1024]{1,0:T(8,128)(2,1)S(1)}, u32[]{:S(2)}, u32[]{:S(2)}) collective-permute-start(bf16[8,1024]{1,0:T(8,128)(2,1)S(1)} %project_far.1.refs_0_), channel_id=1, source_target_pairs={{0,3},{1,2},{2,1},{3,0},{4,7},{5,6},{6,5},{7,4},{8,11},{9,10},{10,... | collective-permute-start | bytes 49160 | tf_op jit(solution)/shard_map/ppermute | solution.py:436
  21.7 3.8 %collective-permute-start.9 = (bf16[8,1024]{1,0:T(8,128)(2,1)S(1)}, bf16[8,1024]{1,0:T(8,128)(2,1)S(1)}, u32[]{:S(2)}, u32[]{:S(2)}) collective-permute-start(bf16[8,1024]{1,0:T(8,128)(2,1)S(1)} %get-tuple-element.33), channel_id=1, source_target_pairs={{0,1},{1,0},{2,3},{3,2},{4,5},{5,4},{6,7},{7,6},{8,9},{9,8},{10,11... | collective-permute-start | bytes 49160 | tf_op jit(solution)/shard_map/ppermute | solution.py:436
  22.2 3.7 %collective-permute-start.10 = (bf16[8,1024]{1,0:T(8,128)(2,1)S(1)}, bf16[8,1024]{1,0:T(8,128)(2,1)S(1)}, u32[]{:S(2)}, u32[]{:S(2)}) collective-permute-start(bf16[8,1024]{1,0:T(8,128)(2,1)S(1)} %get-tuple-element.34), channel_id=1, source_target_pairs={{0,2},{1,3},{2,0},{3,1},{4,6},{5,7},{6,4},{7,5},{8,10},{9,11},{10,... | collective-permute-start | bytes 49160 | tf_op jit(solution)/shard_map/ppermute | solution.py:436

commit v7 on v5

--- a/solution.py
+++ b/solution.py
@@ -248,22 +248,36 @@
     @pl.when(prefill)
     def _():
         lists_ready()
-        copies = []
+
+        def page_copy(at):
+            return pltpu.make_async_copy(kv.at[page_list[at]], chosen.at[at], sems.at[at])
+
+        def arrive(first, last):
+            for at in range(first, last):
+
+                @pl.when(slot_list[at] >= 0)
+                def _(at=at):
+                    page_copy(at).wait()
+
         for k in range(groups):
             target = lax.bitwise_xor(group, k)
             list_pages(send, wanted, group, target, kv.shape[0], page_list, slot_list, k * PARTS)
             for c in range(PARTS):
                 at = k * PARTS + c
-                copy = pltpu.make_async_copy(kv.at[page_list[at]], chosen.at[at], sems.at[at])
-                copy.start()
-                copies.append(copy)
-                entry = slot_list[at].astype(jnp.float32)
-                entries[at : at + 1, :] = jnp.full((1, LANES), entry, jnp.float32)
-        for copy in copies[:PARTS]:
-            copy.wait()
+                entry = slot_list[at]
+                entries[at : at + 1, :] = jnp.full((1, LANES), entry.astype(jnp.float32), jnp.float32)
+
+                @pl.when(entry >= 0)
+                def _(at=at):
+                    page_copy(at).start()
+
+                @pl.when(entry < 0)
+                def _(at=at):
+                    chosen[at] = jnp.zeros(chosen.shape[1:], chosen.dtype)
+
+        arrive(0, PARTS)
         owner_part(qa, chosen.at[pl.ds(0, PARTS)], entries[:PARTS, :], sent, held, per_held, maxp)
-        for copy in copies[PARTS:]:
-            copy.wait()
+        arrive(PARTS, groups * PARTS)
 
     @pl.when(jnp.logical_not(prefill))
     def _():

time: 26.6 us -> 26.8 us (level)
  no operation moved by 1% of the time
where the time goes in v7:
time: 26.8 us; the launch traced here: 26.4 us
  starting transfers between devices  11.8 us (44%)
  Pallas kernels  8.03 us (30%)
  waiting for transfers between devices  4.92 us (18%)
  other arithmetic  1.5 us (6%)
    ppermute x7, starting transfers between devices, paired(): return lax.ppermute(value, ('role', 'group'), pairs)  6.22 us
    ppermute x3, starting transfers between devices, per_device(): lax.ppermute(part, 'tp', [(i, i ^ d) for i in range(tps)])  3.5 us
    pallas_call x1, Pallas kernels, per_device(): pl.pallas_call(functools.partial(first_kernel, held, per_held, groups, ma...  3.48 us
    ppermute x3, waiting for transfers between devices, per_device(): lax.ppermute(part, 'tp', [(i, i ^ d) for i in range(tps)])  2.59 us
    pallas_call x2, Pallas kernels, project(): pl.pallas_call(functools.partial(project_kernel, steps), out_shape=[jax.S...  2.38 us
    ppermute x1, starting transfers between devices, per_device(): partner = lax.ppermute(attended, 'role', [(0, 1), (1, 0)])  2.11 us
    pallas_call x2, Pallas kernels, per_device(): pl.pallas_call(functools.partial(second_kernel, held, per_held, maxp, fir...  1.84 us
    ppermute x7, waiting for transfers between devices, paired(): return lax.ppermute(value, ('role', 'group'), pairs)  1.48 us
  transfers between devices with their start and end apart: 11, of which 7 were waited for; matrix products, arithmetic and copies ran while one was open for 0% of the time, Pallas kernels for 20%

profile of v7, /device:TPU:0, one launch (start us, length us, event | category | flops | bytes accessed | tf_op | source)
XLA Modules:
  0.0 26.4 jit_solution(17039498388954899913)
XLA Ops:
  0.0 0.9 %fusion.qa = bf16[8,2176]{1,0:T(8,128)(2,1)S(1)} fusion(s32[1,8]{1,0:T(1,128)} %lengths_hbm.1, s32[8,8]{1,0:T(8,128)} %bitcast.12, bf16[8,2048]{1,0:T(8,128)(2,1)} %bitcast.11), kind=kLoop, calls=%fused_computation.1 | loop fusion | flops 156672 | bytes 67872 | tf_op jit(solution)/shard_map/add | solution.py:362
  0.9 0.5 %collective-permute-start.1 = (bf16[8,2176]{1,0:T(8,128)(2,1)S(1)}, bf16[8,2176]{1,0:T(8,128)(2,1)S(1)}, u32[]{:S(2)}, u32[]{:S(2)}) collective-permute-start(bf16[8,2176]{1,0:T(8,128)(2,1)S(1)} %fusion.qa), channel_id=1, source_target_pairs={{16,4},{0,16},{20,0},{4,20},{24,12},{8,24},{28,8},{12,28},{17,5},{... | collective-permute-start | bytes 104456 | tf_op jit(solution)/shard_map/ppermute | solution.py:366
  1.3 2.7 %collective-permute-start = (bf16[8,2176]{1,0:T(8,128)(2,1)S(1)}, bf16[8,2176]{1,0:T(8,128)(2,1)S(1)}, u32[]{:S(2)}, u32[]{:S(2)}) collective-permute-start(bf16[8,2176]{1,0:T(8,128)(2,1)S(1)} %fusion.qa), channel_id=1, source_target_pairs={{16,8},{0,16},{20,12},{4,20},{24,0},{8,24},{28,4},{12,28},{17,9},{... | collective-permute-start | bytes 104456 | tf_op jit(solution)/shard_map/ppermute | solution.py:366
  4.0 1.1 %collective-permute-start.2 = (bf16[8,2176]{1,0:T(8,128)(2,1)S(1)}, bf16[8,2176]{1,0:T(8,128)(2,1)S(1)}, u32[]{:S(2)}, u32[]{:S(2)}) collective-permute-start(bf16[8,2176]{1,0:T(8,128)(2,1)S(1)} %fusion.qa), channel_id=1, source_target_pairs={{16,12},{0,16},{20,8},{4,20},{24,4},{8,24},{28,0},{12,28},{17,13},... | collective-permute-start | bytes 104456 | tf_op jit(solution)/shard_map/ppermute | solution.py:366
  5.1 3.5 %resident.1 = (bf16[144,128]{1,0:T(8,128)(2,1)S(1)}, bf16[64,128,512]{2,1,0:T(8,128)(2,1)S(1)}, f32[24,128]{1,0:T(8,128)S(1)}, f32[72,128]{1,0:T(8,128)S(1)}) custom-call(bf16[8,2176]{1,0:T(8,128)(2,1)S(1)} %fusion.qa, s32[3,4,12]{2,1,0:T(4,128)} %bitcast.14, s32[4,6]{1,0:T(4,128)} %wanted_hbm.1, s32[8,8]{1,0:T(8,128)} %bitcast.13, s32[1,8]{1,0:T(1,128)} %lengths_hbm.1, ...), custom_call_target="tpu_custom_call" | custom-call | tf_op jit(solution)/shard_map/resident/pallas_call | solution.py:379
  8.6 1.2 %owned.2 = (bf16[144,128]{1,0:T(8,128)(2,1)S(1)}, bf16[144,128]{1,0:T(8,128)(2,1)S(1)}) custom-call(bf16[64,128,512]{2,1,0:T(8,128)(2,1)S(1)} %get-tuple-element.22.chosen.pages, f32[24,128]{1,0:T(8,128)S(1)} %get-tuple-element.23.entries, bf16[8,2176]{1,0:T(8,128)(2,1)S(1)} %collective-permute-done.refs_0_, bf16[8,2176]{1,0:T(8,128)(2,1)S(1)} %collective-permute-done.1.refs_1_), custom_call_target="tpu_custom_call" | custom-call | flops 20000000000 | bytes 8388608 | tf_op jit(solution)/shard_map/owned/pallas_call | solution.py:403
  9.9 0.6 %owned.3 = bf16[144,128]{1,0:T(8,128)(2,1)S(1)} custom-call(bf16[64,128,512]{2,1,0:T(8,128)(2,1)S(1)} %get-tuple-element.22.chosen.pages, f32[24,128]{1,0:T(8,128)S(1)} %get-tuple-element.23.entries, bf16[8,2176]{1,0:T(8,128)(2,1)S(1)} %collective-permute-done.2.refs_0_, bf16[144,128]{1,0:T(8,128)(2,1)S(1)} %get-tuple-element.32.refs_1_, ...), custom_call_target="tpu_custom_call" | custom-call | flops 20000000000 | bytes 8388608 | tf_op jit(solution)/shard_map/owned/pallas_call | solution.py:403
  10.5 0.8 %collective-permute-start.3 = (bf16[144,128]{1,0:T(8,128)(2,1)S(1)}, bf16[144,128]{1,0:T(8,128)(2,1)S(1)}, u32[]{:S(2)}, u32[]{:S(2)}) collective-permute-start(bf16[144,128]{1,0:T(8,128)(2,1)S(1)} %owned.3), channel_id=1, source_target_pairs={{0,28},{16,0},{4,24},{20,4},{8,20},{24,8},{12,16},{28,12},{1,29},{... | collective-permute-start | bytes 110600 | tf_op jit(solution)/shard_map/ppermute | solution.py:366
  11.4 0.7 %collective-permute-start.4 = (bf16[144,128]{1,0:T(8,128)(2,1)S(1)}, bf16[144,128]{1,0:T(8,128)(2,1)S(1)}, u32[]{:S(2)}, u32[]{:S(2)}) collective-permute-start(bf16[144,128]{1,0:T(8,128)(2,1)S(1)} %get-tuple-element.31.refs_2_), channel_id=1, source_target_pairs={{0,24},{16,0},{4,28},{20,4},{8,16},{24,8},{12,20},{28,12},{1,25},{... | collective-permute-start | bytes 110600 | tf_op jit(solution)/shard_map/ppermute | solution.py:366
  12.5 0.5 %collective-permute-done.3.refs_2_ = bf16[144,128]{1,0:T(8,128)(2,1)S(1)} collective-permute-done((bf16[144,128]{1,0:T(8,128)(2,1)S(1)}, bf16[144,128]{1,0:T(8,128)(2,1)S(1)}, u32[]{:S(2)}, u32[]{:S(2)}) %collective-permute-start.3) | collective-permute-done | bytes 36896 | tf_op jit(solution)/shard_map/ppermute | solution.py:366
  13.0 0.7 %collective-permute-done.4.refs_3_ = bf16[144,128]{1,0:T(8,128)(2,1)S(1)} collective-permute-done((bf16[144,128]{1,0:T(8,128)(2,1)S(1)}, bf16[144,128]{1,0:T(8,128)(2,1)S(1)}, u32[]{:S(2)}, u32[]{:S(2)}) %collective-permute-start.4) | collective-permute-done | bytes 36896 | tf_op jit(solution)/shard_map/ppermute | solution.py:366
  13.7 0.3 %collective-permute-done.5.refs_4_ = bf16[144,128]{1,0:T(8,128)(2,1)S(1)} collective-permute-done((bf16[144,128]{1,0:T(8,128)(2,1)S(1)}, bf16[144,128]{1,0:T(8,128)(2,1)S(1)}, u32[]{:S(2)}, u32[]{:S(2)}) %collective-permute-start.5) | collective-permute-done | bytes 36896 | tf_op jit(solution)/shard_map/ppermute | solution.py:366
  14.0 0.3 %merge.1.attended = bf16[8,2048]{1,0:T(8,128)(2,1)S(1)} custom-call(f32[144,128]{1,0:T(8,128)S(1)} %get-tuple-element.28.refs_0_, f32[144,128]{1,0:T(8,128)S(1)} %get-tuple-element.29.refs_1_, bf16[144,128]{1,0:T(8,128)(2,1)S(1)} %collective-permute-done.3.refs_2_, bf16[144,128]{1,0:T(8,128)(2,1)S(1)} %collective-permute-done.4.refs_3_, ...), custom_call_target="tpu_custom_call" | custom-call | tf_op jit(solution)/shard_map/merge/pallas_call | solution.py:422
  14.4 2.1 %collective-permute-start.7 = (bf16[8,2048]{1,0:T(8,128)(2,1)S(1)}, bf16[8,2048]{1,0:T(8,128)(2,1)S(1)}, u32[]{:S(2)}, u32[]{:S(2)}) collective-permute-start(bf16[8,2048]{1,0:T(8,128)(2,1)S(1)} %merge.1.attended), channel_id=1, source_target_pairs={{0,16},{16,0},{1,17},{17,1},{2,18},{18,2},{3,19},{19,3},{4,20},{20... | collective-permute-start | bytes 98312 | tf_op jit(solution)/shard_map/ppermute | solution.py:430
  16.5 0.9 %collective-permute-done.7.partner = bf16[8,2048]{1,0:T(8,128)(2,1)S(1)} collective-permute-done((bf16[8,2048]{1,0:T(8,128)(2,1)S(1)}, bf16[8,2048]{1,0:T(8,128)(2,1)S(1)}, u32[]{:S(2)}, u32[]{:S(2)}) %collective-permute-start.7) | collective-permute-done | bytes 32800 | tf_op jit(solution)/shard_map/ppermute | solution.py:430
  17.3 1.7 %project.1 = (bf16[8,1024]{1,0:T(8,128)(2,1)S(1)}, bf16[8,1024]{1,0:T(8,128)(2,1)S(1)}, bf16[8,1024]{1,0:T(8,128)(2,1)S(1)}) custom-call(bf16[8,2048]{1,0:T(8,128)(2,1)S(1)} %merge.1.attended, bf16[8,2048]{1,0:T(8,128)(2,1)S(1)} %collective-permute-done.7.partner, bf16[2048,4096]{1,0:T(8,128)(2,1)S(1)} %bitcast.8), custom_call_target="tpu_custom_call" | custom-call | flops 201326592 | bytes 12582912 | tf_op jit(solution)/shard_map/project/pallas_call | solution.py:434
  19.1 2.5 %collective-permute-start.8 = (bf16[8,1024]{1,0:T(8,128)(2,1)S(1)}, bf16[8,1024]{1,0:T(8,128)(2,1)S(1)}, u32[]{:S(2)}, u32[]{:S(2)}) collective-permute-start(bf16[8,1024]{1,0:T(8,128)(2,1)S(1)} %get-tuple-element.34), channel_id=1, source_target_pairs={{0,3},{1,2},{2,1},{3,0},{4,7},{5,6},{6,5},{7,4},{8,11},{9,10},{10,... | collective-permute-start | bytes 49160 | tf_op jit(solution)/shard_map/ppermute | solution.py:448
  21.5 0.5 %collective-permute-start.9 = (bf16[8,1024]{1,0:T(8,128)(2,1)S(1)}, bf16[8,1024]{1,0:T(8,128)(2,1)S(1)}, u32[]{:S(2)}, u32[]{:S(2)}) collective-permute-start(bf16[8,1024]{1,0:T(8,128)(2,1)S(1)} %get-tuple-element.35), channel_id=1, source_target_pairs={{0,1},{1,0},{2,3},{3,2},{4,5},{5,4},{6,7},{7,6},{8,9},{9,8},{10,11... | collective-permute-start | bytes 49160 | tf_op jit(solution)/shard_map/ppermute | solution.py:448
  22.1 0.5 %collective-permute-start.10 = (bf16[8,1024]{1,0:T(8,128)(2,1)S(1)}, bf16[8,1024]{1,0:T(8,128)(2,1)S(1)}, u32[]{:S(2)}, u32[]{:S(2)}) collective-permute-start(bf16[8,1024]{1,0:T(8,128)(2,1)S(1)} %get-tuple-element.36), channel_id=1, source_target_pairs={{0,2},{1,3},{2,0},{3,1},{4,6},{5,7},{6,4},{7,5},{8,10},{9,11},{10,... | collective-permute-start | bytes 49160 | tf_op jit(solution)/shard_map/ppermute | solution.py:448
  22.6 0.6 %project_own.1 = f32[8,1024]{1,0:T(8,128)S(1)} custom-call(bf16[8,2048]{1,0:T(8,128)(2,1)S(1)} %merge.1.attended, bf16[8,2048]{1,0:T(8,128)(2,1)S(1)} %collective-permute-done.7.partner, bf16[2048,4096]{1,0:T(8,128)(2,1)S(1)} %bitcast.8), custom_call_target="tpu_custom_call" | custom-call | flops 67108864 | bytes 4194304 | tf_op jit(solution)/shard_map/project_own/pallas_call | solution.py:434
  23.2 0.5 %collective-permute-done.8 = bf16[8,1024]{1,0:T(8,128)(2,1)S(1)} collective-permute-done((bf16[8,1024]{1,0:T(8,128)(2,1)S(1)}, bf16[8,1024]{1,0:T(8,128)(2,1)S(1)}, u32[]{:S(2)}, u32[]{:S(2)}) %collective-permute-start.8) | collective-permute-done | bytes 16416 | tf_op jit(solution)/shard_map/ppermute | solution.py:448
  23.7 1.5 %collective-permute-done.9 = bf16[8,1024]{1,0:T(8,128)(2,1)S(1)} collective-permute-done((bf16[8,1024]{1,0:T(8,128)(2,1)S(1)}, bf16[8,1024]{1,0:T(8,128)(2,1)S(1)}, u32[]{:S(2)}, u32[]{:S(2)}) %collective-permute-start.9) | collective-permute-done | bytes 16416 | tf_op jit(solution)/shard_map/ppermute | solution.py:448
  25.3 0.5 %collective-permute-done.10 = bf16[8,1024]{1,0:T(8,128)(2,1)S(1)} collective-permute-done((bf16[8,1024]{1,0:T(8,128)(2,1)S(1)}, bf16[8,1024]{1,0:T(8,128)(2,1)S(1)}, u32[]{:S(2)}, u32[]{:S(2)}) %collective-permute-start.10) | collective-permute-done | bytes 16416 | tf_op jit(solution)/shard_map/ppermute | solution.py:448
  25.8 0.6 %fusion.1 = bf16[1,8,1024]{2,1,0:T(8,128)(2,1)} fusion(bf16[8,1024]{1,0:T(8,128)(2,1)S(1)} %collective-permute-done.10, bf16[8,1024]{1,0:T(8,128)(2,1)S(1)} %collective-permute-done.9, f32[8,1024]{1,0:T(8,128)S(1)} %project_own.1, bf16[8,1024]{1,0:T(8,128)(2,1)S(1)} %collective-permute-done.8), kind=kLoop, calls=%fused_computation.3 | loop fusion | flops 57344 | bytes 98304 | tf_op jit(solution)/shard_map/broadcast_in_dim | solution.py:451
  (18 shorter events, 0.5 us)
Async XLA Ops:
  0.9 7.7 %collective-permute-start.1 = (bf16[8,2176]{1,0:T(8,128)(2,1)S(1)}, bf16[8,2176]{1,0:T(8,128)(2,1)S(1)}, u32[]{:S(2)}, u32[]{:S(2)}) collective-permute-start(bf16[8,2176]{1,0:T(8,128)(2,1)S(1)} %fusion.qa), channel_id=1, source_target_pairs={{16,4},{0,16},{20,0},{4,20},{24,12},{8,24},{28,8},{12,28},{17,5},{... | collective-permute-start | bytes 104456 | tf_op jit(solution)/shard_map/ppermute | solution.py:366
  1.3 7.3 %collective-permute-start = (bf16[8,2176]{1,0:T(8,128)(2,1)S(1)}, bf16[8,2176]{1,0:T(8,128)(2,1)S(1)}, u32[]{:S(2)}, u32[]{:S(2)}) collective-permute-start(bf16[8,2176]{1,0:T(8,128)(2,1)S(1)} %fusion.qa), channel_id=1, source_target_pairs={{16,8},{0,16},{20,12},{4,20},{24,0},{8,24},{28,4},{12,28},{17,9},{... | collective-permute-start | bytes 104456 | tf_op jit(solution)/shard_map/ppermute | solution.py:366
  4.0 5.8 %collective-permute-start.2 = (bf16[8,2176]{1,0:T(8,128)(2,1)S(1)}, bf16[8,2176]{1,0:T(8,128)(2,1)S(1)}, u32[]{:S(2)}, u32[]{:S(2)}) collective-permute-start(bf16[8,2176]{1,0:T(8,128)(2,1)S(1)} %fusion.qa), channel_id=1, source_target_pairs={{16,12},{0,16},{20,8},{4,20},{24,4},{8,24},{28,0},{12,28},{17,13},... | collective-permute-start | bytes 104456 | tf_op jit(solution)/shard_map/ppermute | solution.py:366
  9.8 7.5 %slice-start = ((s8[16777216]{0:T(1024)(128)(4,1)}), s8[4194304]{0:T(1024)(128)(4,1)S(1)}, s32[]{:S(2)}) async-start(s8[16777216]{0:T(1024)(128)(4,1)} %bitcast.7), calls=%async_computation | async-start | bytes 8388608
  9.8 2.7 %copy-start = (bf16[1,8,512]{2,1,0:T(8,128)(2,1)S(1)}, bf16[1,8,512]{2,1,0:T(8,128)(2,1)}, u32[]{:S(2)}) copy-start(bf16[1,8,512]{2,1,0:T(8,128)(2,1)} %param.14) | copy-start | bytes 24580
  9.8 7.5 %slice-start.1 = ((s8[16777216]{0:T(1024)(128)(4,1)}), s8[4194304]{0:T(1024)(128)(4,1)S(1)}, s32[]{:S(2)}) async-start(s8[16777216]{0:T(1024)(128)(4,1)} %bitcast.7), calls=%async_computation.1 | async-start | bytes 8388608
  9.8 7.5 %slice-start.2 = ((s8[16777216]{0:T(1024)(128)(4,1)}), s8[4194304]{0:T(1024)(128)(4,1)S(1)}, s32[]{:S(2)}) async-start(s8[16777216]{0:T(1024)(128)(4,1)} %bitcast.7), calls=%async_computation.2 | async-start | bytes 8388608
  9.9 7.5 %slice-start.3 = ((s8[16777216]{0:T(1024)(128)(4,1)}), s8[4194304]{0:T(1024)(128)(4,1)S(1)}, s32[]{:S(2)}) async-start(s8[16777216]{0:T(1024)(128)(4,1)} %bitcast.7), calls=%async_computation.3 | async-start | bytes 8388608
  10.5 2.5 %collective-permute-start.3 = (bf16[144,128]{1,0:T(8,128)(2,1)S(1)}, bf16[144,128]{1,0:T(8,128)(2,1)S(1)}, u32[]{:S(2)}, u32[]{:S(2)}) collective-permute-start(bf16[144,128]{1,0:T(8,128)(2,1)S(1)} %owned.3), channel_id=1, source_target_pairs={{0,28},{16,0},{4,24},{20,4},{8,20},{24,8},{12,16},{28,12},{1,29},{... | collective-permute-start | bytes 110600 | tf_op jit(solution)/shard_map/ppermute | solution.py:366
  11.4 2.3 %collective-permute-start.4 = (bf16[144,128]{1,0:T(8,128)(2,1)S(1)}, bf16[144,128]{1,0:T(8,128)(2,1)S(1)}, u32[]{:S(2)}, u32[]{:S(2)}) collective-permute-start(bf16[144,128]{1,0:T(8,128)(2,1)S(1)} %get-tuple-element.31.refs_2_), channel_id=1, source_target_pairs={{0,24},{16,0},{4,28},{20,4},{8,16},{24,8},{12,20},{28,12},{1,25},{... | collective-permute-start | bytes 110600 | tf_op jit(solution)/shard_map/ppermute | solution.py:366
  12.0 2.0 %collective-permute-start.5 = (bf16[144,128]{1,0:T(8,128)(2,1)S(1)}, bf16[144,128]{1,0:T(8,128)(2,1)S(1)}, u32[]{:S(2)}, u32[]{:S(2)}) collective-permute-start(bf16[144,128]{1,0:T(8,128)(2,1)S(1)} %get-tuple-element.32.refs_1_), channel_id=1, source_target_pairs={{0,20},{16,0},{4,16},{20,4},{8,28},{24,8},{12,24},{28,12},{1,21},{... | collective-permute-start | bytes 110600 | tf_op jit(solution)/shard_map/ppermute | solution.py:366
  12.3 1.8 %collective-permute-start.6 = (bf16[144,128]{1,0:T(8,128)(2,1)S(1)}, bf16[144,128]{1,0:T(8,128)(2,1)S(1)}, u32[]{:S(2)}, u32[]{:S(2)}) collective-permute-start(bf16[144,128]{1,0:T(8,128)(2,1)S(1)} %get-tuple-element.33), channel_id=1, source_target_pairs={{0,16},{16,0},{4,20},{20,4},{8,24},{24,8},{12,28},{28,12},{1,17},{... | collective-permute-start | bytes 110600 | tf_op jit(solution)/shard_map/ppermute | solution.py:366
  14.4 3.0 %collective-permute-start.7 = (bf16[8,2048]{1,0:T(8,128)(2,1)S(1)}, bf16[8,2048]{1,0:T(8,128)(2,1)S(1)}, u32[]{:S(2)}, u32[]{:S(2)}) collective-permute-start(bf16[8,2048]{1,0:T(8,128)(2,1)S(1)} %merge.1.attended), channel_id=1, source_target_pairs={{0,16},{16,0},{1,17},{17,1},{2,18},{18,2},{3,19},{19,3},{4,20},{20... | collective-permute-start | bytes 98312 | tf_op jit(solution)/shard_map/ppermute | solution.py:430
  19.1 4.7 %collective-permute-start.8 = (bf16[8,1024]{1,0:T(8,128)(2,1)S(1)}, bf16[8,1024]{1,0:T(8,128)(2,1)S(1)}, u32[]{:S(2)}, u32[]{:S(2)}) collective-permute-start(bf16[8,1024]{1,0:T(8,128)(2,1)S(1)} %get-tuple-element.34), channel_id=1, source_target_pairs={{0,3},{1,2},{2,1},{3,0},{4,7},{5,6},{6,5},{7,4},{8,11},{9,10},{10,... | collective-permute-start | bytes 49160 | tf_op jit(solution)/shard_map/ppermute | solution.py:448
  21.5 3.7 %collective-permute-start.9 = (bf16[8,1024]{1,0:T(8,128)(2,1)S(1)}, bf16[8,1024]{1,0:T(8,128)(2,1)S(1)}, u32[]{:S(2)}, u32[]{:S(2)}) collective-permute-start(bf16[8,1024]{1,0:T(8,128)(2,1)S(1)} %get-tuple-element.35), channel_id=1, source_target_pairs={{0,1},{1,0},{2,3},{3,2},{4,5},{5,4},{6,7},{7,6},{8,9},{9,8},{10,11... | collective-permute-start | bytes 49160 | tf_op jit(solution)/shard_map/ppermute | solution.py:448
  22.1 3.7 %collective-permute-start.10 = (bf16[8,1024]{1,0:T(8,128)(2,1)S(1)}, bf16[8,1024]{1,0:T(8,128)(2,1)S(1)}, u32[]{:S(2)}, u32[]{:S(2)}) collective-permute-start(bf16[8,1024]{1,0:T(8,128)(2,1)S(1)} %get-tuple-element.36), channel_id=1, source_target_pairs={{0,2},{1,3},{2,0},{3,1},{4,6},{5,7},{6,4},{7,5},{8,10},{9,11},{10,... | collective-permute-start | bytes 49160 | tf_op jit(solution)/shard_map/ppermute | solution.py:448

commit v8 on v5

--- a/solution.py
+++ b/solution.py
@@ -130,7 +130,7 @@
     chunks = jnp.maximum((found + CHUNK - 1) // CHUNK, STATIC[0])
 
     def fill(i, _):
-        page_copy(0, i).start()
+        pages[i] = jnp.zeros(pages.shape[1:], pages.dtype)
         listed[0, i] = 0
         listed[1, i] = 0
         return 0
@@ -148,12 +148,11 @@
 
     lax.fori_loop(0, chunks, describe, 0)
 
-    def wait(c, _):
-        for i in range(CHUNK):
-            page_copy(0, c * CHUNK + i).wait()
+    def wait(i, _):
+        page_copy(0, i).wait()
         return 0
 
-    lax.fori_loop(0, chunks, wait, 0)
+    lax.fori_loop(0, found, wait, 0)
 
 
 def resident_part(qa, pages, valid, out, held, per_held):

time: 26.6 us -> 26.6 us (level)
  no operation moved by 1% of the time
where the time goes in v8:
time: 26.6 us; the launch traced here: 26.3 us
  starting transfers between devices  11.7 us (44%)
  Pallas kernels  8.07 us (30%)
  waiting for transfers between devices  4.92 us (18%)
  other arithmetic  1.5 us (6%)
    ppermute x7, starting transfers between devices, paired(): return lax.ppermute(value, ('role', 'group'), pairs)  6.41 us
    pallas_call x1, Pallas kernels, per_device(): pl.pallas_call(functools.partial(first_kernel, held, per_held, groups, ma...  3.52 us
    ppermute x3, starting transfers between devices, per_device(): lax.ppermute(part, 'tp', [(i, i ^ d) for i in range(tps)])  3.5 us
    ppermute x3, waiting for transfers between devices, per_device(): lax.ppermute(part, 'tp', [(i, i ^ d) for i in range(tps)])  2.59 us
    pallas_call x2, Pallas kernels, project(): pl.pallas_call(functools.partial(project_kernel, steps), out_shape=[jax.S...  2.38 us
    pallas_call x2, Pallas kernels, per_device(): pl.pallas_call(functools.partial(second_kernel, held, per_held, maxp, fir...  1.83 us
    ppermute x1, starting transfers between devices, per_device(): partner = lax.ppermute(attended, 'role', [(0, 1), (1, 0)])  1.75 us
    ppermute x7, waiting for transfers between devices, paired(): return lax.ppermute(value, ('role', 'group'), pairs)  1.48 us
  transfers between devices with their start and end apart: 11, of which 7 were waited for; matrix products, arithmetic and copies ran while one was open for 0% of the time, Pallas kernels for 20%

profile of v8, /device:TPU:0, one launch (start us, length us, event | category | flops | bytes accessed | tf_op | source)
XLA Modules:
  0.0 26.3 jit_solution(1063175454740857525)
XLA Ops:
  0.0 0.9 %fusion.qa = bf16[8,2176]{1,0:T(8,128)(2,1)S(1)} fusion(s32[1,8]{1,0:T(1,128)} %lengths_hbm.1, s32[8,8]{1,0:T(8,128)} %bitcast.12, bf16[8,2048]{1,0:T(8,128)(2,1)} %bitcast.11), kind=kLoop, calls=%fused_computation.1 | loop fusion | flops 156672 | bytes 67872 | tf_op jit(solution)/shard_map/add | solution.py:347
  0.9 0.5 %collective-permute-start.1 = (bf16[8,2176]{1,0:T(8,128)(2,1)S(1)}, bf16[8,2176]{1,0:T(8,128)(2,1)S(1)}, u32[]{:S(2)}, u32[]{:S(2)}) collective-permute-start(bf16[8,2176]{1,0:T(8,128)(2,1)S(1)} %fusion.qa), channel_id=1, source_target_pairs={{16,4},{0,16},{20,0},{4,20},{24,12},{8,24},{28,8},{12,28},{17,5},{... | collective-permute-start | bytes 104456 | tf_op jit(solution)/shard_map/ppermute | solution.py:351
  1.3 2.7 %collective-permute-start = (bf16[8,2176]{1,0:T(8,128)(2,1)S(1)}, bf16[8,2176]{1,0:T(8,128)(2,1)S(1)}, u32[]{:S(2)}, u32[]{:S(2)}) collective-permute-start(bf16[8,2176]{1,0:T(8,128)(2,1)S(1)} %fusion.qa), channel_id=1, source_target_pairs={{16,8},{0,16},{20,12},{4,20},{24,0},{8,24},{28,4},{12,28},{17,9},{... | collective-permute-start | bytes 104456 | tf_op jit(solution)/shard_map/ppermute | solution.py:351
  4.0 1.1 %collective-permute-start.2 = (bf16[8,2176]{1,0:T(8,128)(2,1)S(1)}, bf16[8,2176]{1,0:T(8,128)(2,1)S(1)}, u32[]{:S(2)}, u32[]{:S(2)}) collective-permute-start(bf16[8,2176]{1,0:T(8,128)(2,1)S(1)} %fusion.qa), channel_id=1, source_target_pairs={{16,12},{0,16},{20,8},{4,20},{24,4},{8,24},{28,0},{12,28},{17,13},... | collective-permute-start | bytes 104456 | tf_op jit(solution)/shard_map/ppermute | solution.py:351
  5.1 3.5 %resident.1 = (bf16[144,128]{1,0:T(8,128)(2,1)S(1)}, bf16[64,128,512]{2,1,0:T(8,128)(2,1)S(1)}, f32[24,128]{1,0:T(8,128)S(1)}, f32[72,128]{1,0:T(8,128)S(1)}) custom-call(bf16[8,2176]{1,0:T(8,128)(2,1)S(1)} %fusion.qa, s32[3,4,12]{2,1,0:T(4,128)} %bitcast.14, s32[4,6]{1,0:T(4,128)} %wanted_hbm.1, s32[8,8]{1,0:T(8,128)} %bitcast.13, s32[1,8]{1,0:T(1,128)} %lengths_hbm.1, ...), custom_call_target="tpu_custom_call" | custom-call | tf_op jit(solution)/shard_map/resident/pallas_call | solution.py:364
  8.6 1.2 %owned.2 = (bf16[144,128]{1,0:T(8,128)(2,1)S(1)}, bf16[144,128]{1,0:T(8,128)(2,1)S(1)}) custom-call(bf16[64,128,512]{2,1,0:T(8,128)(2,1)S(1)} %get-tuple-element.22.chosen.pages, f32[24,128]{1,0:T(8,128)S(1)} %get-tuple-element.23.entries, bf16[8,2176]{1,0:T(8,128)(2,1)S(1)} %collective-permute-done.refs_0_, bf16[8,2176]{1,0:T(8,128)(2,1)S(1)} %collective-permute-done.1.refs_1_), custom_call_target="tpu_custom_call" | custom-call | flops 20000000000 | bytes 8388608 | tf_op jit(solution)/shard_map/owned/pallas_call | solution.py:388
  9.9 0.6 %owned.3 = bf16[144,128]{1,0:T(8,128)(2,1)S(1)} custom-call(bf16[64,128,512]{2,1,0:T(8,128)(2,1)S(1)} %get-tuple-element.22.chosen.pages, f32[24,128]{1,0:T(8,128)S(1)} %get-tuple-element.23.entries, bf16[8,2176]{1,0:T(8,128)(2,1)S(1)} %collective-permute-done.2.refs_0_, bf16[144,128]{1,0:T(8,128)(2,1)S(1)} %get-tuple-element.32.refs_1_, ...), custom_call_target="tpu_custom_call" | custom-call | flops 20000000000 | bytes 8388608 | tf_op jit(solution)/shard_map/owned/pallas_call | solution.py:388
  10.6 0.7 %collective-permute-start.3 = (bf16[144,128]{1,0:T(8,128)(2,1)S(1)}, bf16[144,128]{1,0:T(8,128)(2,1)S(1)}, u32[]{:S(2)}, u32[]{:S(2)}) collective-permute-start(bf16[144,128]{1,0:T(8,128)(2,1)S(1)} %owned.3), channel_id=1, source_target_pairs={{0,28},{16,0},{4,24},{20,4},{8,20},{24,8},{12,16},{28,12},{1,29},{... | collective-permute-start | bytes 110600 | tf_op jit(solution)/shard_map/ppermute | solution.py:351
  11.2 1.0 %collective-permute-start.4 = (bf16[144,128]{1,0:T(8,128)(2,1)S(1)}, bf16[144,128]{1,0:T(8,128)(2,1)S(1)}, u32[]{:S(2)}, u32[]{:S(2)}) collective-permute-start(bf16[144,128]{1,0:T(8,128)(2,1)S(1)} %get-tuple-element.31.refs_2_), channel_id=1, source_target_pairs={{0,24},{16,0},{4,28},{20,4},{8,16},{24,8},{12,20},{28,12},{1,25},{... | collective-permute-start | bytes 110600 | tf_op jit(solution)/shard_map/ppermute | solution.py:351
  12.4 0.4 %collective-permute-start.6 = (bf16[144,128]{1,0:T(8,128)(2,1)S(1)}, bf16[144,128]{1,0:T(8,128)(2,1)S(1)}, u32[]{:S(2)}, u32[]{:S(2)}) collective-permute-start(bf16[144,128]{1,0:T(8,128)(2,1)S(1)} %get-tuple-element.33), channel_id=1, source_target_pairs={{0,16},{16,0},{4,20},{20,4},{8,24},{24,8},{12,28},{28,12},{1,17},{... | collective-permute-start | bytes 110600 | tf_op jit(solution)/shard_map/ppermute | solution.py:351
  12.9 1.0 %collective-permute-done.4.refs_3_ = bf16[144,128]{1,0:T(8,128)(2,1)S(1)} collective-permute-done((bf16[144,128]{1,0:T(8,128)(2,1)S(1)}, bf16[144,128]{1,0:T(8,128)(2,1)S(1)}, u32[]{:S(2)}, u32[]{:S(2)}) %collective-permute-start.4) | collective-permute-done | bytes 36896 | tf_op jit(solution)/shard_map/ppermute | solution.py:351
  13.9 0.3 %collective-permute-done.5.refs_4_ = bf16[144,128]{1,0:T(8,128)(2,1)S(1)} collective-permute-done((bf16[144,128]{1,0:T(8,128)(2,1)S(1)}, bf16[144,128]{1,0:T(8,128)(2,1)S(1)}, u32[]{:S(2)}, u32[]{:S(2)}) %collective-permute-start.5) | collective-permute-done | bytes 36896 | tf_op jit(solution)/shard_map/ppermute | solution.py:351
  14.2 0.3 %merge.1.attended = bf16[8,2048]{1,0:T(8,128)(2,1)S(1)} custom-call(f32[144,128]{1,0:T(8,128)S(1)} %get-tuple-element.28.refs_0_, f32[144,128]{1,0:T(8,128)S(1)} %get-tuple-element.29.refs_1_, bf16[144,128]{1,0:T(8,128)(2,1)S(1)} %collective-permute-done.3.refs_2_, bf16[144,128]{1,0:T(8,128)(2,1)S(1)} %collective-permute-done.4.refs_3_, ...), custom_call_target="tpu_custom_call" | custom-call | tf_op jit(solution)/shard_map/merge/pallas_call | solution.py:407
  14.6 1.8 %collective-permute-start.7 = (bf16[8,2048]{1,0:T(8,128)(2,1)S(1)}, bf16[8,2048]{1,0:T(8,128)(2,1)S(1)}, u32[]{:S(2)}, u32[]{:S(2)}) collective-permute-start(bf16[8,2048]{1,0:T(8,128)(2,1)S(1)} %merge.1.attended), channel_id=1, source_target_pairs={{0,16},{16,0},{1,17},{17,1},{2,18},{18,2},{3,19},{19,3},{4,20},{20... | collective-permute-start | bytes 98312 | tf_op jit(solution)/shard_map/ppermute | solution.py:415
  16.3 0.9 %collective-permute-done.7.partner = bf16[8,2048]{1,0:T(8,128)(2,1)S(1)} collective-permute-done((bf16[8,2048]{1,0:T(8,128)(2,1)S(1)}, bf16[8,2048]{1,0:T(8,128)(2,1)S(1)}, u32[]{:S(2)}, u32[]{:S(2)}) %collective-permute-start.7) | collective-permute-done | bytes 32800 | tf_op jit(solution)/shard_map/ppermute | solution.py:415
  17.2 1.7 %project.1 = (bf16[8,1024]{1,0:T(8,128)(2,1)S(1)}, bf16[8,1024]{1,0:T(8,128)(2,1)S(1)}, bf16[8,1024]{1,0:T(8,128)(2,1)S(1)}) custom-call(bf16[8,2048]{1,0:T(8,128)(2,1)S(1)} %merge.1.attended, bf16[8,2048]{1,0:T(8,128)(2,1)S(1)} %collective-permute-done.7.partner, bf16[2048,4096]{1,0:T(8,128)(2,1)S(1)} %bitcast.8), custom_call_target="tpu_custom_call" | custom-call | flops 201326592 | bytes 12582912 | tf_op jit(solution)/shard_map/project/pallas_call | solution.py:419
  19.0 2.5 %collective-permute-start.8 = (bf16[8,1024]{1,0:T(8,128)(2,1)S(1)}, bf16[8,1024]{1,0:T(8,128)(2,1)S(1)}, u32[]{:S(2)}, u32[]{:S(2)}) collective-permute-start(bf16[8,1024]{1,0:T(8,128)(2,1)S(1)} %get-tuple-element.34), channel_id=1, source_target_pairs={{0,3},{1,2},{2,1},{3,0},{4,7},{5,6},{6,5},{7,4},{8,11},{9,10},{10,... | collective-permute-start | bytes 49160 | tf_op jit(solution)/shard_map/ppermute | solution.py:433
  21.4 0.5 %collective-permute-start.9 = (bf16[8,1024]{1,0:T(8,128)(2,1)S(1)}, bf16[8,1024]{1,0:T(8,128)(2,1)S(1)}, u32[]{:S(2)}, u32[]{:S(2)}) collective-permute-start(bf16[8,1024]{1,0:T(8,128)(2,1)S(1)} %get-tuple-element.35), channel_id=1, source_target_pairs={{0,1},{1,0},{2,3},{3,2},{4,5},{5,4},{6,7},{7,6},{8,9},{9,8},{10,11... | collective-permute-start | bytes 49160 | tf_op jit(solution)/shard_map/ppermute | solution.py:433
  22.0 0.5 %collective-permute-start.10 = (bf16[8,1024]{1,0:T(8,128)(2,1)S(1)}, bf16[8,1024]{1,0:T(8,128)(2,1)S(1)}, u32[]{:S(2)}, u32[]{:S(2)}) collective-permute-start(bf16[8,1024]{1,0:T(8,128)(2,1)S(1)} %get-tuple-element.36), channel_id=1, source_target_pairs={{0,2},{1,3},{2,0},{3,1},{4,6},{5,7},{6,4},{7,5},{8,10},{9,11},{10,... | collective-permute-start | bytes 49160 | tf_op jit(solution)/shard_map/ppermute | solution.py:433
  22.5 0.6 %project_own.1 = f32[8,1024]{1,0:T(8,128)S(1)} custom-call(bf16[8,2048]{1,0:T(8,128)(2,1)S(1)} %merge.1.attended, bf16[8,2048]{1,0:T(8,128)(2,1)S(1)} %collective-permute-done.7.partner, bf16[2048,4096]{1,0:T(8,128)(2,1)S(1)} %bitcast.8), custom_call_target="tpu_custom_call" | custom-call | flops 67108864 | bytes 4194304 | tf_op jit(solution)/shard_map/project_own/pallas_call | solution.py:419
  23.1 0.5 %collective-permute-done.8 = bf16[8,1024]{1,0:T(8,128)(2,1)S(1)} collective-permute-done((bf16[8,1024]{1,0:T(8,128)(2,1)S(1)}, bf16[8,1024]{1,0:T(8,128)(2,1)S(1)}, u32[]{:S(2)}, u32[]{:S(2)}) %collective-permute-start.8) | collective-permute-done | bytes 16416 | tf_op jit(solution)/shard_map/ppermute | solution.py:433
  23.6 1.5 %collective-permute-done.9 = bf16[8,1024]{1,0:T(8,128)(2,1)S(1)} collective-permute-done((bf16[8,1024]{1,0:T(8,128)(2,1)S(1)}, bf16[8,1024]{1,0:T(8,128)(2,1)S(1)}, u32[]{:S(2)}, u32[]{:S(2)}) %collective-permute-start.9) | collective-permute-done | bytes 16416 | tf_op jit(solution)/shard_map/ppermute | solution.py:433
  25.2 0.5 %collective-permute-done.10 = bf16[8,1024]{1,0:T(8,128)(2,1)S(1)} collective-permute-done((bf16[8,1024]{1,0:T(8,128)(2,1)S(1)}, bf16[8,1024]{1,0:T(8,128)(2,1)S(1)}, u32[]{:S(2)}, u32[]{:S(2)}) %collective-permute-start.10) | collective-permute-done | bytes 16416 | tf_op jit(solution)/shard_map/ppermute | solution.py:433
  25.7 0.6 %fusion.1 = bf16[1,8,1024]{2,1,0:T(8,128)(2,1)} fusion(bf16[8,1024]{1,0:T(8,128)(2,1)S(1)} %collective-permute-done.10, bf16[8,1024]{1,0:T(8,128)(2,1)S(1)} %collective-permute-done.9, f32[8,1024]{1,0:T(8,128)S(1)} %project_own.1, bf16[8,1024]{1,0:T(8,128)(2,1)S(1)} %collective-permute-done.8), kind=kLoop, calls=%fused_computation.3 | loop fusion | flops 57344 | bytes 98304 | tf_op jit(solution)/shard_map/broadcast_in_dim | solution.py:436
  (18 shorter events, 0.3 us)
Async XLA Ops:
  0.9 7.7 %collective-permute-start.1 = (bf16[8,2176]{1,0:T(8,128)(2,1)S(1)}, bf16[8,2176]{1,0:T(8,128)(2,1)S(1)}, u32[]{:S(2)}, u32[]{:S(2)}) collective-permute-start(bf16[8,2176]{1,0:T(8,128)(2,1)S(1)} %fusion.qa), channel_id=1, source_target_pairs={{16,4},{0,16},{20,0},{4,20},{24,12},{8,24},{28,8},{12,28},{17,5},{... | collective-permute-start | bytes 104456 | tf_op jit(solution)/shard_map/ppermute | solution.py:351
  1.3 7.3 %collective-permute-start = (bf16[8,2176]{1,0:T(8,128)(2,1)S(1)}, bf16[8,2176]{1,0:T(8,128)(2,1)S(1)}, u32[]{:S(2)}, u32[]{:S(2)}) collective-permute-start(bf16[8,2176]{1,0:T(8,128)(2,1)S(1)} %fusion.qa), channel_id=1, source_target_pairs={{16,8},{0,16},{20,12},{4,20},{24,0},{8,24},{28,4},{12,28},{17,9},{... | collective-permute-start | bytes 104456 | tf_op jit(solution)/shard_map/ppermute | solution.py:351
  4.0 5.8 %collective-permute-start.2 = (bf16[8,2176]{1,0:T(8,128)(2,1)S(1)}, bf16[8,2176]{1,0:T(8,128)(2,1)S(1)}, u32[]{:S(2)}, u32[]{:S(2)}) collective-permute-start(bf16[8,2176]{1,0:T(8,128)(2,1)S(1)} %fusion.qa), channel_id=1, source_target_pairs={{16,12},{0,16},{20,8},{4,20},{24,4},{8,24},{28,0},{12,28},{17,13},... | collective-permute-start | bytes 104456 | tf_op jit(solution)/shard_map/ppermute | solution.py:351
  9.9 7.3 %slice-start = ((s8[16777216]{0:T(1024)(128)(4,1)}), s8[4194304]{0:T(1024)(128)(4,1)S(1)}, s32[]{:S(2)}) async-start(s8[16777216]{0:T(1024)(128)(4,1)} %bitcast.7), calls=%async_computation | async-start | bytes 8388608
  9.9 2.9 %copy-start = (bf16[1,8,512]{2,1,0:T(8,128)(2,1)S(1)}, bf16[1,8,512]{2,1,0:T(8,128)(2,1)}, u32[]{:S(2)}) copy-start(bf16[1,8,512]{2,1,0:T(8,128)(2,1)} %param.14) | copy-start | bytes 24580
  9.9 7.3 %slice-start.1 = ((s8[16777216]{0:T(1024)(128)(4,1)}), s8[4194304]{0:T(1024)(128)(4,1)S(1)}, s32[]{:S(2)}) async-start(s8[16777216]{0:T(1024)(128)(4,1)} %bitcast.7), calls=%async_computation.1 | async-start | bytes 8388608
  9.9 7.3 %slice-start.2 = ((s8[16777216]{0:T(1024)(128)(4,1)}), s8[4194304]{0:T(1024)(128)(4,1)S(1)}, s32[]{:S(2)}) async-start(s8[16777216]{0:T(1024)(128)(4,1)} %bitcast.7), calls=%async_computation.2 | async-start | bytes 8388608
  9.9 7.3 %slice-start.3 = ((s8[16777216]{0:T(1024)(128)(4,1)}), s8[4194304]{0:T(1024)(128)(4,1)S(1)}, s32[]{:S(2)}) async-start(s8[16777216]{0:T(1024)(128)(4,1)} %bitcast.7), calls=%async_computation.3 | async-start | bytes 8388608
  10.6 2.3 %collective-permute-start.3 = (bf16[144,128]{1,0:T(8,128)(2,1)S(1)}, bf16[144,128]{1,0:T(8,128)(2,1)S(1)}, u32[]{:S(2)}, u32[]{:S(2)}) collective-permute-start(bf16[144,128]{1,0:T(8,128)(2,1)S(1)} %owned.3), channel_id=1, source_target_pairs={{0,28},{16,0},{4,24},{20,4},{8,20},{24,8},{12,16},{28,12},{1,29},{... | collective-permute-start | bytes 110600 | tf_op jit(solution)/shard_map/ppermute | solution.py:351
  11.2 2.6 %collective-permute-start.4 = (bf16[144,128]{1,0:T(8,128)(2,1)S(1)}, bf16[144,128]{1,0:T(8,128)(2,1)S(1)}, u32[]{:S(2)}, u32[]{:S(2)}) collective-permute-start(bf16[144,128]{1,0:T(8,128)(2,1)S(1)} %get-tuple-element.31.refs_2_), channel_id=1, source_target_pairs={{0,24},{16,0},{4,28},{20,4},{8,16},{24,8},{12,20},{28,12},{1,25},{... | collective-permute-start | bytes 110600 | tf_op jit(solution)/shard_map/ppermute | solution.py:351
  12.3 2.0 %collective-permute-start.5 = (bf16[144,128]{1,0:T(8,128)(2,1)S(1)}, bf16[144,128]{1,0:T(8,128)(2,1)S(1)}, u32[]{:S(2)}, u32[]{:S(2)}) collective-permute-start(bf16[144,128]{1,0:T(8,128)(2,1)S(1)} %get-tuple-element.32.refs_1_), channel_id=1, source_target_pairs={{0,20},{16,0},{4,16},{20,4},{8,28},{24,8},{12,24},{28,12},{1,21},{... | collective-permute-start | bytes 110600 | tf_op jit(solution)/shard_map/ppermute | solution.py:351
  12.4 1.9 %collective-permute-start.6 = (bf16[144,128]{1,0:T(8,128)(2,1)S(1)}, bf16[144,128]{1,0:T(8,128)(2,1)S(1)}, u32[]{:S(2)}, u32[]{:S(2)}) collective-permute-start(bf16[144,128]{1,0:T(8,128)(2,1)S(1)} %get-tuple-element.33), channel_id=1, source_target_pairs={{0,16},{16,0},{4,20},{20,4},{8,24},{24,8},{12,28},{28,12},{1,17},{... | collective-permute-start | bytes 110600 | tf_op jit(solution)/shard_map/ppermute | solution.py:351
  14.6 2.6 %collective-permute-start.7 = (bf16[8,2048]{1,0:T(8,128)(2,1)S(1)}, bf16[8,2048]{1,0:T(8,128)(2,1)S(1)}, u32[]{:S(2)}, u32[]{:S(2)}) collective-permute-start(bf16[8,2048]{1,0:T(8,128)(2,1)S(1)} %merge.1.attended), channel_id=1, source_target_pairs={{0,16},{16,0},{1,17},{17,1},{2,18},{18,2},{3,19},{19,3},{4,20},{20... | collective-permute-start | bytes 98312 | tf_op jit(solution)/shard_map/ppermute | solution.py:415
  19.0 4.7 %collective-permute-start.8 = (bf16[8,1024]{1,0:T(8,128)(2,1)S(1)}, bf16[8,1024]{1,0:T(8,128)(2,1)S(1)}, u32[]{:S(2)}, u32[]{:S(2)}) collective-permute-start(bf16[8,1024]{1,0:T(8,128)(2,1)S(1)} %get-tuple-element.34), channel_id=1, source_target_pairs={{0,3},{1,2},{2,1},{3,0},{4,7},{5,6},{6,5},{7,4},{8,11},{9,10},{10,... | collective-permute-start | bytes 49160 | tf_op jit(solution)/shard_map/ppermute | solution.py:433
  21.4 3.7 %collective-permute-start.9 = (bf16[8,1024]{1,0:T(8,128)(2,1)S(1)}, bf16[8,1024]{1,0:T(8,128)(2,1)S(1)}, u32[]{:S(2)}, u32[]{:S(2)}) collective-permute-start(bf16[8,1024]{1,0:T(8,128)(2,1)S(1)} %get-tuple-element.35), channel_id=1, source_target_pairs={{0,1},{1,0},{2,3},{3,2},{4,5},{5,4},{6,7},{7,6},{8,9},{9,8},{10,11... | collective-permute-start | bytes 49160 | tf_op jit(solution)/shard_map/ppermute | solution.py:433
  22.0 3.7 %collective-permute-start.10 = (bf16[8,1024]{1,0:T(8,128)(2,1)S(1)}, bf16[8,1024]{1,0:T(8,128)(2,1)S(1)}, u32[]{:S(2)}, u32[]{:S(2)}) collective-permute-start(bf16[8,1024]{1,0:T(8,128)(2,1)S(1)} %get-tuple-element.36), channel_id=1, source_target_pairs={{0,2},{1,3},{2,0},{3,1},{4,6},{5,7},{6,4},{7,5},{8,10},{9,11},{10,... | collective-permute-start | bytes 49160 | tf_op jit(solution)/shard_map/ppermute | solution.py:433

commit v9 on v5

--- a/solution.py
+++ b/solution.py
@@ -429,7 +429,7 @@
             name=name,
         )(attended, partner, out_weight)
 
-    steps = sorted(range(1, tps), key=lambda d: -d.bit_count())
+    steps = sorted(range(1, tps), key=lambda d: d.bit_count())
     sent = project(steps, jnp.bfloat16, "project")
     arrived = [lax.ppermute(part, "tp", [(i, i ^ d) for i in range(tps)]) for d, part in zip(steps, sent)]
     own = project([0], jnp.float32, "project_own")[0]

time: 26.6 us -> 27.7 us (1.041)
  waiting for transfers between devices: 4.92 us -> 5.85 us
    ppermute x3, waiting for transfers between devices: 2.59 us -> 3.51 us  [per_device(): lax.ppermute(part, 'tp', [(i, i ^ d) for i in range(tps)])]
  transfers between devices with their start and end apart: 11 -> 11, of which waited for: 7 -> 6; matrix products, arithmetic and copies ran while one was open for 0% -> 0% of each run, Pallas kernels for 20% -> 20%
where the time goes in v9:
time: 27.7 us; the launch traced here: 27.4 us
  starting transfers between devices  11.8 us (43%)
  Pallas kernels  8.07 us (29%)
  waiting for transfers between devices  5.85 us (21%)
  other arithmetic  1.5 us (5%)
    ppermute x7, starting transfers between devices, paired(): return lax.ppermute(value, ('role', 'group'), pairs)  6.41 us
    pallas_call x1, Pallas kernels, per_device(): pl.pallas_call(functools.partial(first_kernel, held, per_held, groups, ma...  3.52 us
    ppermute x3, waiting for transfers between devices, per_device(): lax.ppermute(part, 'tp', [(i, i ^ d) for i in range(tps)])  3.51 us
    ppermute x3, starting transfers between devices, per_device(): lax.ppermute(part, 'tp', [(i, i ^ d) for i in range(tps)])  3.5 us
    pallas_call x2, Pallas kernels, project(): pl.pallas_call(functools.partial(project_kernel, steps), out_shape=[jax.S...  2.38 us
    ppermute x1, starting transfers between devices, per_device(): partner = lax.ppermute(attended, 'role', [(0, 1), (1, 0)])  1.88 us
    pallas_call x2, Pallas kernels, per_device(): pl.pallas_call(functools.partial(second_kernel, held, per_held, maxp, fir...  1.83 us
    ppermute x7, waiting for transfers between devices, paired(): return lax.ppermute(value, ('role', 'group'), pairs)  1.48 us
  transfers between devices with their start and end apart: 11, of which 6 were waited for; matrix products, arithmetic and copies ran while one was open for 0% of the time, Pallas kernels for 20%

profile of v9, /device:TPU:0, one launch (start us, length us, event | category | flops | bytes accessed | tf_op | source)
XLA Modules:
  0.0 27.4 jit_solution(6505140290063121254)
XLA Ops:
  0.0 0.9 %fusion.qa = bf16[8,2176]{1,0:T(8,128)(2,1)S(1)} fusion(s32[1,8]{1,0:T(1,128)} %lengths_hbm.1, s32[8,8]{1,0:T(8,128)} %bitcast.12, bf16[8,2048]{1,0:T(8,128)(2,1)} %bitcast.11), kind=kLoop, calls=%fused_computation.1 | loop fusion | flops 156672 | bytes 67872 | tf_op jit(solution)/shard_map/add | solution.py:348
  0.9 0.5 %collective-permute-start.1 = (bf16[8,2176]{1,0:T(8,128)(2,1)S(1)}, bf16[8,2176]{1,0:T(8,128)(2,1)S(1)}, u32[]{:S(2)}, u32[]{:S(2)}) collective-permute-start(bf16[8,2176]{1,0:T(8,128)(2,1)S(1)} %fusion.qa), channel_id=1, source_target_pairs={{16,4},{0,16},{20,0},{4,20},{24,12},{8,24},{28,8},{12,28},{17,5},{... | collective-permute-start | bytes 104456 | tf_op jit(solution)/shard_map/ppermute | solution.py:352
  1.3 2.7 %collective-permute-start = (bf16[8,2176]{1,0:T(8,128)(2,1)S(1)}, bf16[8,2176]{1,0:T(8,128)(2,1)S(1)}, u32[]{:S(2)}, u32[]{:S(2)}) collective-permute-start(bf16[8,2176]{1,0:T(8,128)(2,1)S(1)} %fusion.qa), channel_id=1, source_target_pairs={{16,8},{0,16},{20,12},{4,20},{24,0},{8,24},{28,4},{12,28},{17,9},{... | collective-permute-start | bytes 104456 | tf_op jit(solution)/shard_map/ppermute | solution.py:352
  4.0 1.1 %collective-permute-start.2 = (bf16[8,2176]{1,0:T(8,128)(2,1)S(1)}, bf16[8,2176]{1,0:T(8,128)(2,1)S(1)}, u32[]{:S(2)}, u32[]{:S(2)}) collective-permute-start(bf16[8,2176]{1,0:T(8,128)(2,1)S(1)} %fusion.qa), channel_id=1, source_target_pairs={{16,12},{0,16},{20,8},{4,20},{24,4},{8,24},{28,0},{12,28},{17,13},... | collective-permute-start | bytes 104456 | tf_op jit(solution)/shard_map/ppermute | solution.py:352
  5.1 3.5 %resident.1 = (bf16[144,128]{1,0:T(8,128)(2,1)S(1)}, bf16[64,128,512]{2,1,0:T(8,128)(2,1)S(1)}, f32[24,128]{1,0:T(8,128)S(1)}, f32[72,128]{1,0:T(8,128)S(1)}) custom-call(bf16[8,2176]{1,0:T(8,128)(2,1)S(1)} %fusion.qa, s32[3,4,12]{2,1,0:T(4,128)} %bitcast.14, s32[4,6]{1,0:T(4,128)} %wanted_hbm.1, s32[8,8]{1,0:T(8,128)} %bitcast.13, s32[1,8]{1,0:T(1,128)} %lengths_hbm.1, ...), custom_call_target="tpu_custom_call" | custom-call | tf_op jit(solution)/shard_map/resident/pallas_call | solution.py:365
  8.6 1.2 %owned.2 = (bf16[144,128]{1,0:T(8,128)(2,1)S(1)}, bf16[144,128]{1,0:T(8,128)(2,1)S(1)}) custom-call(bf16[64,128,512]{2,1,0:T(8,128)(2,1)S(1)} %get-tuple-element.22.chosen.pages, f32[24,128]{1,0:T(8,128)S(1)} %get-tuple-element.23.entries, bf16[8,2176]{1,0:T(8,128)(2,1)S(1)} %collective-permute-done.refs_0_, bf16[8,2176]{1,0:T(8,128)(2,1)S(1)} %collective-permute-done.1.refs_1_), custom_call_target="tpu_custom_call" | custom-call | flops 20000000000 | bytes 8388608 | tf_op jit(solution)/shard_map/owned/pallas_call | solution.py:389
  9.9 0.6 %owned.3 = bf16[144,128]{1,0:T(8,128)(2,1)S(1)} custom-call(bf16[64,128,512]{2,1,0:T(8,128)(2,1)S(1)} %get-tuple-element.22.chosen.pages, f32[24,128]{1,0:T(8,128)S(1)} %get-tuple-element.23.entries, bf16[8,2176]{1,0:T(8,128)(2,1)S(1)} %collective-permute-done.2.refs_0_, bf16[144,128]{1,0:T(8,128)(2,1)S(1)} %get-tuple-element.32.refs_1_, ...), custom_call_target="tpu_custom_call" | custom-call | flops 20000000000 | bytes 8388608 | tf_op jit(solution)/shard_map/owned/pallas_call | solution.py:389
  10.6 0.8 %collective-permute-start.3 = (bf16[144,128]{1,0:T(8,128)(2,1)S(1)}, bf16[144,128]{1,0:T(8,128)(2,1)S(1)}, u32[]{:S(2)}, u32[]{:S(2)}) collective-permute-start(bf16[144,128]{1,0:T(8,128)(2,1)S(1)} %owned.3), channel_id=1, source_target_pairs={{0,28},{16,0},{4,24},{20,4},{8,20},{24,8},{12,16},{28,12},{1,29},{... | collective-permute-start | bytes 110600 | tf_op jit(solution)/shard_map/ppermute | solution.py:352
  11.4 0.9 %collective-permute-start.4 = (bf16[144,128]{1,0:T(8,128)(2,1)S(1)}, bf16[144,128]{1,0:T(8,128)(2,1)S(1)}, u32[]{:S(2)}, u32[]{:S(2)}) collective-permute-start(bf16[144,128]{1,0:T(8,128)(2,1)S(1)} %get-tuple-element.31.refs_2_), channel_id=1, source_target_pairs={{0,24},{16,0},{4,28},{20,4},{8,16},{24,8},{12,20},{28,12},{1,25},{... | collective-permute-start | bytes 110600 | tf_op jit(solution)/shard_map/ppermute | solution.py:352
  12.4 0.4 %collective-permute-start.6 = (bf16[144,128]{1,0:T(8,128)(2,1)S(1)}, bf16[144,128]{1,0:T(8,128)(2,1)S(1)}, u32[]{:S(2)}, u32[]{:S(2)}) collective-permute-start(bf16[144,128]{1,0:T(8,128)(2,1)S(1)} %get-tuple-element.33), channel_id=1, source_target_pairs={{0,16},{16,0},{4,20},{20,4},{8,24},{24,8},{12,28},{28,12},{1,17},{... | collective-permute-start | bytes 110600 | tf_op jit(solution)/shard_map/ppermute | solution.py:352
  12.8 0.2 collective-permute-done.3.refs_2_
  13.0 0.9 %collective-permute-done.4.refs_3_ = bf16[144,128]{1,0:T(8,128)(2,1)S(1)} collective-permute-done((bf16[144,128]{1,0:T(8,128)(2,1)S(1)}, bf16[144,128]{1,0:T(8,128)(2,1)S(1)}, u32[]{:S(2)}, u32[]{:S(2)}) %collective-permute-start.4) | collective-permute-done | bytes 36896 | tf_op jit(solution)/shard_map/ppermute | solution.py:352
  13.9 0.3 %collective-permute-done.5.refs_4_ = bf16[144,128]{1,0:T(8,128)(2,1)S(1)} collective-permute-done((bf16[144,128]{1,0:T(8,128)(2,1)S(1)}, bf16[144,128]{1,0:T(8,128)(2,1)S(1)}, u32[]{:S(2)}, u32[]{:S(2)}) %collective-permute-start.5) | collective-permute-done | bytes 36896 | tf_op jit(solution)/shard_map/ppermute | solution.py:352
  14.2 0.3 %merge.1.attended = bf16[8,2048]{1,0:T(8,128)(2,1)S(1)} custom-call(f32[144,128]{1,0:T(8,128)S(1)} %get-tuple-element.28.refs_0_, f32[144,128]{1,0:T(8,128)S(1)} %get-tuple-element.29.refs_1_, bf16[144,128]{1,0:T(8,128)(2,1)S(1)} %collective-permute-done.3.refs_2_, bf16[144,128]{1,0:T(8,128)(2,1)S(1)} %collective-permute-done.4.refs_3_, ...), custom_call_target="tpu_custom_call" | custom-call | tf_op jit(solution)/shard_map/merge/pallas_call | solution.py:408
  14.6 1.9 %collective-permute-start.7 = (bf16[8,2048]{1,0:T(8,128)(2,1)S(1)}, bf16[8,2048]{1,0:T(8,128)(2,1)S(1)}, u32[]{:S(2)}, u32[]{:S(2)}) collective-permute-start(bf16[8,2048]{1,0:T(8,128)(2,1)S(1)} %merge.1.attended), channel_id=1, source_target_pairs={{0,16},{16,0},{1,17},{17,1},{2,18},{18,2},{3,19},{19,3},{4,20},{20... | collective-permute-start | bytes 98312 | tf_op jit(solution)/shard_map/ppermute | solution.py:416
  16.5 0.9 %collective-permute-done.7.partner = bf16[8,2048]{1,0:T(8,128)(2,1)S(1)} collective-permute-done((bf16[8,2048]{1,0:T(8,128)(2,1)S(1)}, bf16[8,2048]{1,0:T(8,128)(2,1)S(1)}, u32[]{:S(2)}, u32[]{:S(2)}) %collective-permute-start.7) | collective-permute-done | bytes 32800 | tf_op jit(solution)/shard_map/ppermute | solution.py:416
  17.3 1.7 %project.1 = (bf16[8,1024]{1,0:T(8,128)(2,1)S(1)}, bf16[8,1024]{1,0:T(8,128)(2,1)S(1)}, bf16[8,1024]{1,0:T(8,128)(2,1)S(1)}) custom-call(bf16[8,2048]{1,0:T(8,128)(2,1)S(1)} %merge.1.attended, bf16[8,2048]{1,0:T(8,128)(2,1)S(1)} %collective-permute-done.7.partner, bf16[2048,4096]{1,0:T(8,128)(2,1)S(1)} %bitcast.8), custom_call_target="tpu_custom_call" | custom-call | flops 201326592 | bytes 12582912 | tf_op jit(solution)/shard_map/project/pallas_call | solution.py:420
  19.1 1.5 %collective-permute-start.8 = (bf16[8,1024]{1,0:T(8,128)(2,1)S(1)}, bf16[8,1024]{1,0:T(8,128)(2,1)S(1)}, u32[]{:S(2)}, u32[]{:S(2)}) collective-permute-start(bf16[8,1024]{1,0:T(8,128)(2,1)S(1)} %get-tuple-element.34), channel_id=1, source_target_pairs={{0,1},{1,0},{2,3},{3,2},{4,5},{5,4},{6,7},{7,6},{8,9},{9,8},{10,11... | collective-permute-start | bytes 49160 | tf_op jit(solution)/shard_map/ppermute | solution.py:434
  20.6 1.5 %collective-permute-start.9 = (bf16[8,1024]{1,0:T(8,128)(2,1)S(1)}, bf16[8,1024]{1,0:T(8,128)(2,1)S(1)}, u32[]{:S(2)}, u32[]{:S(2)}) collective-permute-start(bf16[8,1024]{1,0:T(8,128)(2,1)S(1)} %get-tuple-element.35), channel_id=1, source_target_pairs={{0,2},{1,3},{2,0},{3,1},{4,6},{5,7},{6,4},{7,5},{8,10},{9,11},{10,... | collective-permute-start | bytes 49160 | tf_op jit(solution)/shard_map/ppermute | solution.py:434
  22.1 0.5 %collective-permute-start.10 = (bf16[8,1024]{1,0:T(8,128)(2,1)S(1)}, bf16[8,1024]{1,0:T(8,128)(2,1)S(1)}, u32[]{:S(2)}, u32[]{:S(2)}) collective-permute-start(bf16[8,1024]{1,0:T(8,128)(2,1)S(1)} %get-tuple-element.36), channel_id=1, source_target_pairs={{0,3},{1,2},{2,1},{3,0},{4,7},{5,6},{6,5},{7,4},{8,11},{9,10},{10,... | collective-permute-start | bytes 49160 | tf_op jit(solution)/shard_map/ppermute | solution.py:434
  22.6 0.6 %project_own.1 = f32[8,1024]{1,0:T(8,128)S(1)} custom-call(bf16[8,2048]{1,0:T(8,128)(2,1)S(1)} %merge.1.attended, bf16[8,2048]{1,0:T(8,128)(2,1)S(1)} %collective-permute-done.7.partner, bf16[2048,4096]{1,0:T(8,128)(2,1)S(1)} %bitcast.8), custom_call_target="tpu_custom_call" | custom-call | flops 67108864 | bytes 4194304 | tf_op jit(solution)/shard_map/project_own/pallas_call | solution.py:420
  23.2 1.1 %collective-permute-done.9 = bf16[8,1024]{1,0:T(8,128)(2,1)S(1)} collective-permute-done((bf16[8,1024]{1,0:T(8,128)(2,1)S(1)}, bf16[8,1024]{1,0:T(8,128)(2,1)S(1)}, u32[]{:S(2)}, u32[]{:S(2)}) %collective-permute-start.9) | collective-permute-done | bytes 16416 | tf_op jit(solution)/shard_map/ppermute | solution.py:434
  24.3 2.4 %collective-permute-done.10 = bf16[8,1024]{1,0:T(8,128)(2,1)S(1)} collective-permute-done((bf16[8,1024]{1,0:T(8,128)(2,1)S(1)}, bf16[8,1024]{1,0:T(8,128)(2,1)S(1)}, u32[]{:S(2)}, u32[]{:S(2)}) %collective-permute-start.10) | collective-permute-done | bytes 16416 | tf_op jit(solution)/shard_map/ppermute | solution.py:434
  26.7 0.6 %fusion.1 = bf16[1,8,1024]{2,1,0:T(8,128)(2,1)} fusion(bf16[8,1024]{1,0:T(8,128)(2,1)S(1)} %collective-permute-done.10, bf16[8,1024]{1,0:T(8,128)(2,1)S(1)} %collective-permute-done.9, f32[8,1024]{1,0:T(8,128)S(1)} %project_own.1, bf16[8,1024]{1,0:T(8,128)(2,1)S(1)} %collective-permute-done.8), kind=kLoop, calls=%fused_computation.3 | loop fusion | flops 57344 | bytes 98304 | tf_op jit(solution)/shard_map/broadcast_in_dim | solution.py:437
  (18 shorter events, 0.2 us)
Async XLA Ops:
  0.9 7.7 %collective-permute-start.1 = (bf16[8,2176]{1,0:T(8,128)(2,1)S(1)}, bf16[8,2176]{1,0:T(8,128)(2,1)S(1)}, u32[]{:S(2)}, u32[]{:S(2)}) collective-permute-start(bf16[8,2176]{1,0:T(8,128)(2,1)S(1)} %fusion.qa), channel_id=1, source_target_pairs={{16,4},{0,16},{20,0},{4,20},{24,12},{8,24},{28,8},{12,28},{17,5},{... | collective-permute-start | bytes 104456 | tf_op jit(solution)/shard_map/ppermute | solution.py:352
  1.3 7.3 %collective-permute-start = (bf16[8,2176]{1,0:T(8,128)(2,1)S(1)}, bf16[8,2176]{1,0:T(8,128)(2,1)S(1)}, u32[]{:S(2)}, u32[]{:S(2)}) collective-permute-start(bf16[8,2176]{1,0:T(8,128)(2,1)S(1)} %fusion.qa), channel_id=1, source_target_pairs={{16,8},{0,16},{20,12},{4,20},{24,0},{8,24},{28,4},{12,28},{17,9},{... | collective-permute-start | bytes 104456 | tf_op jit(solution)/shard_map/ppermute | solution.py:352
  4.0 5.8 %collective-permute-start.2 = (bf16[8,2176]{1,0:T(8,128)(2,1)S(1)}, bf16[8,2176]{1,0:T(8,128)(2,1)S(1)}, u32[]{:S(2)}, u32[]{:S(2)}) collective-permute-start(bf16[8,2176]{1,0:T(8,128)(2,1)S(1)} %fusion.qa), channel_id=1, source_target_pairs={{16,12},{0,16},{20,8},{4,20},{24,4},{8,24},{28,0},{12,28},{17,13},... | collective-permute-start | bytes 104456 | tf_op jit(solution)/shard_map/ppermute | solution.py:352
  9.9 7.5 %slice-start = ((s8[16777216]{0:T(1024)(128)(4,1)}), s8[4194304]{0:T(1024)(128)(4,1)S(1)}, s32[]{:S(2)}) async-start(s8[16777216]{0:T(1024)(128)(4,1)} %bitcast.7), calls=%async_computation | async-start | bytes 8388608
  9.9 2.9 %copy-start = (bf16[1,8,512]{2,1,0:T(8,128)(2,1)S(1)}, bf16[1,8,512]{2,1,0:T(8,128)(2,1)}, u32[]{:S(2)}) copy-start(bf16[1,8,512]{2,1,0:T(8,128)(2,1)} %param.14) | copy-start | bytes 24580
  9.9 7.4 %slice-start.1 = ((s8[16777216]{0:T(1024)(128)(4,1)}), s8[4194304]{0:T(1024)(128)(4,1)S(1)}, s32[]{:S(2)}) async-start(s8[16777216]{0:T(1024)(128)(4,1)} %bitcast.7), calls=%async_computation.1 | async-start | bytes 8388608
  9.9 7.4 %slice-start.2 = ((s8[16777216]{0:T(1024)(128)(4,1)}), s8[4194304]{0:T(1024)(128)(4,1)S(1)}, s32[]{:S(2)}) async-start(s8[16777216]{0:T(1024)(128)(4,1)} %bitcast.7), calls=%async_computation.2 | async-start | bytes 8388608
  9.9 7.4 %slice-start.3 = ((s8[16777216]{0:T(1024)(128)(4,1)}), s8[4194304]{0:T(1024)(128)(4,1)S(1)}, s32[]{:S(2)}) async-start(s8[16777216]{0:T(1024)(128)(4,1)} %bitcast.7), calls=%async_computation.3 | async-start | bytes 8388608
  10.6 2.4 %collective-permute-start.3 = (bf16[144,128]{1,0:T(8,128)(2,1)S(1)}, bf16[144,128]{1,0:T(8,128)(2,1)S(1)}, u32[]{:S(2)}, u32[]{:S(2)}) collective-permute-start(bf16[144,128]{1,0:T(8,128)(2,1)S(1)} %owned.3), channel_id=1, source_target_pairs={{0,28},{16,0},{4,24},{20,4},{8,20},{24,8},{12,16},{28,12},{1,29},{... | collective-permute-start | bytes 110600 | tf_op jit(solution)/shard_map/ppermute | solution.py:352
  11.4 2.5 %collective-permute-start.4 = (bf16[144,128]{1,0:T(8,128)(2,1)S(1)}, bf16[144,128]{1,0:T(8,128)(2,1)S(1)}, u32[]{:S(2)}, u32[]{:S(2)}) collective-permute-start(bf16[144,128]{1,0:T(8,128)(2,1)S(1)} %get-tuple-element.31.refs_2_), channel_id=1, source_target_pairs={{0,24},{16,0},{4,28},{20,4},{8,16},{24,8},{12,20},{28,12},{1,25},{... | collective-permute-start | bytes 110600 | tf_op jit(solution)/shard_map/ppermute | solution.py:352
  12.3 2.0 %collective-permute-start.5 = (bf16[144,128]{1,0:T(8,128)(2,1)S(1)}, bf16[144,128]{1,0:T(8,128)(2,1)S(1)}, u32[]{:S(2)}, u32[]{:S(2)}) collective-permute-start(bf16[144,128]{1,0:T(8,128)(2,1)S(1)} %get-tuple-element.32.refs_1_), channel_id=1, source_target_pairs={{0,20},{16,0},{4,16},{20,4},{8,28},{24,8},{12,24},{28,12},{1,21},{... | collective-permute-start | bytes 110600 | tf_op jit(solution)/shard_map/ppermute | solution.py:352
  12.4 1.9 %collective-permute-start.6 = (bf16[144,128]{1,0:T(8,128)(2,1)S(1)}, bf16[144,128]{1,0:T(8,128)(2,1)S(1)}, u32[]{:S(2)}, u32[]{:S(2)}) collective-permute-start(bf16[144,128]{1,0:T(8,128)(2,1)S(1)} %get-tuple-element.33), channel_id=1, source_target_pairs={{0,16},{16,0},{4,20},{20,4},{8,24},{24,8},{12,28},{28,12},{1,17},{... | collective-permute-start | bytes 110600 | tf_op jit(solution)/shard_map/ppermute | solution.py:352
  14.6 2.7 %collective-permute-start.7 = (bf16[8,2048]{1,0:T(8,128)(2,1)S(1)}, bf16[8,2048]{1,0:T(8,128)(2,1)S(1)}, u32[]{:S(2)}, u32[]{:S(2)}) collective-permute-start(bf16[8,2048]{1,0:T(8,128)(2,1)S(1)} %merge.1.attended), channel_id=1, source_target_pairs={{0,16},{16,0},{1,17},{17,1},{2,18},{18,2},{3,19},{19,3},{4,20},{20... | collective-permute-start | bytes 98312 | tf_op jit(solution)/shard_map/ppermute | solution.py:416
  19.1 4.2 %collective-permute-start.8 = (bf16[8,1024]{1,0:T(8,128)(2,1)S(1)}, bf16[8,1024]{1,0:T(8,128)(2,1)S(1)}, u32[]{:S(2)}, u32[]{:S(2)}) collective-permute-start(bf16[8,1024]{1,0:T(8,128)(2,1)S(1)} %get-tuple-element.34), channel_id=1, source_target_pairs={{0,1},{1,0},{2,3},{3,2},{4,5},{5,4},{6,7},{7,6},{8,9},{9,8},{10,11... | collective-permute-start | bytes 49160 | tf_op jit(solution)/shard_map/ppermute | solution.py:434
  20.6 3.7 %collective-permute-start.9 = (bf16[8,1024]{1,0:T(8,128)(2,1)S(1)}, bf16[8,1024]{1,0:T(8,128)(2,1)S(1)}, u32[]{:S(2)}, u32[]{:S(2)}) collective-permute-start(bf16[8,1024]{1,0:T(8,128)(2,1)S(1)} %get-tuple-element.35), channel_id=1, source_target_pairs={{0,2},{1,3},{2,0},{3,1},{4,6},{5,7},{6,4},{7,5},{8,10},{9,11},{10,... | collective-permute-start | bytes 49160 | tf_op jit(solution)/shard_map/ppermute | solution.py:434
  22.1 4.6 %collective-permute-start.10 = (bf16[8,1024]{1,0:T(8,128)(2,1)S(1)}, bf16[8,1024]{1,0:T(8,128)(2,1)S(1)}, u32[]{:S(2)}, u32[]{:S(2)}) collective-permute-start(bf16[8,1024]{1,0:T(8,128)(2,1)S(1)} %get-tuple-element.36), channel_id=1, source_target_pairs={{0,3},{1,2},{2,1},{3,0},{4,7},{5,6},{6,5},{7,4},{8,11},{9,10},{10,... | collective-permute-start | bytes 49160 | tf_op jit(solution)/shard_map/ppermute | solution.py:434
